TPU v7x, 32 devices: a whole 2x2x4 slice. The times are simulated.
32 devices in a mesh: row: 4 (over z), seq: 2 (over y), head: 4 (over x, core).
Axes of the slice: x: 2, y: 2, z: 4, core: 2. Of those that a mesh axis runs over, the one named last changes fastest.
Arguments:
- hidden_in: bfloat16 [8, 2048, 2048], P('row', ('seq', 'head')), may hold values from -6 to 6
- grad_out: bfloat16 [8, 2048, 2048], P('row', ('seq', 'head')), may hold values from -6 to 6
- live_rows: int32 [4], P('row'), may hold values from 1 to 2, as said below
- doc_starts: int32 [8, 2048], P('row'), may hold values from 0 to 1, as said below
- norm_attn: bfloat16 [2048], replicated, may hold values from 0.5 to 1.5
- norm_ffn: bfloat16 [2048], replicated, may hold values from 0.5 to 1.5
- query_weight: bfloat16 [2048, 2048], P(('row', 'seq'), 'head'), may hold values from -0.125 to 0.125
- key_weight: bfloat16 [2048, 512], P(('row', 'seq'), 'head'), may hold values from -0.125 to 0.125
- value_weight: bfloat16 [2048, 512], P(('row', 'seq'), 'head'), may hold values from -0.125 to 0.125
- out_weight: bfloat16 [2048, 2048], P('head', ('row', 'seq')), may hold values from -0.5 to 0.5
- gate_weight: bfloat16 [2048, 8192], P(('row', 'seq'), 'head'), may hold values from -0.125 to 0.125
- up_weight: bfloat16 [2048, 8192], P(('row', 'seq'), 'head'), may hold values from -0.125 to 0.125
- down_weight: bfloat16 [8192, 2048], P('head', ('row', 'seq')), may hold values from -0.0625 to 0.0625
- query_adapt_in: bfloat16 [2048, 8], replicated, may hold values from -0.125 to 0.125
- query_adapt_out: bfloat16 [8, 2048], P(None, 'head'), may hold values from -0.59765625 to 0.59765625
- key_adapt_in: bfloat16 [2048, 8], replicated, may hold values from -0.125 to 0.125
- key_adapt_out: bfloat16 [8, 512], P(None, 'head'), may hold values from -0.59765625 to 0.59765625
- value_adapt_in: bfloat16 [2048, 8], replicated, may hold values from -0.125 to 0.125
- value_adapt_out: bfloat16 [8, 512], P(None, 'head'), may hold values from -0.59765625 to 0.59765625
- outproj_adapt_in: bfloat16 [2048, 8], P('head'), may hold values from -0.5 to 0.5
- projection_adapter_second: bfloat16 [8, 2048], replicated, may hold values from -0.59765625 to 0.59765625
- query_feature: bfloat16 [32, 64, 64], P('head'), may hold values from -0.75 to 0.75
- key_feature: bfloat16 [8, 64, 64], P('head'), may hold values from -0.75 to 0.75
Outputs:
- block_out: bfloat16 [8, 2048, 2048], P('row', ('seq', 'head'))
- grad_hidden: bfloat16 [8, 2048, 2048], P('row', ('seq', 'head'))
- grad_query_in: float32 [2048, 8], P(('row', 'seq', 'head'))
- grad_query_out: float32 [8, 2048], P(None, 'head')
- grad_key_in: float32 [2048, 8], P(('row', 'seq', 'head'))
- grad_key_out: float32 [8, 512], P(None, 'head')
- grad_value_in: float32 [2048, 8], P(('row', 'seq', 'head'))
- grad_value_out: float32 [8, 512], P(None, 'head')
- grad_outproj_in: float32 [2048, 8], P('head')
- grad_outproj_out: float32 [8, 2048], P(None, ('row', 'seq', 'head'))
- grad_query_feature: float32 [32, 64, 64], P('head')
- grad_key_feature: float32 [8, 64, 64], P('head')
Inputs may be any that keep to these rules, and one draw needn't show every extreme that they name: Row slots 0 to live_rows[g] - 1 of the 2 slots of row group g are live, the others add nothing to any gradient; some group is full and some other group has a single live slot. `doc_starts`: 1 marks the first token of a document in a packed row; each row group has a row without marks.
All inputs are finite; a program needn't handle non-finite values.
Results may differ from a plain program's by a relative error of at most 0.028.
Values may be sent and summed in bfloat16 or wider, within the bound.
A program may use at most 224 MiB of HBM per device.

v0:
```python
import functools

import jax
import jax.numpy as jnp
from jax import lax
from jax.experimental import pallas as pl
from jax.experimental.pallas import tpu as pltpu
from jax.sharding import PartitionSpec as P

HD = 64
RANK = 8
WIN = 64
FF_CHUNKS = 4

NORM_EPS = 1e-05
ADAPTER_SCALE = 2.0
F32 = jnp.float32
BF16 = jnp.bfloat16
HIGHEST = lax.Precision.HIGHEST


def shift(block, axis, distance):
    size = lax.axis_size(axis)
    return lax.ppermute(block, axis, [(i, (i + distance) % size) for i in range(size)])


def flip_core(block):
    return lax.ppermute(block, "head", [(i, i ^ 1) for i in range(lax.axis_size("head"))])


def flip_x(block):
    return lax.ppermute(block, "head", [(i, i ^ 2) for i in range(lax.axis_size("head"))])


def dot(a, b, dims=((1,), (0,))):
    return lax.dot_general(a, b, (dims, ((), ())), preferred_element_type=F32)


def rms_scaled(values, gain_vec):
    return (
        values * lax.rsqrt(jnp.mean(values * values, axis=-1, keepdims=True) + NORM_EPS) * gain_vec
    )


def rms_back(values, gain_vec, grad_in):
    factor = lax.rsqrt(jnp.mean(values * values, axis=-1, keepdims=True) + NORM_EPS)
    scaled = gain_vec * grad_in
    return factor * scaled - values * factor**3 * jnp.mean(values * scaled, axis=-1, keepdims=True)


def hedgehog(values):
    return jnp.concatenate(
        [jax.nn.softmax(values, axis=-1), jax.nn.softmax(-values, axis=-1)], axis=-1
    )


def paired(blocks):
    return jnp.concatenate([blocks[:, :-1], blocks[:, 1:]], axis=2)


def unpaired(grad_pair):
    half_width = grad_pair.shape[2] // 2
    rest_pad = ((0, 0),) * (grad_pair.ndim - 2)
    lower_half = jnp.pad(grad_pair[:, :, :half_width], ((0, 0), (0, 1)) + rest_pad)
    upper_half = jnp.pad(grad_pair[:, :, half_width:], ((0, 0), (1, 0)) + rest_pad)
    return lower_half + upper_half


def gather_zy(shard):
    rows, seqs = lax.axis_size("row"), lax.axis_size("seq")
    held = {(0, 0): shard}
    for k in range(1, rows):
        held[k, 0] = shift(held[k - 1, 0], "row", 1)
    for k in range(rows):
        for l in range(1, seqs):
            held[k, l] = shift(held[k, l - 1], "seq", 1)
    return held


def assemble(*held_sets):
    rows, seqs = lax.axis_size("row"), lax.axis_size("seq")
    row, seq = lax.axis_index("row"), lax.axis_index("seq")
    x_place = lax.axis_index("head") // 2
    depth, width = held_sets[0][0, 0].shape
    whole = jnp.zeros((rows * seqs * depth, len(held_sets) * width), held_sets[0][0, 0].dtype)
    for d, held in enumerate(held_sets):
        column = lax.rem(x_place + d, 2) * width if d or len(held_sets) > 1 else 0
        for (k, l), block in held.items():
            place = lax.rem(row - k + rows, rows) * seqs + lax.rem(seq - l + seqs, seqs)
            whole = lax.dynamic_update_slice(whole, block, (place * depth, column))
    return whole


def gather_x(held):
    return {k: flip_x(v) for k, v in held.items()}


def scatter_sum(parts, axis):
    size, place = lax.axis_size(axis), lax.axis_index(axis)
    total = lax.dynamic_index_in_dim(parts, place, 0, keepdims=False)
    for k in range(1, size):
        away = lax.dynamic_index_in_dim(parts, lax.rem(place + k, size), 0, keepdims=False)
        total = total + shift(away, axis, k)
    return total


def full_sum(part, axis):
    size = lax.axis_size(axis)
    step = 1
    while step < size:
        sent = part.astype(BF16)
        got = lax.ppermute(sent, axis, [(i, i ^ step) for i in range(size)])
        part = sent.astype(F32) + got.astype(F32)
        step *= 2
    return part


def ffn_pre_kernel(x_ref, cot_ref, w_ref, mixed_ref, gg_ref, gu_ref):
    width = mixed_ref.shape[1]
    x, cot = x_ref[...], cot_ref[...]
    gate = dot(x, w_ref[:, :width])
    up = dot(x, w_ref[:, width : 2 * width])
    gm = dot(cot, w_ref[:, 2 * width :])
    sig = jax.nn.sigmoid(gate)
    silu = gate * sig
    mixed_ref[...] = (silu * up).astype(BF16)
    gg_ref[...] = (gm * up * (sig + silu * (1.0 - sig))).astype(BF16)
    gu_ref[...] = (gm * silu).astype(BF16)


def ffn_pre(x, cot, w):
    tokens, depth = x.shape
    width = w.shape[1] // 3
    tile = min(256, tokens)
    out = jax.ShapeDtypeStruct((tokens, width), BF16)
    return pl.pallas_call(
        ffn_pre_kernel,
        grid=(tokens // tile,),
        in_specs=[
            pl.BlockSpec((tile, depth), lambda i: (i, 0)),
            pl.BlockSpec((tile, depth), lambda i: (i, 0)),
            pl.BlockSpec((depth, 3 * width), lambda i: (0, 0)),
        ],
        out_specs=[pl.BlockSpec((tile, width), lambda i: (i, 0))] * 3,
        out_shape=[out, out, out],
        compiler_params=pltpu.CompilerParams(vmem_limit_bytes=48 * 2**20),
        cost_estimate=pl.CostEstimate(
            flops=6 * tokens * depth * width,
            bytes_accessed=4 * tokens * depth + 6 * depth * width + 6 * tokens * width,
            transcendentals=tokens * width,
        ),
        name="ffn_pre",
    )(x, cot, w)


def ffn_post_kernel(chunks, *refs):
    lhs = refs[: 3 * chunks]
    weights = refs[3 * chunks : 4 * chunks]
    gn_ref, y_ref = refs[4 * chunks :]
    nt = ((1,), (1,))
    width = lhs[0].shape[1]
    gn = None
    y = None
    for j in range(chunks):
        mixed, gg, gu = (r[...] for r in lhs[3 * j : 3 * j + 3])
        w = weights[j]
        part = dot(gg, w[:, :width], nt) + dot(gu, w[:, width : 2 * width], nt)
        gn = part if gn is None else gn + part
        part = dot(mixed, w[:, 2 * width :], nt)
        y = part if y is None else y + part
    gn_ref[...] = gn.astype(BF16)
    y_ref[...] = y.astype(BF16)


def ffn_post(acts, weights):
    chunks = len(weights)
    tokens, width = acts[0][0].shape
    depth = weights[0].shape[0]
    tile = min(256, tokens)
    cols = min(512, depth)
    out = jax.ShapeDtypeStruct((tokens, depth), BF16)
    return pl.pallas_call(
        functools.partial(ffn_post_kernel, chunks),
        grid=(depth // cols, tokens // tile),
        in_specs=[pl.BlockSpec((tile, width), lambda d, i: (i, 0))] * (3 * chunks)
        + [pl.BlockSpec((cols, 3 * width), lambda d, i: (d, 0))] * chunks,
        out_specs=[pl.BlockSpec((tile, cols), lambda d, i: (i, d))] * 2,
        out_shape=[out, out],
        compiler_params=pltpu.CompilerParams(vmem_limit_bytes=48 * 2**20),
        cost_estimate=pl.CostEstimate(
            flops=6 * tokens * depth * width * chunks,
            bytes_accessed=(6 * depth * width + 6 * tokens * width) * chunks + 4 * tokens * depth,
            transcendentals=0,
        ),
        name="ffn_post",
    )(*[a for trio in acts for a in trio], *weights)


def local(
    hidden_in,
    grad_out,
    live_rows,
    doc_starts,
    norm_attn,
    norm_ffn,
    query_weight,
    key_weight,
    value_weight,
    out_weight,
    gate_weight,
    up_weight,
    down_weight,
    query_adapt_in,
    query_adapt_out,
    key_adapt_in,
    key_adapt_out,
    value_adapt_in,
    value_adapt_out,
    outproj_adapt_in,
    projection_adapter_second,
    query_feature,
    key_feature,
):
    rows, seqs, heads = lax.axis_size("row"), lax.axis_size("seq"), lax.axis_size("head")
    head = lax.axis_index("head")
    core = lax.rem(head, 2)
    x_count = heads // 2
    x_place = head // 2
    slots, share_len, model_dim = hidden_in.shape
    piece_len = 2 * share_len
    pieces = seqs * x_count
    piece = lax.axis_index("seq") * x_count + x_place
    blocks = piece_len // WIN
    ext_len = piece_len + WIN
    feat_dim = 2 * HD
    score_scale = HD ** (-0.5)
    q_cols, k_cols = query_weight.shape[1], key_weight.shape[1]
    ff_cols = gate_weight.shape[1]

    def in_order(own, other):
        first = jnp.where(core == 0, own, other)
        second = jnp.where(core == 0, other, own)
        return jnp.concatenate([first, second], axis=1)

    def own_half(both):
        return lax.dynamic_slice_in_dim(both, core * share_len, share_len, 1)

    def other_half(both):
        return lax.dynamic_slice_in_dim(both, (1 - core) * share_len, share_len, 1)

    qkv_shard = jnp.concatenate([query_weight, key_weight, value_weight], axis=1)
    out_shard = out_weight.T
    down_shard = down_weight.T
    chunk = ff_cols // FF_CHUNKS
    ffn_shards = [
        jnp.concatenate(
            [w[:, j * chunk : (j + 1) * chunk] for w in (gate_weight, up_weight, down_shard)], axis=1
        )
        for j in range(FF_CHUNKS)
    ]
    qkv_held = gather_zy(qkv_shard)
    qkv_mat = assemble(qkv_held, gather_x(qkv_held))
    out_held = gather_zy(out_shard)
    out_mat = assemble(out_held, gather_x(out_held))
    ffn_mats = [assemble(gather_zy(s)) for s in ffn_shards]

    def both(own, axis):
        other = flip_x(own)
        return jnp.concatenate(
            [jnp.where(x_place == 0, own, other), jnp.where(x_place == 0, other, own)], axis=axis
        )

    q_out, k_out, v_out = (both(v, 1) for v in (query_adapt_out, key_adapt_out, value_adapt_out))
    o_in = both(outproj_adapt_in, 0)
    query_feat_all = both(query_feature, 0)
    key_feat = both(key_feature, 0)
    groups = key_feat.shape[0]
    per_group = query_feat_all.shape[0] // groups
    query_feat = query_feat_all.reshape(groups, per_group, HD, HD)

    doc_ids = jnp.cumsum(doc_starts, axis=1)
    padded_docs = jnp.concatenate(
        [jnp.full((slots, WIN + 1), -1, jnp.int32), doc_ids], axis=1
    )
    piece_docs = padded_docs[:, ::piece_len][:, : pieces + 1]
    near_docs = lax.dynamic_slice_in_dim(padded_docs, piece * piece_len, ext_len + 1, 1)
    end_docs = near_docs[:, ::WIN][:, : blocks + 1]
    carry_doc = end_docs[:, 0]
    next_doc = end_docs[:, blocks]
    key_docs = near_docs[:, 1:]
    query_docs = near_docs[:, WIN + 1 :].reshape(slots, blocks, WIN)
    ext_pos = jnp.arange(ext_len)
    block_pos = jnp.arange(blocks + 1)
    row_pos = jnp.arange(WIN)[:, None]
    col_pos = jnp.arange(2 * WIN)[None, :]
    state_mask = (
        (ext_pos[None, None, :] < WIN * block_pos[None, :, None])
        & (key_docs[:, None, :] == end_docs[:, :, None])
    ).astype(F32)
    carry_in = (end_docs == carry_doc[:, None]).astype(F32)
    state_valid = (query_docs == end_docs[:, :blocks, None]).astype(F32)[:, :, :, None, None, None]
    pair_docs = paired(key_docs.reshape(slots, blocks + 1, WIN))
    same_doc = query_docs[:, :, :, None] == pair_docs[:, :, None, :]
    window_mask = (same_doc & (col_pos > row_pos) & (col_pos <= row_pos + WIN)).astype(F32)[
        :, None, None
    ]
    linear_mask = (same_doc & (col_pos <= row_pos)).astype(F32)[:, None, None]

    def from_pieces(block):
        held = []
        for d, start in enumerate((block, flip_x(block))):
            for l in range(seqs):
                if l:
                    start = shift(start, "seq", 1)
                source = (
                    lax.rem(lax.axis_index("seq") - l + seqs, seqs) * x_count
                    + lax.rem(x_place + d, x_count)
                )
                held.append((source, start))
        return held[1:]

    gain_attn = norm_attn.astype(F32)
    gain_ffn = norm_ffn.astype(F32)
    slot_live = (jnp.arange(slots) < live_rows[0])[:, None, None]
    grad_low = jnp.where(slot_live, grad_out, jnp.zeros_like(grad_out))
    grad_share = grad_low.astype(F32)
    rows_float = hidden_in.astype(F32)
    normed_share = rms_scaled(rows_float, gain_attn).astype(BF16)
    normed = in_order(normed_share, flip_core(normed_share))
    cot_x = flip_x(grad_low)

    flat = normed.reshape(slots * piece_len, model_dim)

    full = dot(flat, qkv_mat)
    set_cols = q_cols + 2 * k_cols

    def of_sets(v, start, count):
        return jnp.concatenate(
            [v[:, d * set_cols + start : d * set_cols + start + count] for d in range(2)], axis=1
        )

    def project(start, count, adapt_in, adapter_output):
        small = dot(flat, adapt_in).astype(BF16)
        low = (of_sets(full, start, count) + ADAPTER_SCALE * dot(small, adapter_output)).astype(BF16)
        return small, low.reshape(slots, piece_len, -1)

    small_query, query_low = project(0, q_cols, query_adapt_in, q_out)
    small_key, key_low = project(q_cols, k_cols, key_adapt_in, k_out)
    small_value, value_low = project(q_cols + k_cols, k_cols, value_adapt_in, v_out)

    def along_pieces(block, distance):
        route = []
        for p in range(pieces):
            to = p + distance
            if 0 <= to < pieces:
                for c in range(2):
                    route.append((2 * p + c, 2 * to + c))
        return lax.ppermute(block, ("seq", "head"), route)

    key_edge, value_edge = (along_pieces(v[:, -WIN:], 1) for v in (key_low, value_low))
    key_blk = jnp.concatenate([key_edge, key_low], axis=1).reshape(
        slots, blocks + 1, WIN, groups, HD
    )
    value_blk = jnp.concatenate([value_edge, value_low], axis=1).reshape(
        slots, blocks + 1, WIN, groups, HD
    )
    query_blk = query_low.reshape(slots, blocks, WIN, groups, per_group, HD)
    query_logit = jnp.einsum(
        "rbigqd,gqde->rbigqe", query_blk, query_feat, preferred_element_type=F32
    )
    phi_query = hedgehog(query_logit).astype(BF16)
    key_logit = jnp.einsum("rbigd,gde->rbige", key_blk, key_feat, preferred_element_type=F32)
    phi_key = hedgehog(key_logit).astype(BF16)
    key_pair = paired(key_blk)
    value_pair = paired(value_blk)
    phi_pair = paired(phi_key)
    scores = (
        jnp.einsum("rbigqd,rbjgd->rgqbij", query_blk, key_pair, preferred_element_type=F32)
        * score_scale
    )
    lin_score = jnp.einsum("rbigqf,rbjgf->rgqbij", phi_query, phi_pair, preferred_element_type=F32)
    exp_score = jnp.exp(scores)
    weights = (exp_score * window_mask + lin_score * linear_mask).astype(BF16)
    phi_flat = phi_key.reshape(slots, ext_len, groups, feat_dim).astype(F32)
    value_flat = value_blk.reshape(slots, ext_len, groups, HD).astype(F32)
    masked_phi = state_mask[:, :, :, None, None] * phi_flat[:, None]
    local_state = jnp.einsum("rbegf,regd->rbgfd", masked_phi, value_flat, precision=HIGHEST)
    local_norm = jnp.sum(masked_phi, axis=2)

    def with_norm(state, norm):
        return jnp.concatenate([state, norm[..., None]], axis=-1)

    carry = jnp.zeros((slots, groups, feat_dim, HD + 1), F32)
    for source, part in from_pieces(
        with_norm(local_state[:, blocks], local_norm[:, blocks]).astype(BF16)
    ):
        after = lax.dynamic_index_in_dim(piece_docs, source + 1, 1, keepdims=False)
        keep = (source < piece) & (after == carry_doc)
        carry = carry + jnp.where(keep[:, None, None, None], part.astype(F32), 0.0)
    carry_state, carry_norm = carry[..., :HD], carry[..., HD]
    block_state = (
        local_state[:, :blocks] + carry_in[:, :blocks, None, None, None] * carry_state[:, None]
    ).astype(BF16)
    block_norm = (
        local_norm[:, :blocks] + carry_in[:, :blocks, None, None] * carry_norm[:, None]
    ).astype(BF16)
    numer_sum = jnp.einsum(
        "rgqbij,rbjgd->rbigqd", weights, value_pair, preferred_element_type=F32
    ) + state_valid * jnp.einsum(
        "rbigqf,rbgfd->rbigqd", phi_query, block_state, preferred_element_type=F32
    )
    denominator = jnp.sum(weights, axis=-1, dtype=F32).transpose(0, 3, 4, 1, 2) + state_valid[
        ..., 0
    ] * jnp.einsum("rbigqf,rbgf->rbigq", phi_query, block_norm, preferred_element_type=F32)
    attn_float = numer_sum / denominator[..., None]
    attn = attn_float.reshape(slots * piece_len, -1).astype(BF16)

    proj_part = dot(attn, out_mat, ((1,), (1,))).reshape(slots, piece_len, model_dim)
    low_part = dot(attn, o_in).reshape(slots, piece_len, RANK)
    proj_sum = own_half(proj_part) + flip_core(other_half(proj_part).astype(BF16)).astype(F32)
    low_mix = (own_half(low_part) + flip_core(other_half(low_part))).astype(BF16)
    mid_rows = (
        rows_float
        + proj_sum
        + ADAPTER_SCALE
        * dot(low_mix.reshape(-1, RANK), projection_adapter_second).reshape(rows_float.shape)
    )

    nmid = rms_scaled(mid_rows, gain_ffn).astype(BF16)
    nmid_x = flip_x(nmid)

    def chip_tokens(own):
        return jnp.concatenate([own, flip_core(own)], axis=0).reshape(-1, model_dim)

    tokens = [(chip_tokens(nmid), chip_tokens(grad_low)), (chip_tokens(nmid_x), chip_tokens(cot_x))]
    acts = [[ffn_pre(x, c, w) for w in ffn_mats] for x, c in tokens]

    def to_own(mine, away):
        mine, away = (v.reshape(2, slots, share_len, model_dim) for v in (mine, away))
        there = (away[0].astype(F32) + flip_core(away[1]).astype(F32)).astype(BF16)
        back = flip_x(there)
        return mine[0].astype(F32) + flip_core(mine[1]).astype(F32) + back.astype(F32)

    gn_away, y_away = ffn_post(acts[1], ffn_mats)
    gn_mine, y_mine = ffn_post(acts[0], ffn_mats)
    grad_nmid = to_own(gn_mine, gn_away)
    block_out = (mid_rows + to_own(y_mine, y_away)).astype(BF16)
    grad_mid = grad_share + rms_back(mid_rows, gain_ffn, grad_nmid)

    branch_share = grad_mid.astype(BF16)
    branch = in_order(branch_share, flip_core(branch_share)).reshape(-1, model_dim)
    grad_low_mix = (
        ADAPTER_SCALE * dot(branch, projection_adapter_second, ((1,), (1,)))
    ).astype(BF16)
    sum_o_in = dot(attn, grad_low_mix, ((0,), (0,)))
    sum_o_out = ADAPTER_SCALE * dot(
        low_mix.reshape(-1, RANK), branch_share.reshape(-1, model_dim), ((0,), (0,))
    )
    grad_attn = (dot(branch, out_mat) + dot(grad_low_mix, o_in, ((1,), (1,)))).astype(BF16)

    grad_blk = grad_attn.reshape(slots, blocks, WIN, groups, per_group, HD).astype(F32)
    grad_numer = (grad_blk / denominator[..., None]).astype(BF16)
    grad_denom = (-jnp.sum(grad_blk * attn_float, axis=-1) / denominator).astype(BF16)
    grad_weight = (
        jnp.einsum("rbigqd,rbjgd->rgqbij", grad_numer, value_pair, preferred_element_type=F32)
        + grad_denom.transpose(0, 3, 4, 1, 2).astype(F32)[..., None]
    )
    grad_score = (exp_score * window_mask * grad_weight).astype(BF16)
    grad_lin = (linear_mask * grad_weight).astype(BF16)
    grad_query = (
        jnp.einsum("rgqbij,rbjgd->rbigqd", grad_score, key_pair, preferred_element_type=F32)
        * score_scale
    )
    grad_key_pair = (
        jnp.einsum("rgqbij,rbigqd->rbjgd", grad_score, query_blk, preferred_element_type=F32)
        * score_scale
    )
    grad_value_pair = jnp.einsum(
        "rgqbij,rbigqd->rbjgd", weights, grad_numer, preferred_element_type=F32
    )
    grad_phi_query = jnp.einsum(
        "rgqbij,rbjgf->rbigqf", grad_lin, phi_pair, preferred_element_type=F32
    ) + state_valid * (
        jnp.einsum("rbigqd,rbgfd->rbigqf", grad_numer, block_state, preferred_element_type=F32)
        + grad_denom.astype(F32)[..., None] * block_norm.astype(F32)[:, :, None, :, None, :]
    )
    grad_phi_pair = jnp.einsum(
        "rgqbij,rbigqf->rbjgf", grad_lin, phi_query, preferred_element_type=F32
    )
    phi_valid = phi_query * state_valid.astype(BF16)
    grad_state = jnp.einsum(
        "rbigqf,rbigqd->rbgfd", phi_valid, grad_numer, preferred_element_type=F32
    )
    grad_norm = jnp.einsum("rbigqf,rbigq->rbgf", phi_valid, grad_denom, preferred_element_type=F32)
    grad_carry = jnp.sum(carry_in[:, :blocks, None, None, None] * grad_state, axis=1)
    grad_carry_norm = jnp.sum(carry_in[:, :blocks, None, None] * grad_norm, axis=1)
    later = jnp.zeros((slots, groups, feat_dim, HD + 1), F32)
    for source, part in from_pieces(with_norm(grad_carry, grad_carry_norm).astype(BF16)):
        start = lax.dynamic_index_in_dim(piece_docs, source, 1, keepdims=False)
        keep = (source > piece) & (start == next_doc)
        later = later + jnp.where(keep[:, None, None, None], part.astype(F32), 0.0)
    state_all = jnp.concatenate([grad_state, later[:, None, :, :, :HD]], axis=1)
    norm_all = jnp.concatenate([grad_norm, later[:, None, :, :, HD]], axis=1)
    via_phi = jnp.einsum("rbgfd,regd->rbegf", state_all, value_flat, precision=HIGHEST)
    state_phi = jnp.einsum("rbe,rbegf->regf", state_mask, via_phi, precision=HIGHEST) + jnp.einsum(
        "rbe,rbgf->regf", state_mask, norm_all, precision=HIGHEST
    )
    grad_phi_key = unpaired(grad_phi_pair) + state_phi.reshape(
        slots, blocks + 1, WIN, groups, feat_dim
    )
    via_value = jnp.einsum("rbgfd,regf->rbegd", state_all, phi_flat, precision=HIGHEST)
    state_value = jnp.einsum("rbe,rbegd->regd", state_mask, via_value, precision=HIGHEST)
    grad_value_blk = unpaired(grad_value_pair) + state_value.reshape(
        slots, blocks + 1, WIN, groups, HD
    )
    _, pull_key = jax.vjp(hedgehog, key_logit)
    grad_key_logit = pull_key(grad_phi_key)[0].astype(BF16)
    grad_key_blk = unpaired(grad_key_pair) + jnp.einsum(
        "rbige,gde->rbigd", grad_key_logit, key_feat, preferred_element_type=F32
    )
    sum_k_feat = jnp.einsum(
        "rbigd,rbige->gde", key_blk, grad_key_logit, preferred_element_type=F32
    )
    _, pull_query = jax.vjp(hedgehog, query_logit)
    grad_query_logit = pull_query(grad_phi_query)[0].astype(BF16)
    grad_query = grad_query + jnp.einsum(
        "rbigqe,gqde->rbigqd", grad_query_logit, query_feat, preferred_element_type=F32
    )
    sum_q_feat = jnp.einsum(
        "rbigqd,rbigqe->gqde", query_blk, grad_query_logit, preferred_element_type=F32
    )
    grad_key_ext = grad_key_blk.reshape(slots, ext_len, groups * HD)
    grad_value_ext = grad_value_blk.reshape(slots, ext_len, groups * HD)
    tail_pad = ((0, 0), (piece_len - WIN, 0), (0, 0))

    def fold_back(ext):
        back = along_pieces(ext[:, :WIN].astype(BF16), -1).astype(F32)
        return (ext[:, WIN:] + jnp.pad(back, tail_pad)).astype(BF16)

    grad_key_low = fold_back(grad_key_ext).reshape(slots * piece_len, -1)
    grad_value_low = fold_back(grad_value_ext).reshape(slots * piece_len, -1)
    grad_query_low = grad_query.reshape(slots * piece_len, -1).astype(BF16)

    nt = ((1,), (1,))
    half = lambda v, d: v[:, d * (v.shape[1] // 2) : (d + 1) * (v.shape[1] // 2)]
    stacked = jnp.concatenate(
        [half(v, d) for d in range(2) for v in (grad_query_low, grad_key_low, grad_value_low)], axis=1
    )
    grad_normed_part = dot(stacked, qkv_mat, nt)
    small_part = jnp.concatenate(
        [
            ADAPTER_SCALE * dot(g, b, nt)
            for g, b in ((grad_query_low, q_out), (grad_key_low, k_out), (grad_value_low, v_out))
        ],
        axis=1,
    )
    outs = [
        ADAPTER_SCALE * dot(s, g, ((0,), (0,)))
        for s, g in (
            (small_query, grad_query_low),
            (small_key, grad_key_low),
            (small_value, grad_value_low),
        )
    ]
    grad_normed_part = grad_normed_part.reshape(slots, piece_len, model_dim)
    small_part = small_part.reshape(slots, piece_len, 3 * RANK)
    grad_normed = own_half(grad_normed_part) + flip_core(
        other_half(grad_normed_part).astype(BF16)
    ).astype(F32)
    small_low = (own_half(small_part) + flip_core(other_half(small_part))).astype(BF16)
    small_low = small_low.reshape(-1, 3 * RANK)
    adapt_in_all = jnp.concatenate([query_adapt_in, key_adapt_in, value_adapt_in], axis=1)
    grad_normed = grad_normed + dot(small_low, adapt_in_all, nt).reshape(rows_float.shape)
    sum_in = dot(small_low, normed_share.reshape(-1, model_dim), ((0,), (0,)))
    grad_hidden = (grad_mid + rms_back(rows_float, gain_attn, grad_normed)).astype(BF16)

    by_rows = jnp.concatenate([sum_in, sum_o_out], axis=0)
    width = model_dim // (rows * seqs * heads)
    by_rows = by_rows.reshape(4 * RANK, rows, seqs, heads, width).transpose(3, 2, 1, 0, 4)
    for axis in ("head", "seq", "row"):
        by_rows = scatter_sum(by_rows, axis)
    in_parts = by_rows.reshape(4, RANK, width)

    def to_heads(pair, axis):
        size = pair.shape[axis] // 2
        mine = lax.dynamic_slice_in_dim(pair, x_place * size, size, axis)
        away = lax.dynamic_slice_in_dim(pair, (1 - x_place) * size, size, axis)
        return mine + flip_x(away.astype(BF16)).astype(F32)

    cols = [
        to_heads(outs[0], 1),
        to_heads(outs[1], 1),
        to_heads(outs[2], 1),
        to_heads(sum_o_in, 0),
        to_heads(sum_q_feat.reshape(groups * per_group, HD, HD), 0),
        to_heads(sum_k_feat, 0),
    ]
    for axis in ("seq", "row"):
        cols = [full_sum(c, axis) for c in cols]
    return (
        block_out,
        grad_hidden,
        in_parts[0].T,
        cols[0],
        in_parts[1].T,
        cols[1],
        in_parts[2].T,
        cols[2],
        cols[3],
        in_parts[3],
        cols[4],
        cols[5],
    )


def solution(mesh):
    return jax.shard_map(
        local,
        mesh=mesh,
        in_specs=(
            P("row", ("seq", "head"), None),
            P("row", ("seq", "head"), None),
            P("row"),
            P("row", None),
            P(),
            P(),
            P(("row", "seq"), "head"),
            P(("row", "seq"), "head"),
            P(("row", "seq"), "head"),
            P("head", ("row", "seq")),
            P(("row", "seq"), "head"),
            P(("row", "seq"), "head"),
            P("head", ("row", "seq")),
            P(),
            P(None, "head"),
            P(),
            P(None, "head"),
            P(),
            P(None, "head"),
            P("head", None),
            P(),
            P("head", None, None),
            P("head", None, None),
        ),
        out_specs=(
            P("row", ("seq", "head"), None),
            P("row", ("seq", "head"), None),
            P(("row", "seq", "head"), None),
            P(None, "head"),
            P(("row", "seq", "head"), None),
            P(None, "head"),
            P(("row", "seq", "head"), None),
            P(None, "head"),
            P("head", None),
            P(None, ("row", "seq", "head")),
            P("head", None, None),
            P("head", None, None),
        ),
        check_vma=False,
    )
```

profile of v0, /device:TPU:0, one launch (start us, length us, event | category | flops | bytes accessed | tf_op | source)
XLA Modules:
  0.0 1532.8 jit_solution(3545589842110624116)
XLA Ops:
  128.2 29.6 %collective-permute-done.2 = bf16[256,768]{1,0:T(8,128)(2,1)} collective-permute-done((bf16[256,768]{1,0:T(8,128)(2,1)}, bf16[256,768]{1,0:T(8,128)(2,1)}, u32[]{:S(2)}, u32[]{:S(2)}) %collective-permute-start.2) | collective-permute-done | bytes 393248 | tf_op jit(solution)/shard_map/ppermute | solution.py:24
  176.8 12.3 collective-permute-done.13
  363.6 30.1 %collective-permute-done.15 = bf16[256,768]{1,0:T(8,128)(2,1)S(1)} collective-permute-done((bf16[256,768]{1,0:T(8,128)(2,1)}, bf16[256,768]{1,0:T(8,128)(2,1)S(1)}, u32[]{:S(2)}, u32[]{:S(2)}) %collective-permute-start.15) | collective-permute-done | bytes 393248 | tf_op jit(solution)/shard_map/ppermute | solution.py:32
  403.3 20.8 %fusion.251 = f32[1024,1536]{1,0:T(8,128)S(1)} fusion(bf16[1024,2048]{1,0:T(8,128)(2,1)S(1)} %bitcast.425, bf16[2048,1536]{1,0:T(8,128)(2,1)} %dynamic_update_slice.207), kind=kOutput, calls=%fused_computation.497 | convolution fusion | flops 6442450944 | bytes 16777216 | tf_op jit(solution)/shard_map/dot_general | solution.py:36
  450.7 14.4 fusion.246
  494.5 13.3 fusion.248
  533.4 11.7 fusion.102
  594.7 13.5 collective-permute-done.57
  611.1 27.1 %collective-permute-done.23 = bf16[2,4,128,65]{2,3,1,0:T(8,128)(2,1)S(1)} collective-permute-done((bf16[2,4,128,65]{2,3,1,0:T(8,128)(2,1)S(1)}, bf16[2,4,128,65]{2,3,1,0:T(8,128)(2,1)S(1)}, u32[]{:S(2)}, u32[]{:S(2)}) %collective-permute-start.23) | collective-permute-done | bytes 133152 | tf_op jit(solution)/shard_map/ppermute | solution.py:24
  662.2 14.3 fusion.250
  712.7 27.7 %collective-permute-done.51 = bf16[256,1536]{1,0:T(8,128)(2,1)S(1)} collective-permute-done((bf16[256,1536]{1,0:T(8,128)(2,1)}, bf16[256,1536]{1,0:T(8,128)(2,1)S(1)}, u32[]{:S(2)}, u32[]{:S(2)}) %collective-permute-start.51) | collective-permute-done | bytes 786464 | tf_op jit(solution)/shard_map/ppermute | solution.py:24
  758.7 15.5 %collective-permute-done.72 = bf16[256,1536]{1,0:T(8,128)(2,1)} collective-permute-done((bf16[256,1536]{1,0:T(8,128)(2,1)}, bf16[256,1536]{1,0:T(8,128)(2,1)}, u32[]{:S(2)}, u32[]{:S(2)}) %collective-permute-start.72) | collective-permute-done | bytes 786464 | tf_op jit(solution)/shard_map/ppermute | solution.py:24
  780.5 10.5 collective-permute-done.66
  793.9 13.9 collective-permute-done.59
  812.7 11.9 collective-permute-done.52
  825.6 15.5 %collective-permute-done.73 = bf16[256,1536]{1,0:T(8,128)(2,1)S(1)} collective-permute-done((bf16[256,1536]{1,0:T(8,128)(2,1)}, bf16[256,1536]{1,0:T(8,128)(2,1)S(1)}, u32[]{:S(2)}, u32[]{:S(2)}) %collective-permute-start.73) | collective-permute-done | bytes 786464 | tf_op jit(solution)/shard_map/ppermute | solution.py:24
  848.4 10.9 ffn_pre.11
  862.3 10.9 ffn_pre.10
  876.2 10.9 ffn_pre.9
  888.2 10.9 ffn_pre.8
  901.4 10.9 ffn_pre.15
  914.3 11.3 ffn_pre.14
  927.6 11.3 ffn_pre.13
  939.8 10.9 ffn_pre.12
  950.8 39.8 %ffn_post.3 = (bf16[1024,2048]{1,0:T(8,128)(2,1)}, bf16[1024,2048]{1,0:T(8,128)(2,1)}) custom-call(bf16[1024,512]{1,0:T(8,128)(2,1)S(1)} %get-tuple-element.53.refs_0_, bf16[1024,512]{1,0:T(8,128)(2,1)S(1)} %get-tuple-element.54.refs_1_, bf16[1024,512]{1,0:T(8,128)(2,1)S(1)} %get-tuple-element.55.refs_2_, bf16[1024,512]{1,0:T(8,128)(2,1)S(1)} %get-tuple-element.56.refs_3_, ...), custom_call_target="tpu_custom_call" | custom-call | flops 25769803776 | bytes 46137344 | tf_op jit(solution)/shard_map/ffn_post/pallas_call | solution.py:182
  997.2 39.3 %ffn_post.2 = (bf16[1024,2048]{1,0:T(8,128)(2,1)}, bf16[1024,2048]{1,0:T(8,128)(2,1)}) custom-call(bf16[1024,512]{1,0:T(8,128)(2,1)S(1)} %get-tuple-element.40.refs_0_, bf16[1024,512]{1,0:T(8,128)(2,1)S(1)} %get-tuple-element.41.refs_1_, bf16[1024,512]{1,0:T(8,128)(2,1)S(1)} %get-tuple-element.42.refs_2_, bf16[1024,512]{1,0:T(8,128)(2,1)S(1)} %get-tuple-element.43.refs_3_, ...), custom_call_target="tpu_custom_call" | custom-call | flops 25769803776 | bytes 46137344 | tf_op jit(solution)/shard_map/ffn_post/pallas_call | solution.py:182
  1050.2 41.0 %collective-permute-done.83 = bf16[2,256,2048]{2,1,0:T(8,128)(2,1)S(1)} collective-permute-done((bf16[2,256,2048]{2,1,0:T(8,128)(2,1)S(1)}, bf16[2,256,2048]{2,1,0:T(8,128)(2,1)S(1)}, u32[]{:S(2)}, u32[]{:S(2)}) %collective-permute-start.83) | collective-permute-done | bytes 2097184 | tf_op jit(solution)/shard_map/ppermute | solution.py:32
  1092.4 42.9 %collective-permute-done.80 = bf16[2,256,2048]{2,1,0:T(8,128)(2,1)S(1)} collective-permute-done((bf16[2,256,2048]{2,1,0:T(8,128)(2,1)}, bf16[2,256,2048]{2,1,0:T(8,128)(2,1)S(1)}, u32[]{:S(2)}, u32[]{:S(2)}) %collective-permute-start.80) | collective-permute-done | bytes 2097184 | tf_op jit(solution)/shard_map/ppermute | solution.py:32
  1250.6 14.3 multiply_reduce_fusion.2
  1265.0 14.4 add_convert_fusion
  1349.9 11.9 convolution_bitcast_fusion
  1361.8 30.1 %fusion.4 = f32[2,576,1,4,128]{4,2,3,1,0:T(1,128)} fusion(pred[2,9,576,1,1]{1,3,4,2,0:T(4,128)(4,1)} %copy.503, f32[2,9,576,4,128]{4,2,1,3,0:T(8,128)} %convolution_bitcast_fusion), kind=kOutput, calls=%fused_computation.4 | convolution fusion | flops 63700992 | bytes 23603328 | tf_op jit(solution)/shard_map/rbe,rbegf->regf/dot_general | solution.py:505
  (1011 shorter events, 924.6 us)
Async XLA Ops:
  78.9 79.2 %collective-permute-start.60 = (bf16[256,1536]{1,0:T(8,128)(2,1)}, bf16[256,1536]{1,0:T(8,128)(2,1)}, u32[]{:S(2)}, u32[]{:S(2)}) collective-permute-start(bf16[256,1536]{1,0:T(8,128)(2,1)} %get-tuple-element.127), channel_id=1, source_target_pairs={{0,8},{8,16},{16,24},{24,0},{1,9},{9,17},{17,25},{25,1},{2,10},{10... | collective-permute-start | bytes 2359304 | tf_op jit(solution)/shard_map/ppermute | solution.py:24
  90.5 69.4 %collective-permute-start.53 = (bf16[256,1536]{1,0:T(8,128)(2,1)}, bf16[256,1536]{1,0:T(8,128)(2,1)}, u32[]{:S(2)}, u32[]{:S(2)}) collective-permute-start(bf16[256,1536]{1,0:T(8,128)(2,1)} %get-tuple-element.129), channel_id=1, source_target_pairs={{0,8},{8,16},{16,24},{24,0},{1,9},{9,17},{17,25},{25,1},{2,10},{10... | collective-permute-start | bytes 2359304 | tf_op jit(solution)/shard_map/ppermute | solution.py:24
  104.5 55.9 %collective-permute-start.46 = (bf16[256,1536]{1,0:T(8,128)(2,1)}, bf16[256,1536]{1,0:T(8,128)(2,1)}, u32[]{:S(2)}, u32[]{:S(2)}) collective-permute-start(bf16[256,1536]{1,0:T(8,128)(2,1)} %get-tuple-element.131), channel_id=1, source_target_pairs={{0,8},{8,16},{16,24},{24,0},{1,9},{9,17},{17,25},{25,1},{2,10},{10... | collective-permute-start | bytes 2359304 | tf_op jit(solution)/shard_map/ppermute | solution.py:24
  106.1 56.0 %collective-permute-start.67 = (bf16[256,1536]{1,0:T(8,128)(2,1)}, bf16[256,1536]{1,0:T(8,128)(2,1)}, u32[]{:S(2)}, u32[]{:S(2)}) collective-permute-start(bf16[256,1536]{1,0:T(8,128)(2,1)} %get-tuple-element.125), channel_id=1, source_target_pairs={{0,8},{8,16},{16,24},{24,0},{1,9},{9,17},{17,25},{25,1},{2,10},{10... | collective-permute-start | bytes 2359304 | tf_op jit(solution)/shard_map/ppermute | solution.py:24
  107.7 50.2 %collective-permute-start.2 = (bf16[256,768]{1,0:T(8,128)(2,1)}, bf16[256,768]{1,0:T(8,128)(2,1)}, u32[]{:S(2)}, u32[]{:S(2)}) collective-permute-start(bf16[256,768]{1,0:T(8,128)(2,1)} %collective-permute-done.1), channel_id=1, source_target_pairs={{0,8},{8,16},{16,24},{24,0},{1,9},{9,17},{17,25},{25,1},{2,10},{10... | collective-permute-start | bytes 1179656 | tf_op jit(solution)/shard_map/ppermute | solution.py:24
  162.1 73.2 %collective-permute-start.10 = (bf16[256,768]{1,0:T(8,128)(2,1)}, bf16[256,768]{1,0:T(8,128)(2,1)}, u32[]{:S(2)}, u32[]{:S(2)}) collective-permute-start(bf16[256,768]{1,0:T(8,128)(2,1)} %collective-permute-done.2), channel_id=1, source_target_pairs={{0,2},{1,3},{2,0},{3,1},{4,6},{5,7},{6,4},{7,5},{8,10},{9,11},{10,... | collective-permute-start | bytes 1179656 | tf_op jit(solution)/shard_map/ppermute | solution.py:32
  167.3 68.1 %collective-permute-start.3 = (bf16[256,768]{1,0:T(8,128)(2,1)}, bf16[256,768]{1,0:T(8,128)(2,1)}, u32[]{:S(2)}, u32[]{:S(2)}) collective-permute-start(bf16[256,768]{1,0:T(8,128)(2,1)} %collective-permute-done.2), channel_id=1, source_target_pairs={{0,8},{8,16},{16,24},{24,0},{1,9},{9,17},{17,25},{25,1},{2,10},{10... | collective-permute-start | bytes 1179656 | tf_op jit(solution)/shard_map/ppermute | solution.py:24
  174.0 65.5 %collective-permute-start.14 = (bf16[256,768]{1,0:T(8,128)(2,1)}, bf16[256,768]{1,0:T(8,128)(2,1)}, u32[]{:S(2)}, u32[]{:S(2)}) collective-permute-start(bf16[256,768]{1,0:T(8,128)(2,1)} %collective-permute-done.6), channel_id=1, source_target_pairs={{0,2},{1,3},{2,0},{3,1},{4,6},{5,7},{6,4},{7,5},{8,10},{9,11},{10,... | collective-permute-start | bytes 1179656 | tf_op jit(solution)/shard_map/ppermute | solution.py:32
  176.8 222.2 %collective-permute-start = (bf16[2,256,2048]{2,1,0:T(8,128)(2,1)}, bf16[2,256,2048]{2,1,0:T(8,128)(2,1)}, u32[]{:S(2)}, u32[]{:S(2)}) collective-permute-start(bf16[2,256,2048]{2,1,0:T(8,128)(2,1)} %fusion.22), channel_id=1, source_target_pairs={{0,1},{1,0},{2,3},{3,2},{4,5},{5,4},{6,7},{7,6},{8,9},{9,8},{10,11... | collective-permute-start | bytes 6291464 | tf_op jit(solution)/shard_map/ppermute | solution.py:28
  235.4 111.2 %collective-permute-start.61 = (bf16[256,1536]{1,0:T(8,128)(2,1)}, bf16[256,1536]{1,0:T(8,128)(2,1)}, u32[]{:S(2)}, u32[]{:S(2)}) collective-permute-start(bf16[256,1536]{1,0:T(8,128)(2,1)} %collective-permute-done.60), channel_id=1, source_target_pairs={{0,8},{8,16},{16,24},{24,0},{1,9},{9,17},{17,25},{25,1},{2,10},{10... | collective-permute-start | bytes 2359304 | tf_op jit(solution)/shard_map/ppermute | solution.py:24
  237.5 117.9 %collective-permute-start.54 = (bf16[256,1536]{1,0:T(8,128)(2,1)}, bf16[256,1536]{1,0:T(8,128)(2,1)}, u32[]{:S(2)}, u32[]{:S(2)}) collective-permute-start(bf16[256,1536]{1,0:T(8,128)(2,1)} %collective-permute-done.53), channel_id=1, source_target_pairs={{0,8},{8,16},{16,24},{24,0},{1,9},{9,17},{17,25},{25,1},{2,10},{10... | collective-permute-start | bytes 2359304 | tf_op jit(solution)/shard_map/ppermute | solution.py:24
  243.5 114.0 %collective-permute-start.47 = (bf16[256,1536]{1,0:T(8,128)(2,1)}, bf16[256,1536]{1,0:T(8,128)(2,1)}, u32[]{:S(2)}, u32[]{:S(2)}) collective-permute-start(bf16[256,1536]{1,0:T(8,128)(2,1)} %collective-permute-done.46), channel_id=1, source_target_pairs={{0,8},{8,16},{16,24},{24,0},{1,9},{9,17},{17,25},{25,1},{2,10},{10... | collective-permute-start | bytes 2359304 | tf_op jit(solution)/shard_map/ppermute | solution.py:24
  247.6 112.0 %collective-permute-start.68 = (bf16[256,1536]{1,0:T(8,128)(2,1)}, bf16[256,1536]{1,0:T(8,128)(2,1)}, u32[]{:S(2)}, u32[]{:S(2)}) collective-permute-start(bf16[256,1536]{1,0:T(8,128)(2,1)} %collective-permute-done.67), channel_id=1, source_target_pairs={{0,8},{8,16},{16,24},{24,0},{1,9},{9,17},{17,25},{25,1},{2,10},{10... | collective-permute-start | bytes 2359304 | tf_op jit(solution)/shard_map/ppermute | solution.py:24
  346.5 396.8 %collective-permute-start.77 = (bf16[2,256,2048]{2,1,0:T(8,128)(2,1)}, bf16[2,256,2048]{2,1,0:T(8,128)(2,1)}, u32[]{:S(2)}, u32[]{:S(2)}) collective-permute-start(bf16[2,256,2048]{2,1,0:T(8,128)(2,1)} %broadcast_select_fusion), channel_id=1, source_target_pairs={{0,2},{1,3},{2,0},{3,1},{4,6},{5,7},{6,4},{7,5},{8,10},{9,11},{10,... | collective-permute-start | bytes 6291464 | tf_op jit(solution)/shard_map/ppermute | solution.py:32
  355.5 123.6 %collective-permute-start.45 = (bf16[2,256,2048]{2,1,0:T(8,128)(2,1)}, bf16[2,256,2048]{2,1,0:T(8,128)(2,1)}, u32[]{:S(2)}, u32[]{:S(2)}) collective-permute-start(bf16[2,256,2048]{2,1,0:T(8,128)(2,1)} %broadcast_select_fusion), channel_id=1, source_target_pairs={{0,1},{1,0},{2,3},{3,2},{4,5},{5,4},{6,7},{7,6},{8,9},{9,8},{10,11... | collective-permute-start | bytes 6291464 | tf_op jit(solution)/shard_map/ppermute | solution.py:28
  359.6 211.1 %collective-permute-start.63 = (bf16[256,1536]{1,0:T(8,128)(2,1)}, bf16[256,1536]{1,0:T(8,128)(2,1)}, u32[]{:S(2)}, u32[]{:S(2)}) collective-permute-start(bf16[256,1536]{1,0:T(8,128)(2,1)} %get-tuple-element.127), channel_id=1, source_target_pairs={{0,4},{4,0},{1,5},{5,1},{2,6},{6,2},{3,7},{7,3},{8,12},{12,8},{9,1... | collective-permute-start | bytes 2359304 | tf_op jit(solution)/shard_map/ppermute | solution.py:24
  393.7 180.0 %collective-permute-start.64 = (bf16[256,1536]{1,0:T(8,128)(2,1)}, bf16[256,1536]{1,0:T(8,128)(2,1)}, u32[]{:S(2)}, u32[]{:S(2)}) collective-permute-start(bf16[256,1536]{1,0:T(8,128)(2,1)} %collective-permute-done.60), channel_id=1, source_target_pairs={{0,4},{4,0},{1,5},{5,1},{2,6},{6,2},{3,7},{7,3},{8,12},{12,8},{9,1... | collective-permute-start | bytes 2359304 | tf_op jit(solution)/shard_map/ppermute | solution.py:24
  398.9 178.0 %collective-permute-start.65 = (bf16[256,1536]{1,0:T(8,128)(2,1)}, bf16[256,1536]{1,0:T(8,128)(2,1)}, u32[]{:S(2)}, u32[]{:S(2)}) collective-permute-start(bf16[256,1536]{1,0:T(8,128)(2,1)} %collective-permute-done.61), channel_id=1, source_target_pairs={{0,4},{4,0},{1,5},{5,1},{2,6},{6,2},{3,7},{7,3},{8,12},{12,8},{9,1... | collective-permute-start | bytes 2359304 | tf_op jit(solution)/shard_map/ppermute | solution.py:24
  513.4 55.0 %collective-permute-start.62 = (bf16[256,1536]{1,0:T(8,128)(2,1)}, bf16[256,1536]{1,0:T(8,128)(2,1)}, u32[]{:S(2)}, u32[]{:S(2)}) collective-permute-start(bf16[256,1536]{1,0:T(8,128)(2,1)} %collective-permute-done.61), channel_id=1, source_target_pairs={{0,8},{8,16},{16,24},{24,0},{1,9},{9,17},{17,25},{25,1},{2,10},{10... | collective-permute-start | bytes 2359304 | tf_op jit(solution)/shard_map/ppermute | solution.py:24
  576.9 129.2 %collective-permute-start.49 = (bf16[256,1536]{1,0:T(8,128)(2,1)}, bf16[256,1536]{1,0:T(8,128)(2,1)}, u32[]{:S(2)}, u32[]{:S(2)}) collective-permute-start(bf16[256,1536]{1,0:T(8,128)(2,1)} %get-tuple-element.131), channel_id=1, source_target_pairs={{0,4},{4,0},{1,5},{5,1},{2,6},{6,2},{3,7},{7,3},{8,12},{12,8},{9,1... | collective-permute-start | bytes 2359304 | tf_op jit(solution)/shard_map/ppermute | solution.py:24
  582.4 127.0 %collective-permute-start.50 = (bf16[256,1536]{1,0:T(8,128)(2,1)}, bf16[256,1536]{1,0:T(8,128)(2,1)}, u32[]{:S(2)}, u32[]{:S(2)}) collective-permute-start(bf16[256,1536]{1,0:T(8,128)(2,1)} %collective-permute-done.46), channel_id=1, source_target_pairs={{0,4},{4,0},{1,5},{5,1},{2,6},{6,2},{3,7},{7,3},{8,12},{12,8},{9,1... | collective-permute-start | bytes 2359304 | tf_op jit(solution)/shard_map/ppermute | solution.py:24
  638.2 62.8 %collective-permute-start.58 = (bf16[256,1536]{1,0:T(8,128)(2,1)}, bf16[256,1536]{1,0:T(8,128)(2,1)}, u32[]{:S(2)}, u32[]{:S(2)}) collective-permute-start(bf16[256,1536]{1,0:T(8,128)(2,1)} %collective-permute-done.54), channel_id=1, source_target_pairs={{0,4},{4,0},{1,5},{5,1},{2,6},{6,2},{3,7},{7,3},{8,12},{12,8},{9,1... | collective-permute-start | bytes 2359304 | tf_op jit(solution)/shard_map/ppermute | solution.py:24
  639.8 63.4 %collective-permute-start.48 = (bf16[256,1536]{1,0:T(8,128)(2,1)}, bf16[256,1536]{1,0:T(8,128)(2,1)}, u32[]{:S(2)}, u32[]{:S(2)}) collective-permute-start(bf16[256,1536]{1,0:T(8,128)(2,1)} %collective-permute-done.47), channel_id=1, source_target_pairs={{0,8},{8,16},{16,24},{24,0},{1,9},{9,17},{17,25},{25,1},{2,10},{10... | collective-permute-start | bytes 2359304 | tf_op jit(solution)/shard_map/ppermute | solution.py:24
  745.6 96.4 %collective-permute-start.78 = (bf16[2,256,2048]{2,1,0:T(8,128)(2,1)}, bf16[2,256,2048]{2,1,0:T(8,128)(2,1)S(1)}, u32[]{:S(2)}, u32[]{:S(2)}) collective-permute-start(bf16[2,256,2048]{2,1,0:T(8,128)(2,1)} %collective-permute-done.77), channel_id=1, source_target_pairs={{0,1},{1,0},{2,3},{3,2},{4,5},{5,4},{6,7},{7,6},{8,9},{9,8},{10,11... | collective-permute-start | bytes 6291464 | tf_op jit(solution)/shard_map/ppermute | solution.py:28
  757.3 50.5 %collective-permute-start.59 = (bf16[256,1536]{1,0:T(8,128)(2,1)}, bf16[256,1536]{1,0:T(8,128)(2,1)S(1)}, u32[]{:S(2)}, u32[]{:S(2)}) collective-permute-start(bf16[256,1536]{1,0:T(8,128)(2,1)} %copy-done.111), channel_id=1, source_target_pairs={{0,4},{4,0},{1,5},{5,1},{2,6},{6,2},{3,7},{7,3},{8,12},{12,8},{9,1... | collective-permute-start | bytes 2359304 | tf_op jit(solution)/shard_map/ppermute | solution.py:24
  774.2 71.9 %collective-permute-start.75 = (bf16[2,256,2048]{2,1,0:T(8,128)(2,1)S(1)}, bf16[2,256,2048]{2,1,0:T(8,128)(2,1)S(1)}, u32[]{:S(2)}, u32[]{:S(2)}) collective-permute-start(bf16[2,256,2048]{2,1,0:T(8,128)(2,1)S(1)} %multiply_convert_fusion.2), channel_id=1, source_target_pairs={{0,2},{1,3},{2,0},{3,1},{4,6},{5,7},{6,4},{7,5},{8,10},{9,11},{10,... | collective-permute-start | bytes 6291464 | tf_op jit(solution)/shard_map/ppermute | solution.py:32
  776.3 69.8 %collective-permute-start.44 = (bf16[2,256,2048]{2,1,0:T(8,128)(2,1)S(1)}, bf16[2,256,2048]{2,1,0:T(8,128)(2,1)S(1)}, u32[]{:S(2)}, u32[]{:S(2)}) collective-permute-start(bf16[2,256,2048]{2,1,0:T(8,128)(2,1)S(1)} %multiply_convert_fusion.2), channel_id=1, source_target_pairs={{0,1},{1,0},{2,3},{3,2},{4,5},{5,4},{6,7},{7,6},{8,9},{9,8},{10,11... | collective-permute-start | bytes 6291464 | tf_op jit(solution)/shard_map/ppermute | solution.py:28
  846.1 53.0 %collective-permute-start.76 = (bf16[2,256,2048]{2,1,0:T(8,128)(2,1)S(1)}, bf16[2,256,2048]{2,1,0:T(8,128)(2,1)S(1)}, u32[]{:S(2)}, u32[]{:S(2)}) collective-permute-start(bf16[2,256,2048]{2,1,0:T(8,128)(2,1)S(1)} %collective-permute-done.75), channel_id=1, source_target_pairs={{0,1},{1,0},{2,3},{3,2},{4,5},{5,4},{6,7},{7,6},{8,9},{9,8},{10,11... | collective-permute-start | bytes 6291464 | tf_op jit(solution)/shard_map/ppermute | solution.py:28
  994.8 51.5 %collective-permute-start.79 = (bf16[2,256,2048]{2,1,0:T(8,128)(2,1)}, bf16[2,256,2048]{2,1,0:T(8,128)(2,1)}, u32[]{:S(2)}, u32[]{:S(2)}) collective-permute-start(bf16[2,256,2048]{2,1,0:T(8,128)(2,1)} %bitcast.57), channel_id=1, source_target_pairs={{0,1},{1,0},{2,3},{3,2},{4,5},{5,4},{6,7},{7,6},{8,9},{9,8},{10,11... | collective-permute-start | bytes 6291464 | tf_op jit(solution)/shard_map/ppermute | solution.py:28
  1050.2 85.2 %collective-permute-start.80 = (bf16[2,256,2048]{2,1,0:T(8,128)(2,1)}, bf16[2,256,2048]{2,1,0:T(8,128)(2,1)S(1)}, u32[]{:S(2)}, u32[]{:S(2)}) collective-permute-start(bf16[2,256,2048]{2,1,0:T(8,128)(2,1)} %fusion.33), channel_id=1, source_target_pairs={{0,2},{1,3},{2,0},{3,1},{4,6},{5,7},{6,4},{7,5},{8,10},{9,11},{10,... | collective-permute-start | bytes 6291464 | tf_op jit(solution)/shard_map/ppermute | solution.py:32
  1209.3 132.5 %collective-permute-start.86 = (bf16[2,4,128,65]{2,3,1,0:T(8,128)(2,1)}, bf16[2,4,128,65]{2,3,1,0:T(8,128)(2,1)}, u32[]{:S(2)}, u32[]{:S(2)}) collective-permute-start(bf16[2,4,128,65]{2,3,1,0:T(8,128)(2,1)} %pad_maximum_fusion.23), channel_id=1, source_target_pairs={{0,2},{1,3},{2,0},{3,1},{4,6},{5,7},{6,4},{7,5},{8,10},{9,11},{10,... | collective-permute-start | bytes 399368 | tf_op jit(solution)/shard_map/ppermute | solution.py:32
  1211.1 136.9 %collective-permute-start.85 = (bf16[2,4,128,65]{2,3,1,0:T(8,128)(2,1)}, bf16[2,4,128,65]{2,3,1,0:T(8,128)(2,1)}, u32[]{:S(2)}, u32[]{:S(2)}) collective-permute-start(bf16[2,4,128,65]{2,3,1,0:T(8,128)(2,1)} %pad_maximum_fusion.23), channel_id=1, source_target_pairs={{0,4},{4,0},{1,5},{5,1},{2,6},{6,2},{3,7},{7,3},{8,12},{12,8},{9,1... | collective-permute-start | bytes 399368 | tf_op jit(solution)/shard_map/ppermute | solution.py:24
  (304 other events, 8900.3 us)
where the time goes:
time: 1540 us; the launch traced here: 1530 us
  local copies, waits for them, and re-layouts  422 us (27%)
  waiting for transfers between devices  381 us (25%)
  matrix products  238 us (15%)
  other arithmetic  187 us (12%)
  Pallas kernels  167 us (11%)
  starting transfers between devices  133 us (9%)
    ppermute x53, waiting for transfers between devices, shift(): lax.ppermute(block, axis, [(i, (i + distance) % size) for i in range(size)])  199 us
    dynamic_update_slice x60, local copies, waits for them, and re-layouts, assemble(): whole = lax.dynamic_update_slice(whole, block, (place * depth, column))  185 us
    ppermute x34, waiting for transfers between devices, flip_x(): lax.ppermute(block, 'head', [(i, i ^ 2) for i in range(lax.axis_size('hea...  162 us
    pallas_call x8, Pallas kernels, ffn_pre(): pl.pallas_call(ffn_pre_kernel, grid=(tokens // tile,), in_specs=[pl.Block...  88 us
    pallas_call x2, Pallas kernels, ffn_post(): pl.pallas_call(functools.partial(ffn_post_kernel, chunks), grid=(depth //...  79.1 us
    dot_general x24, matrix products, dot(): return lax.dot_general(a, b, (dims, ((), ())), preferred_element_type=F32)  65.4 us
    unnamed x449, local copies, waits for them, and re-layouts  57.9 us
    ppermute x53, starting transfers between devices, shift(): lax.ppermute(block, axis, [(i, (i + distance) % size) for i in range(size)])  55.9 us
  transfers between devices with their start and end apart: 123, of which 43 were waited for; matrix products, arithmetic and copies ran while one was open for 45% of the time, Pallas kernels for 5%

commit v1 on v0

v1 whole, which is shorter than its diff:
```python
import functools

import jax
import jax.numpy as jnp
from jax import lax
from jax.experimental import pallas as pl
from jax.experimental.pallas import tpu as pltpu
from jax.sharding import PartitionSpec as P

HD = 64
RANK = 8
WIN = 64
FF_CHUNKS = 4

NORM_EPS = 1e-05
ADAPTER_SCALE = 2.0
F32 = jnp.float32
NT = ((1,), (1,))
TN = ((0,), (0,))
BF16 = jnp.bfloat16


def shift(block, axis, distance):
    size = lax.axis_size(axis)
    return lax.ppermute(block, axis, [(i, (i + distance) % size) for i in range(size)])


def flip_core(block):
    return lax.ppermute(block, "head", [(i, i ^ 1) for i in range(lax.axis_size("head"))])


def flip_x(block):
    return lax.ppermute(block, "head", [(i, i ^ 2) for i in range(lax.axis_size("head"))])


def kernel_call(
    kernel, args, after, *, grid, in_specs, out_specs, out_shape, name, prefetch=0, scratch=(), cost=None
):
    count = len(args)

    def body(*refs):
        kernel(*refs[:count], *refs[count + len(after) :])

    return pl.pallas_call(
        body,
        grid_spec=pltpu.PrefetchScalarGridSpec(
            num_scalar_prefetch=prefetch,
            grid=grid,
            in_specs=list(in_specs) + [pl.BlockSpec(memory_space=pl.ANY)] * len(after),
            out_specs=out_specs,
            scratch_shapes=list(scratch),
        ),
        out_shape=out_shape,
        compiler_params=pltpu.CompilerParams(vmem_limit_bytes=60 * 2**20),
        cost_estimate=cost,
        name=name,
    )(*args, *after)


def copy_kernel(src_ref, dst_ref):
    dst_ref[...] = src_ref[...]


def hold(value, after):
    flat = value.reshape(-1, value.shape[-1])
    tile = min(256, flat.shape[0])
    block = pl.BlockSpec((tile, flat.shape[1]), lambda i: (i, 0))
    held = kernel_call(
        copy_kernel, [flat], after, grid=(flat.shape[0] // tile,), in_specs=[block], out_specs=block,
        out_shape=jax.ShapeDtypeStruct(flat.shape, flat.dtype), name="hold",
    )
    return held.reshape(value.shape)


def dot(a, b, dims=((1,), (0,))):
    return lax.dot_general(a, b, (dims, ((), ())), preferred_element_type=F32)


def tie(value, *after):
    return lax.optimization_barrier((value,) + after)[0]


def rms_scaled(values, gain_vec):
    return (
        values * lax.rsqrt(jnp.mean(values * values, axis=-1, keepdims=True) + NORM_EPS) * gain_vec
    )


def rms_back(values, gain_vec, grad_in):
    factor = lax.rsqrt(jnp.mean(values * values, axis=-1, keepdims=True) + NORM_EPS)
    scaled = gain_vec * grad_in
    return factor * scaled - values * factor**3 * jnp.mean(values * scaled, axis=-1, keepdims=True)


def scatter_sum(parts, axis):
    size, place = lax.axis_size(axis), lax.axis_index(axis)
    total = lax.dynamic_index_in_dim(parts, place, 0, keepdims=False)
    for k in range(1, size):
        away = lax.dynamic_index_in_dim(parts, lax.rem(place + k, size), 0, keepdims=False)
        total = total + shift(away, axis, k)
    return total


def full_sum(part, axis):
    size = lax.axis_size(axis)
    step = 1
    while step < size:
        sent = part.astype(BF16)
        got = lax.ppermute(sent, axis, [(i, i ^ step) for i in range(size)])
        part = sent.astype(F32) + got.astype(F32)
        step *= 2
    return part


def gather_plan(rows, seqs, weights):
    free = {"row": 0.0, "seq": 0.0, "x": 0.0}
    running = []
    plan = []

    def begin(now, starts):
        for t in starts:
            w, link = t[0], t[1]
            end = max(now, free[link]) + weights[w][0]
            free[link] = end
            running.append((end, len(plan), len(running), t))
        return starts

    def spread(w, k, l):
        starts = []
        row_first = weights[w][2]
        if (l == 0 or not row_first) and k + 1 < rows:
            starts.append((w, "row", k + 1, l))
        if (k == 0 or row_first) and l + 1 < seqs:
            starts.append((w, "seq", k, l + 1))
        if weights[w][1]:
            starts.append((w, "x", k, l))
        return starts

    first = [t for w in range(len(weights)) if weights[w][3] == 0 for t in spread(w, 0, 0)]
    plan.append((None, begin(0.0, first)))
    done = 0
    while running:
        event = min(running)
        running.remove(event)
        now, t = event[0], event[3]
        done += 1
        starts = [] if t[1] == "x" else spread(t[0], t[2], t[3])
        for w in range(len(weights)):
            if weights[w][3] == done:
                starts = starts + spread(w, 0, 0)
        plan.append((t, begin(now, starts)))
    return plan


def gather_kernel(plan, rows, seqs, parts, over_x, small_count, *refs):
    count = len(over_x)
    inputs, refs = refs[: count + small_count + 2], refs[count + small_count + 2 :]
    shards, smalls = inputs[:count], inputs[count : count + small_count]
    hidden, cot = inputs[count + small_count :]
    wholes, refs = refs[:count], refs[count:]
    small_outs, refs = refs[:small_count], refs[small_count:]
    hidden_out, cot_mine, cot_away = refs[:3]
    send_sem, recv_sem, copy_sem, more_send, more_recv = refs[3:]
    row, seq, head = lax.axis_index("row"), lax.axis_index("seq"), lax.axis_index("head")
    x_place = head // 2
    across = {"head": lax.rem(head + 2, 4)}
    partner = {"head": head + 1 - 2 * lax.rem(head, 2)}
    away = {
        "row": {"row": lax.rem(row + 1, rows)},
        "seq": {"seq": lax.rem(seq + 1, seqs)},
        "x": across,
    }
    barrier = pltpu.get_barrier_semaphore()
    sources = (
        {"row": lax.rem(row + rows - 1, rows)},
        {"seq": lax.rem(seq + seqs - 1, seqs)},
        across,
        partner,
    )
    for source in sources:
        pl.semaphore_signal(
            barrier, inc=1, device_id=source, device_id_type=pl.DeviceIdType.MESH
        )
    pl.semaphore_wait(barrier, len(sources))

    def slot(p, k, l):
        w, columns = parts[p][0], pl.ds(*parts[p][1])
        depth = shards[w].shape[0]
        place = lax.rem(row - k + rows, rows) * seqs + lax.rem(seq - l + seqs, seqs)
        at = pl.ds(pl.multiple_of(place * depth, depth), depth)
        return wholes[w].at[x_place, at, columns] if over_x[w] else wholes[w].at[at, columns]

    number = {}
    last_x = 0
    for i, (event, starts) in enumerate(plan):
        for t in starts:
            number[t] = len(number)
            if t[1] == "x":
                last_x = i

    def remote(src, dst, send, recv, device):
        return pltpu.make_async_remote_copy(
            src_ref=src, dst_ref=dst, send_sem=send, recv_sem=recv, device_id=device,
            device_id_type=pl.DeviceIdType.MESH,
        )

    def transfer(t):
        w, link, k, l = t
        source = {"row": (k - 1, l), "seq": (k, l - 1), "x": (k, l)}[link]
        dst = slot(w, *source)
        n = number[t]
        src = shards[parts[w][0]].at[:, pl.ds(*parts[w][1])] if source == (0, 0) else dst
        return remote(src, dst, send_sem.at[n], recv_sem.at[n], away[link])

    def more(i, src, dst, device):
        return remote(src, dst, more_send.at[i], more_recv.at[i], device)

    early = [more(i, a, b, across) for i, (a, b) in enumerate(zip(smalls, small_outs))]
    early.append(more(small_count, hidden, hidden_out, partner))
    early.append(more(small_count + 1, cot, cot_mine.at[1], partner))
    cot_x = more(small_count + 2, cot, cot_away.at[0], across)
    cot_last = more(small_count + 3, cot_away.at[0], cot_away.at[1], partner)
    own = [
        pltpu.make_async_copy(
            shards[w].at[:, pl.ds(*columns)], slot(p, 0, 0), copy_sem.at[p]
        )
        for p, (w, columns) in enumerate(parts)
    ] + [pltpu.make_async_copy(cot, cot_mine.at[0], copy_sem.at[len(parts)])]
    for i, (event, starts) in enumerate(plan):
        if event is not None:
            transfer(event).wait_recv()
        for t in starts:
            transfer(t).start()
        if event is None:
            for copy in early + own:
                copy.start()
        if i == last_x:
            cot_x.start()
    cot_x.wait()
    cot_last.start()
    for t in number:
        transfer(t).wait_send()
    for copy in early + own + [cot_last]:
        copy.wait()


def gather(shards, over_x, pieces, smalls, hidden, cot):
    rows, seqs = lax.axis_size("row"), lax.axis_size("seq")
    plan = gather_plan(
        rows,
        seqs,
        [(float(shards[w].shape[0] * c[1]), over_x[w], first, later) for w, c, first, later in pieces],
    )
    parts = [(w, c) for w, c, _, _ in pieces]
    total = sum(len(starts) for _, starts in plan)
    shapes = []
    for shard, x in zip(shards, over_x):
        depth, width = shard.shape
        whole = (rows * seqs * depth, width)
        shapes.append(jax.ShapeDtypeStruct(((2,) + whole) if x else whole, shard.dtype))
    same = lambda v: jax.ShapeDtypeStruct(v.shape, v.dtype)
    twice = jax.ShapeDtypeStruct((2,) + cot.shape, cot.dtype)
    shapes += [same(v) for v in smalls] + [same(hidden), twice, twice]
    more = len(smalls) + 4
    place = pl.BlockSpec(memory_space=pl.ANY)
    outs = pl.pallas_call(
        functools.partial(gather_kernel, plan, rows, seqs, parts, over_x, len(smalls)),
        out_shape=shapes,
        in_specs=[place] * (len(shards) + len(smalls) + 2),
        out_specs=[place] * len(shapes),
        scratch_shapes=[
            pltpu.SemaphoreType.DMA((total,)),
            pltpu.SemaphoreType.DMA((total,)),
            pltpu.SemaphoreType.DMA((len(parts) + 1,)),
            pltpu.SemaphoreType.DMA((more,)),
            pltpu.SemaphoreType.DMA((more,)),
        ],
        compiler_params=pltpu.CompilerParams(collective_id=0, has_side_effects=True),
        name="gather",
    )(*shards, *smalls, hidden, cot)
    n = len(shards)
    return outs[:n], outs[n : n + len(smalls)], outs[-3:]


def ffn_pre_kernel(
    share_len, slots, live_ref, x_ref, more_ref, cot_ref, w_ref, mixed_ref, gg_ref, gu_ref
):
    tile, width = mixed_ref.shape
    first = pl.program_id(0) < pl.num_programs(0) // 2
    slot = lax.rem(pl.program_id(0) * tile // share_len, slots)
    live = (slot < live_ref[0]).astype(F32)
    x, cot = jnp.where(first, x_ref[...], more_ref[...]), cot_ref[...]
    gate = dot(x, w_ref[:, :width])
    up = dot(x, w_ref[:, width : 2 * width])
    gm = dot(cot, w_ref[:, 2 * width :]) * live
    sig = jax.nn.sigmoid(gate)
    silu = gate * sig
    mixed_ref[...] = (silu * up).astype(BF16)
    gg_ref[...] = (gm * up * (sig + silu * (1.0 - sig))).astype(BF16)
    gu_ref[...] = (gm * silu).astype(BF16)


def ffn_pre(x, cot, w, live_rows, share_len, slots, after=()):
    tokens, depth = cot.shape
    width = w.shape[1] // 3
    tile = min(256, share_len)
    half = tokens // tile // 2
    out = jax.ShapeDtypeStruct((tokens, width), BF16)
    return kernel_call(
        functools.partial(ffn_pre_kernel, share_len, slots),
        [live_rows, x[0], x[1], cot, w],
        after,
        prefetch=1,
        grid=(tokens // tile,),
        in_specs=[
            pl.BlockSpec((tile, depth), lambda i, *_: (jnp.minimum(i, half - 1), 0)),
            pl.BlockSpec((tile, depth), lambda i, *_: (jnp.maximum(i - half, 0), 0)),
            pl.BlockSpec((tile, depth), lambda i, *_: (i, 0)),
            pl.BlockSpec((depth, 3 * width), lambda i, *_: (0, 0)),
        ],
        out_specs=[pl.BlockSpec((tile, width), lambda i, *_: (i, 0))] * 3,
        out_shape=[out, out, out],
        cost=pl.CostEstimate(
            flops=6 * tokens * depth * width,
            bytes_accessed=4 * tokens * depth + 6 * depth * width + 6 * tokens * width,
            transcendentals=tokens * width,
        ),
        name="ffn_pre",
    )


def ffn_post_kernel(chunks, start, lhs_count, *refs):
    out_ref = refs[-1]
    weights = refs[lhs_count * chunks : -1]
    width = refs[0].shape[1]
    total = None
    for j in range(chunks):
        for i in range(lhs_count):
            at = (start + i) * width
            part = dot(refs[lhs_count * j + i][...], weights[j][:, at : at + width], ((1,), (1,)))
            total = part if total is None else total + part
    out_ref[...] = total.astype(BF16)


def ffn_post(acts, weights, start, name, after=()):
    chunks, lhs_count = len(weights), len(acts[0])
    tokens, width = acts[0][0].shape
    depth = weights[0].shape[0]
    tile = min(512, tokens)
    cols = min(512, depth)
    return kernel_call(
        functools.partial(ffn_post_kernel, chunks, start, lhs_count),
        [*[a for group in acts for a in group], *weights],
        after,
        grid=(depth // cols, tokens // tile),
        in_specs=[pl.BlockSpec((tile, width), lambda d, i: (i, 0))] * (lhs_count * chunks)
        + [pl.BlockSpec((cols, 3 * width), lambda d, i: (d, 0))] * chunks,
        out_specs=pl.BlockSpec((tile, cols), lambda d, i: (i, d)),
        out_shape=jax.ShapeDtypeStruct((tokens, depth), BF16),
        cost=pl.CostEstimate(
            flops=2 * lhs_count * tokens * depth * width * chunks,
            bytes_accessed=(6 * depth * width + 2 * lhs_count * tokens * width) * chunks
            + 2 * tokens * depth,
            transcendentals=0,
        ),
        name=name,
    )


def lower_lanes(like):
    return lax.broadcasted_iota(jnp.int32, like.shape, 1) < HD


def half_ones():
    r = lax.broadcasted_iota(jnp.int32, (2 * HD, 2 * HD), 0) // HD
    c = lax.broadcasted_iota(jnp.int32, (2 * HD, 2 * HD), 1) // HD
    return (r == c).astype(F32).astype(BF16)


def swap(v):
    return pltpu.roll(v, HD, 1)


def features(x, feat):
    logit = dot(x, feat)
    low = lower_lanes(logit)
    top = jnp.max(jnp.where(low, logit, -jnp.inf), axis=1, keepdims=True)
    bottom = jnp.max(jnp.where(low, -jnp.inf, logit), axis=1, keepdims=True)
    e = jnp.exp(logit - jnp.where(low, top, bottom))
    return e / dot(e.astype(BF16), half_ones())


def features_back(phi, grad):
    p = phi.astype(F32)
    prod = p * grad
    low = lower_lanes(prod)
    first = jnp.sum(jnp.where(low, prod, 0.0), axis=1, keepdims=True)
    second = jnp.sum(jnp.where(low, 0.0, prod), axis=1, keepdims=True)
    g = prod - p * jnp.where(low, first, second)
    return (g - swap(g)).astype(BF16)[:, :HD]


def values_ones(kv):
    kv = kv.astype(F32)
    return jnp.where(lower_lanes(kv), swap(kv), 1.0).astype(BF16)


def key_state_kernel(ends_ref, kv_ref, feat_ref, kdoc_ref, phi_ref, state_ref):
    r = pl.program_id(0)
    kv = kv_ref[0, 0]
    body = kv.shape[0] - WIN
    phi = features(kv[:, :HD], feat_ref[0]).astype(BF16)
    phi_ref[0, 0] = phi
    last = ends_ref[r, body // WIN]
    held = jnp.where(kdoc_ref[0, :body] == last, phi[:body].astype(F32), 0.0).astype(BF16)
    state_ref[0, 0] = dot(held, values_ones(kv[:body]), TN).astype(BF16)


def key_state(ends, kv, feat, kdoc, after=()):
    slots, groups, ext, _ = kv.shape
    block = lambda r, g, *_: (r, g, 0, 0)
    return kernel_call(
        key_state_kernel,
        [ends, kv, feat, kdoc],
        after,
        prefetch=1,
        grid=(slots, groups),
        in_specs=[
            pl.BlockSpec((1, 1, ext, 2 * HD), block),
            pl.BlockSpec((1, HD, 2 * HD), lambda r, g, *_: (g, 0, 0)),
            pl.BlockSpec((1, ext, 2 * HD), lambda r, g, *_: (r, 0, 0)),
        ],
        out_specs=[
            pl.BlockSpec((1, 1, ext, 2 * HD), block),
            pl.BlockSpec((1, 1, 2 * HD, 2 * HD), block),
        ],
        out_shape=[
            jax.ShapeDtypeStruct((slots, groups, ext, 2 * HD), BF16),
            jax.ShapeDtypeStruct((slots, groups, 2 * HD, 2 * HD), BF16),
        ],
        name="key_state",
    )


def block_masks(b, qdoc_ref, pdoc_ref):
    rows = slice(WIN * b, WIN * b + WIN)
    same = qdoc_ref[0, rows] == pdoc_ref[0, b : b + 1]
    row = lax.broadcasted_iota(jnp.int32, (WIN, 2 * WIN), 0)
    col = lax.broadcasted_iota(jnp.int32, (WIN, 2 * WIN), 1)
    linear = same & (col <= row)
    window = same & (col > row) & (col <= row + WIN)
    return window, linear


def next_state(b, ends_ref, r, state, phi_ref, vx_ref, kdoc_ref):
    rows = slice(WIN * (b - 1), WIN * b)
    keep = (ends_ref[r, b] == ends_ref[r, b - 1]).astype(F32)
    held = jnp.where(
        kdoc_ref[0, rows] == ends_ref[r, b], phi_ref[0, 0, rows].astype(F32), 0.0
    ).astype(BF16)
    return state * keep + dot(held, vx_ref[rows], TN)


def block_forward(b, ends_ref, r, q_ref, kv_ref, phi_ref, phiq_ref, vx_ref, state_low, qdoc_ref, pdoc_ref):
    heads = q_ref.shape[1]
    rows, pair = slice(WIN * b, WIN * b + WIN), slice(WIN * b, WIN * b + 2 * WIN)
    window, linear = block_masks(b, qdoc_ref, pdoc_ref)
    valid = qdoc_ref[0, rows] == ends_ref[r, b]
    query = jnp.concatenate([q_ref[0, h, rows] for h in range(heads)], axis=0)
    phi_query = jnp.concatenate([phiq_ref[0, h, rows] for h in range(heads)], axis=0)
    key = kv_ref[0, 0, pair, :HD]
    phi_key = phi_ref[0, 0, pair]
    score = dot(query, key, NT) * (HD**-0.5)
    lin = dot(phi_query, phi_key, NT)
    part = lambda v, h: v[WIN * h : WIN * h + WIN]
    exps = [jnp.where(window, jnp.exp(part(score, h)), 0.0) for h in range(heads)]
    weight = jnp.concatenate(
        [jnp.where(linear, part(lin, h), exps[h]).astype(BF16) for h in range(heads)], axis=0
    )
    phi_valid = jnp.concatenate(
        [jnp.where(valid, part(phi_query, h).astype(F32), 0.0).astype(BF16) for h in range(heads)],
        axis=0,
    )
    both = dot(weight, vx_ref[pair]) + dot(phi_valid, state_low)
    denominator = jnp.where(lower_lanes(both), swap(both), both)
    return (query, phi_query, phi_valid, key, phi_key, exps, weight, both / denominator, denominator,
            window, linear, valid)


def attend_kernel(
    ends_ref, q_ref, kv_ref, phi_ref, feat_ref, carry_ref, qdoc_ref, kdoc_ref, pdoc_ref,
    attn_ref, phiq_ref, vx_ref,
):
    r = pl.program_id(0)
    heads, length = q_ref.shape[1], q_ref.shape[2]
    vx_ref[...] = values_ones(kv_ref[0, 0])
    for h in range(heads):
        phiq_ref[0, h] = features(q_ref[0, h], feat_ref[h]).astype(BF16)
    state = carry_ref[0, 0]
    for b in range(length // WIN):
        if b:
            state = next_state(b, ends_ref, r, state, phi_ref, vx_ref, kdoc_ref)
        out = block_forward(
            b, ends_ref, r, q_ref, kv_ref, phi_ref, phiq_ref, vx_ref, state.astype(BF16), qdoc_ref,
            pdoc_ref,
        )
        attn = out[7]
        low = lower_lanes(attn[:WIN])
        for h in range(0, heads, 2):
            first, second = attn[WIN * h : WIN * h + WIN], attn[WIN * h + WIN : WIN * h + 2 * WIN]
            attn_ref[0, WIN * b : WIN * b + WIN, HD * h : HD * h + 2 * HD] = jnp.where(
                low, first, swap(second)
            ).astype(BF16)


def attention_specs(slots, groups, heads, length):
    ext = length + WIN
    four = lambda r, g, *_: (r, g, 0, 0)
    docs = lambda r, g, *_: (r, 0, 0)
    return dict(
        q=pl.BlockSpec((1, heads, length, HD), four),
        kv=pl.BlockSpec((1, 1, ext, 2 * HD), four),
        phiq=pl.BlockSpec((1, heads, length, 2 * HD), four),
        feat=pl.BlockSpec((heads, HD, 2 * HD), lambda r, g, *_: (g, 0, 0)),
        state=pl.BlockSpec((1, 1, 2 * HD, 2 * HD), four),
        qdoc=pl.BlockSpec((1, length, 2 * HD), docs),
        kdoc=pl.BlockSpec((1, ext, 2 * HD), docs),
        pdoc=pl.BlockSpec((1, length // WIN, 2 * HD), docs),
        tokens=pl.BlockSpec((1, length, heads * HD), lambda r, g, *_: (r, 0, g)),
        fgrad=pl.BlockSpec((1, heads // 2, HD, 2 * HD), four),
    )


def attend(ends, q, kv, phi, feat, carry, qdoc, kdoc, pdoc, after=()):
    slots, all_heads, length, _ = q.shape
    groups = kv.shape[1]
    heads = all_heads // groups
    sp = attention_specs(slots, groups, heads, length)
    return kernel_call(
        attend_kernel,
        [ends, q, kv, phi, feat, carry, qdoc, kdoc, pdoc],
        after,
        prefetch=1,
        grid=(slots, groups),
        in_specs=[sp[n] for n in ("q", "kv", "kv", "feat", "state", "qdoc", "kdoc", "pdoc")],
        out_specs=[sp["tokens"], sp["phiq"]],
        scratch=[pltpu.VMEM((length + WIN, 2 * HD), BF16)],
        out_shape=[
            jax.ShapeDtypeStruct((slots, length, all_heads * HD), BF16),
            jax.ShapeDtypeStruct((slots, all_heads, length, 2 * HD), BF16),
        ],
        name="attend",
    )


def attend_back_kernel(
    ends_ref, q_ref, kv_ref, phi_ref, phiq_ref, feat_ref, carry_ref, qdoc_ref, kdoc_ref, pdoc_ref,
    g_ref, gq_ref, gfeat_ref, gphi_ref, gkv_ref, gcarry_ref, vx_ref, gstate_ref, gphiq_ref, gk_ref,
    gv_ref,
):
    r = pl.program_id(0)
    heads, length = q_ref.shape[1], q_ref.shape[2]
    blocks = length // WIN
    vx_ref[...] = values_ones(kv_ref[0, 0])
    gphi_ref[...] = jnp.zeros_like(gphi_ref)
    gk_ref[...] = jnp.zeros_like(gk_ref)
    gv_ref[...] = jnp.zeros_like(gv_ref)
    scale = HD**-0.5
    state = carry_ref[0, 0]
    for b in range(blocks):
        rows, pair = slice(WIN * b, WIN * b + WIN), slice(WIN * b, WIN * b + 2 * WIN)
        if b:
            state = next_state(b, ends_ref, r, state, phi_ref, vx_ref, kdoc_ref)
        state_low = state.astype(BF16)
        (query, phi_query, phi_valid, key, phi_key, exps, weight, attn, denominator, window, linear,
         valid) = block_forward(
            b, ends_ref, r, q_ref, kv_ref, phi_ref, phiq_ref, vx_ref, state_low, qdoc_ref, pdoc_ref
        )
        grads = []
        for h in range(0, heads, 2):
            g = g_ref[0, rows, HD * h : HD * h + 2 * HD].astype(F32)
            grads += [g, swap(g)]
        grad = jnp.concatenate(grads, axis=0)
        low = lower_lanes(grad)
        grad = jnp.where(low, grad, 0.0)
        g_denom = -jnp.sum(grad * attn, axis=1, keepdims=True)
        gx = (jnp.where(low, grad, g_denom * (1.0 / HD)) / denominator).astype(BF16)
        g_weight = dot(gx, vx_ref[pair], NT)
        part = lambda v, h: v[WIN * h : WIN * h + WIN]
        g_score = jnp.concatenate(
            [(exps[h] * part(g_weight, h)).astype(BF16) for h in range(heads)], axis=0
        )
        g_lin = jnp.concatenate(
            [jnp.where(linear, part(g_weight, h), 0.0).astype(BF16) for h in range(heads)], axis=0
        )
        g_query = dot(g_score, key) * scale
        gk_ref[pair] += dot(g_score, query, TN) * scale
        gv_ref[pair] += dot(weight, gx, TN)
        gphi_ref[0, 0, pair] += dot(g_lin, phi_query, TN)
        from_lin = dot(g_lin, phi_key)
        from_state = dot(gx, state_low, NT)
        gstate_ref[b] = dot(phi_valid, gx, TN)
        for h in range(heads):
            g_phi = part(from_lin, h) + jnp.where(valid, part(from_state, h), 0.0)
            g_logit = features_back(part(phi_query, h), g_phi)
            gphiq_ref[h, rows] = g_logit
        pieces = []
        for h in range(heads):
            g_logit = gphiq_ref[h, rows]
            pieces.append(part(g_query, h) + dot(g_logit, feat_ref[h][:, :HD], NT))
        gq_ref[0, rows] = jnp.concatenate(pieces, axis=1).astype(BF16)
    for h in range(0, heads, 2):
        gfeat_ref[0, h // 2] = jnp.concatenate(
            [dot(q_ref[0, i], gphiq_ref[i], TN) for i in (h, h + 1)], axis=1
        )
    later = gstate_ref[blocks - 1]
    for b in range(blocks - 1, 0, -1):
        rows = slice(WIN * (b - 1), WIN * b)
        low_state = later.astype(BF16)
        mask = kdoc_ref[0, rows] == ends_ref[r, b]
        gphi_ref[0, 0, rows] += jnp.where(mask, dot(vx_ref[rows], low_state, NT), 0.0)
        gv_ref[rows] += jnp.where(mask, dot(phi_ref[0, 0, rows], low_state), 0.0)
        keep = (ends_ref[r, b] == ends_ref[r, b - 1]).astype(F32)
        later = gstate_ref[b - 1] + keep * later
    gcarry_ref[0, 0] = later.astype(BF16)
    gv = gv_ref[...]
    gkv_ref[0, 0, :, :HD] = gk_ref[...]
    gkv_ref[0, 0, :, HD:] = gv[:, :HD]


def attend_back(ends, q, kv, phi, phiq, feat, carry, qdoc, kdoc, pdoc, g, after=()):
    slots, all_heads, length, _ = q.shape
    groups = kv.shape[1]
    heads = all_heads // groups
    ext = length + WIN
    sp = attention_specs(slots, groups, heads, length)
    return kernel_call(
        attend_back_kernel,
        [ends, q, kv, phi, phiq, feat, carry, qdoc, kdoc, pdoc, g],
        after,
        prefetch=1,
        grid=(slots, groups),
        in_specs=[
            sp[n]
            for n in ("q", "kv", "kv", "phiq", "feat", "state", "qdoc", "kdoc", "pdoc", "tokens")
        ],
        out_specs=[sp["tokens"], sp["fgrad"], sp["kv"], sp["kv"], sp["state"]],
        scratch=[
            pltpu.VMEM((ext, 2 * HD), BF16),
            pltpu.VMEM((length // WIN, 2 * HD, 2 * HD), F32),
            pltpu.VMEM((heads, length, HD), BF16),
            pltpu.VMEM((ext, HD), F32),
            pltpu.VMEM((ext, 2 * HD), F32),
        ],
        out_shape=[
            jax.ShapeDtypeStruct((slots, length, all_heads * HD), BF16),
            jax.ShapeDtypeStruct((slots, all_heads // 2, HD, 2 * HD), F32),
            jax.ShapeDtypeStruct((slots, groups, ext, 2 * HD), F32),
            jax.ShapeDtypeStruct((slots, groups, ext, 2 * HD), F32),
            jax.ShapeDtypeStruct((slots, groups, 2 * HD, 2 * HD), BF16),
        ],
        name="attend_back",
    )


def key_back_kernel(
    ends_ref, kv_ref, phi_ref, feat_ref, later_ref, kdoc_ref, gphi_ref, gkv_ref,
    gk_ref, gv_ref, gfeat_ref,
):
    r = pl.program_id(0)
    ext = kv_ref.shape[2]
    body = ext - WIN
    last = ends_ref[r, body // WIN]
    mask = kdoc_ref[0, :body] == last
    keys, vals, feats = [], [], []
    for i in range(2):
        kv, phi = kv_ref[0, i], phi_ref[0, i]
        later = later_ref[0, i].astype(BF16)
        more_phi = jnp.where(mask, dot(values_ones(kv[:body]), later, NT), 0.0)
        more_v = jnp.where(mask, dot(phi[:body], later), 0.0)
        tail = jnp.zeros((WIN, 2 * HD), F32)
        g_phi = gphi_ref[0, i] + jnp.concatenate([more_phi, tail], axis=0)
        g_logit = features_back(phi, g_phi)
        gkv = gkv_ref[0, i]
        keys.append(gkv[:, :HD] + dot(g_logit, feat_ref[i][:, :HD], NT))
        vals.append(gkv[:, HD:] + jnp.concatenate([more_v, tail], axis=0)[:, :HD])
        feats.append(dot(kv[:, :HD], g_logit, TN))
    gfeat_ref[0, 0] = jnp.concatenate(feats, axis=1)
    gk_ref[0] = jnp.concatenate(keys, axis=1)
    gv_ref[0] = jnp.concatenate(vals, axis=1)


def key_back(ends, kv, phi, feat, later, kdoc, gphi, gkv, after=()):
    slots, groups, ext, _ = kv.shape
    four = lambda r, s, *_: (r, s, 0, 0)
    wide = pl.BlockSpec((1, 2, ext, 2 * HD), four)
    out = pl.BlockSpec((1, ext, 2 * HD), lambda r, s, *_: (r, 0, s))
    flat = jax.ShapeDtypeStruct((slots, ext, groups * HD), F32)
    return kernel_call(
        key_back_kernel,
        [ends, kv, phi, feat, later, kdoc, gphi, gkv],
        after,
        prefetch=1,
        grid=(slots, groups // 2),
        in_specs=[
            wide,
            wide,
            pl.BlockSpec((2, HD, 2 * HD), lambda r, s, *_: (s, 0, 0)),
            pl.BlockSpec((1, 2, 2 * HD, 2 * HD), four),
            pl.BlockSpec((1, ext, 2 * HD), lambda r, s, *_: (r, 0, 0)),
            wide,
            wide,
        ],
        out_specs=[out, out, pl.BlockSpec((1, 1, HD, 2 * HD), four)],
        out_shape=[flat, flat, jax.ShapeDtypeStruct((slots, groups // 2, HD, 2 * HD), F32)],
        name="key_back",
    )


def project_kernel(sets, q_cols, k_cols, x_ref, w_ref, a_ref, b_ref, q_ref, kv_ref, small_ref):
    x = x_ref[0]
    width = q_cols + 2 * k_cols
    small = dot(x, a_ref[...]).astype(BF16)
    small_ref[0] = small
    heads, groups = q_cols // HD, k_cols // HD
    for s in range(sets):
        cols = slice(s * width, (s + 1) * width)
        full = dot(x, w_ref[s]) + ADAPTER_SCALE * dot(small, b_ref[:, cols])
        for h in range(heads):
            q_ref[0, s * heads + h] = full[:, h * HD : h * HD + HD].astype(BF16)
        for g in range(0, groups, 2):
            k = full[:, q_cols + g * HD : q_cols + g * HD + 2 * HD]
            start = q_cols + k_cols + g * HD
            v = full[:, start : start + 2 * HD]
            low = lower_lanes(k)
            kv_ref[0, s * groups + g] = jnp.where(low, k, swap(v)).astype(BF16)
            kv_ref[0, s * groups + g + 1] = jnp.where(low, swap(k), v).astype(BF16)


def project(x, w, a, b, q_cols, k_cols, after=()):
    slots, length, depth = x.shape
    sets = w.shape[0]
    heads, groups = sets * q_cols // HD, sets * k_cols // HD
    tile = min(256, length)
    ranks = a.shape[1]
    return kernel_call(
        functools.partial(project_kernel, sets, q_cols, k_cols),
        [x, w, a, b],
        after,
        grid=(slots, length // tile),
        in_specs=[
            pl.BlockSpec((1, tile, depth), lambda r, i: (r, i, 0)),
            pl.BlockSpec(w.shape, lambda r, i: (0, 0, 0)),
            pl.BlockSpec(a.shape, lambda r, i: (0, 0)),
            pl.BlockSpec(b.shape, lambda r, i: (0, 0)),
        ],
        out_specs=[
            pl.BlockSpec((1, heads, tile, HD), lambda r, i: (r, 0, i, 0)),
            pl.BlockSpec((1, groups, tile, 2 * HD), lambda r, i: (r, 0, i, 0)),
            pl.BlockSpec((1, tile, ranks), lambda r, i: (r, i, 0)),
        ],
        out_shape=[
            jax.ShapeDtypeStruct((slots, heads, length, HD), BF16),
            jax.ShapeDtypeStruct((slots, groups, length, 2 * HD), BF16),
            jax.ShapeDtypeStruct((slots, length, ranks), BF16),
        ],
        cost=pl.CostEstimate(
            flops=2 * slots * length * w.size,
            bytes_accessed=2 * (slots * length * depth + w.size),
            transcendentals=0,
        ),
        name="project",
    )


def local(
    hidden_in,
    grad_out,
    live_rows,
    doc_starts,
    norm_attn,
    norm_ffn,
    query_weight,
    key_weight,
    value_weight,
    out_weight,
    gate_weight,
    up_weight,
    down_weight,
    query_adapt_in,
    query_adapt_out,
    key_adapt_in,
    key_adapt_out,
    value_adapt_in,
    value_adapt_out,
    outproj_adapt_in,
    projection_adapter_second,
    query_feature,
    key_feature,
):
    rows, seqs, heads = lax.axis_size("row"), lax.axis_size("seq"), lax.axis_size("head")
    head = lax.axis_index("head")
    core = lax.rem(head, 2)
    x_count = heads // 2
    x_place = head // 2
    slots, share_len, model_dim = hidden_in.shape
    piece_len = 2 * share_len
    pieces = seqs * x_count
    piece = lax.axis_index("seq") * x_count + x_place
    blocks = piece_len // WIN
    ext_len = piece_len + WIN
    q_cols, k_cols = query_weight.shape[1], key_weight.shape[1]
    ff_cols = gate_weight.shape[1]

    def in_order(own, other):
        first = jnp.where(core == 0, own, other)
        second = jnp.where(core == 0, other, own)
        return jnp.concatenate([first, second], axis=1)

    def own_half(both):
        return lax.dynamic_slice_in_dim(both, core * share_len, share_len, 1)

    def other_half(both):
        return lax.dynamic_slice_in_dim(both, (1 - core) * share_len, share_len, 1)

    qkv_shard = jnp.concatenate([query_weight, key_weight, value_weight], axis=1)
    out_shard = out_weight.T
    down_shard = down_weight.T
    chunk = ff_cols // FF_CHUNKS
    ffn_shards = [
        jnp.concatenate(
            [w[:, j * chunk : (j + 1) * chunk] for w in (gate_weight, up_weight, down_shard)], axis=1
        )
        for j in range(FF_CHUNKS)
    ]
    ffn_later = [
        lax.all_gather(v, ("row", "seq"), axis=0, tiled=True) for v in ffn_shards[1:]
    ]
    half_chunk = ffn_shards[0].shape[1] // 2
    own_smalls = [
        query_feature, key_feature, query_adapt_out, key_adapt_out, value_adapt_out, outproj_adapt_in
    ]
    (qkv_mat, out_mat, first_mat), other_smalls, (hidden_other, cot_mine, cot_away) = gather(
        [qkv_shard, out_shard, ffn_shards[0]],
        [True, True, False],
        [
            (0, (0, qkv_shard.shape[1]), True, 0),
            (1, (0, out_shard.shape[1]), True, 0),
            (2, (0, half_chunk), True, rows * seqs),
            (2, (half_chunk, half_chunk), False, rows * seqs),
        ],
        own_smalls,
        hidden_in,
        grad_out,
    )
    ffn_mats = [first_mat] + ffn_later

    def both(i, axis):
        own, other = own_smalls[i], other_smalls[i]
        return jnp.concatenate(
            [jnp.where(x_place == 0, own, other), jnp.where(x_place == 0, other, own)], axis=axis
        )

    query_feat_all, key_feat_all = both(0, 0), both(1, 0)
    q_out, k_out, v_out = both(2, 1), both(3, 1), both(4, 1)
    o_in = both(5, 0)

    doc_ids = jnp.cumsum(doc_starts, axis=1)
    padded_docs = jnp.concatenate(
        [jnp.full((slots, WIN + 1), -1, jnp.int32), doc_ids], axis=1
    )
    piece_docs = padded_docs[:, ::piece_len][:, : pieces + 1]
    near_docs = lax.dynamic_slice_in_dim(padded_docs, piece * piece_len, ext_len + 1, 1)
    end_docs = near_docs[:, ::WIN][:, : blocks + 1]
    carry_doc = end_docs[:, 0]
    next_doc = end_docs[:, blocks]
    key_docs = near_docs[:, 1:]
    key_doc_lanes = jnp.broadcast_to(key_docs[:, :, None], (slots, ext_len, 2 * HD))
    query_doc_lanes = key_doc_lanes[:, WIN:]
    doc_blocks = key_docs.reshape(slots, blocks + 1, WIN)
    pair_docs = jnp.concatenate([doc_blocks[:, :-1], doc_blocks[:, 1:]], axis=2)

    def from_pieces(block):
        held = []
        for d, start in enumerate((block, flip_x(block))):
            for l in range(seqs):
                if l:
                    start = shift(start, "seq", 1)
                source = (
                    lax.rem(lax.axis_index("seq") - l + seqs, seqs) * x_count
                    + lax.rem(x_place + d, x_count)
                )
                held.append((source, start))
        return held[1:]

    gain_attn = norm_attn.astype(F32)
    gain_ffn = norm_ffn.astype(F32)
    slot_live = (jnp.arange(slots) < live_rows[0])[:, None, None]
    grad_low = jnp.where(slot_live, grad_out, jnp.zeros_like(grad_out))
    grad_share = grad_low.astype(F32)
    rows_float = hidden_in.astype(F32)
    normed_share = rms_scaled(rows_float, gain_attn).astype(BF16)
    normed_other = rms_scaled(tie(hidden_other, qkv_mat).astype(F32), gain_attn).astype(BF16)
    normed = in_order(normed_share, normed_other)

    flat = normed.reshape(slots * piece_len, model_dim)
    set_cols = q_cols + 2 * k_cols
    adapt_in_all = jnp.concatenate([query_adapt_in, key_adapt_in, value_adapt_in], axis=1)

    def by_sets(parts):
        return jnp.concatenate(
            [v[:, d * (v.shape[1] // 2) : (d + 1) * (v.shape[1] // 2)] for d in range(2) for v in parts],
            axis=1,
        )

    def diagonal(parts):
        rows = [
            [p if i == j else jnp.zeros((RANK, q.shape[1]), BF16) for j, q in enumerate(parts)]
            for i, p in enumerate(parts)
        ]
        return jnp.concatenate([by_sets(r) for r in rows], axis=0)

    adapt_out_all = diagonal([q_out, k_out, v_out])
    query, kv_own, small = project(
        normed, qkv_mat, adapt_in_all, adapt_out_all, q_cols, k_cols
    )

    def along_pieces(block, distance):
        route = []
        for p in range(pieces):
            to = p + distance
            if 0 <= to < pieces:
                for c in range(2):
                    route.append((2 * p + c, 2 * to + c))
        return lax.ppermute(block, ("seq", "head"), route)

    kv = jnp.concatenate([along_pieces(kv_own[:, :, -WIN:], 1), kv_own], axis=2)
    doubled = lambda feat: jnp.concatenate([feat, -feat], axis=2)
    query_feat, key_feat = doubled(query_feat_all), doubled(key_feat_all)
    phi_key, end_state = key_state(end_docs, kv, key_feat, key_doc_lanes)
    carry = jnp.zeros(end_state.shape, F32)
    for source, part in from_pieces(end_state):
        after = lax.dynamic_index_in_dim(piece_docs, source + 1, 1, keepdims=False)
        keep = (source < piece) & (after == carry_doc)
        carry = carry + jnp.where(keep[:, None, None, None], part.astype(F32), 0.0)
    attn, phi_query = attend(
        end_docs, query, kv, phi_key, query_feat, carry, query_doc_lanes, key_doc_lanes, pair_docs
    )
    attn = attn.reshape(slots * piece_len, -1)

    half_q = q_cols
    proj_part = dot(attn[:, :half_q], out_mat[0], NT) + dot(attn[:, half_q:], out_mat[1], NT)
    proj_part = proj_part.reshape(slots, piece_len, model_dim)
    low_part = dot(attn, o_in).reshape(slots, piece_len, RANK)
    proj_sum = own_half(proj_part) + flip_core(other_half(proj_part).astype(BF16)).astype(F32)
    low_mix = (own_half(low_part) + flip_core(other_half(low_part))).astype(BF16)
    mid_rows = (
        rows_float
        + proj_sum
        + ADAPTER_SCALE
        * dot(low_mix.reshape(-1, RANK), projection_adapter_second).reshape(rows_float.shape)
    )

    nmid = rms_scaled(mid_rows, gain_ffn).astype(BF16)
    nmid_x = flip_x(nmid)

    def chip_tokens(own):
        return own.reshape(-1, model_dim), flip_core(own).reshape(-1, model_dim)

    def sum_away(away):
        away = away.reshape(2, slots, share_len, model_dim)
        return (away[0].astype(F32) + flip_core(away[1]).astype(F32)).astype(BF16)

    def sum_mine(mine, back):
        mine = mine.reshape(2, slots, share_len, model_dim)
        return mine[0].astype(F32) + flip_core(mine[1]).astype(F32) + back.astype(F32)

    flat_tokens = lambda v: v.reshape(-1, model_dim)
    x_mine = chip_tokens(nmid)
    c_mine, c_away = flat_tokens(cot_mine), flat_tokens(cot_away)
    pre = lambda x, c, w, after: ffn_pre(x, c, w, live_rows, share_len, slots, after)
    acts_mine, acts_away, after = [], [], ()
    for w in ffn_mats[:-1]:
        acts_mine.append(pre(x_mine, c_mine, w, after))
        after = (acts_mine[-1][0],)
    x_away = chip_tokens(hold(nmid_x, (acts_mine[1][0],)))
    for w in ffn_mats:
        acts_away.append(pre(x_away, c_away, w, after))
        after = (acts_away[-1][0],)
    gn_away = ffn_post([v[1:] for v in acts_away], ffn_mats, 0, "ffn_gn")
    gn_there = sum_away(gn_away)
    gn_back = flip_x(gn_there)
    acts_mine.append(pre(x_mine, c_mine, ffn_mats[-1], (gn_there,)))
    gn_mine = ffn_post([v[1:] for v in acts_mine], ffn_mats, 0, "ffn_gn")
    y_away = ffn_post([v[:1] for v in acts_away], ffn_mats, 2, "ffn_y", (gn_mine,))
    y_there = sum_away(y_away)
    y_back = flip_x(y_there)
    grad_nmid = sum_mine(gn_mine, gn_back)
    grad_mid = grad_share + rms_back(mid_rows, gain_ffn, grad_nmid)

    branch_share = grad_mid.astype(BF16)
    branch = in_order(branch_share, flip_core(branch_share)).reshape(-1, model_dim)
    grad_low_mix = (
        ADAPTER_SCALE * dot(branch, projection_adapter_second, ((1,), (1,)))
    ).astype(BF16)
    sum_o_in = dot(grad_low_mix, attn, TN)
    sum_o_out = ADAPTER_SCALE * dot(
        low_mix.reshape(-1, RANK), branch_share.reshape(-1, model_dim), ((0,), (0,))
    )
    branch_out = jnp.concatenate([dot(branch, out_mat[0]), dot(branch, out_mat[1])], axis=1)
    grad_attn = (branch_out + dot(grad_low_mix, o_in, NT)).astype(BF16)

    grad_query, feat_query, gphi, gkv, grad_carry = attend_back(
        end_docs, query, kv, phi_key, phi_query, query_feat, carry, query_doc_lanes, key_doc_lanes,
        pair_docs, grad_attn.reshape(slots, piece_len, -1), (y_there,),
    )
    y_mine = ffn_post([v[:1] for v in acts_mine], ffn_mats, 2, "ffn_y", (grad_carry,))
    block_out = (mid_rows + sum_mine(y_mine, y_back)).astype(BF16)
    later = jnp.zeros(grad_carry.shape, F32)
    for source, part in from_pieces(grad_carry):
        start = lax.dynamic_index_in_dim(piece_docs, source, 1, keepdims=False)
        keep = (source > piece) & (start == next_doc)
        later = later + jnp.where(keep[:, None, None, None], part.astype(F32), 0.0)
    grad_key_ext, grad_value_ext, feat_key = key_back(
        end_docs, kv, phi_key, key_feat, later, key_doc_lanes, gphi, gkv, (y_mine,)
    )
    sum_q_feat = jnp.sum(feat_query, axis=0).reshape(2, -1, 2 * HD)
    sum_k_feat = jnp.sum(feat_key, axis=0).reshape(2, -1, 2 * HD)
    tail_pad = ((0, 0), (piece_len - WIN, 0), (0, 0))

    def fold_back(ext):
        back = along_pieces(ext[:, :WIN].astype(BF16), -1).astype(F32)
        return (ext[:, WIN:] + jnp.pad(back, tail_pad)).astype(BF16)

    grad_key_low = fold_back(grad_key_ext).reshape(slots * piece_len, -1)
    grad_value_low = fold_back(grad_value_ext).reshape(slots * piece_len, -1)
    grad_query_low = grad_query.reshape(slots * piece_len, -1)

    nt = ((1,), (1,))
    stacked = by_sets([grad_query_low, grad_key_low, grad_value_low])
    grad_normed_part = dot(stacked[:, :set_cols], qkv_mat[0], nt) + dot(
        stacked[:, set_cols:], qkv_mat[1], nt
    )
    small_part = ADAPTER_SCALE * dot(stacked, adapt_out_all, nt)
    small = small.reshape(slots * piece_len, 3 * RANK)
    outs = [
        ADAPTER_SCALE * dot(small[:, i * RANK : (i + 1) * RANK], g, ((0,), (0,)))
        for i, g in enumerate((grad_query_low, grad_key_low, grad_value_low))
    ]
    grad_normed_part = grad_normed_part.reshape(slots, piece_len, model_dim)
    small_part = small_part.reshape(slots, piece_len, 3 * RANK)
    grad_normed = own_half(grad_normed_part) + flip_core(
        other_half(grad_normed_part).astype(BF16)
    ).astype(F32)
    small_low = (own_half(small_part) + flip_core(other_half(small_part))).astype(BF16)
    small_low = small_low.reshape(-1, 3 * RANK)
    grad_normed = grad_normed + dot(small_low, adapt_in_all, nt).reshape(rows_float.shape)
    sum_in = dot(small_low, normed_share.reshape(-1, model_dim), ((0,), (0,)))
    grad_hidden = (grad_mid + rms_back(rows_float, gain_attn, grad_normed)).astype(BF16)

    by_rows = jnp.concatenate([sum_in, sum_o_out], axis=0)
    width = model_dim // (rows * seqs * heads)
    by_rows = by_rows.reshape(4 * RANK, rows, seqs, heads, width).transpose(3, 2, 1, 0, 4)
    for axis in ("head", "seq", "row"):
        by_rows = scatter_sum(by_rows, axis)
    in_parts = by_rows.reshape(4, RANK, width)

    def lanes_of(v):
        v = v.reshape(RANK, 2, -1, 2 * HD).transpose(1, 2, 0, 3)
        return v.reshape(2, -1, 2 * HD)

    packed = [lanes_of(v) for v in outs + [sum_o_in]] + [sum_q_feat, sum_k_feat]
    sizes = [v.shape[1] for v in packed]
    packed = jnp.concatenate(packed, axis=1)
    kept = lax.dynamic_index_in_dim(packed, x_place, 0, keepdims=False)
    sent = lax.dynamic_index_in_dim(packed, 1 - x_place, 0, keepdims=False)
    packed = kept + flip_x(sent.astype(BF16)).astype(F32)
    for axis in ("seq", "row"):
        packed = full_sum(packed, axis)
    cols, at = [], 0
    for size in sizes:
        cols.append(packed[at : at + size])
        at += size
    from_lanes = lambda v: v.reshape(-1, RANK, 2 * HD).transpose(1, 0, 2).reshape(RANK, -1)
    from_pairs = lambda v: v.reshape(-1, HD, 2, HD).transpose(0, 2, 1, 3).reshape(-1, HD, HD)
    cols = [from_lanes(v) for v in cols[:4]] + [from_pairs(v) for v in cols[4:]]
    cols[3] = cols[3].T

    return (
        block_out,
        grad_hidden,
        in_parts[0].T,
        cols[0],
        in_parts[1].T,
        cols[1],
        in_parts[2].T,
        cols[2],
        cols[3],
        in_parts[3],
        cols[4],
        cols[5],
    )


def solution(mesh):
    return jax.shard_map(
        local,
        mesh=mesh,
        in_specs=(
            P("row", ("seq", "head"), None),
            P("row", ("seq", "head"), None),
            P("row"),
            P("row", None),
            P(),
            P(),
            P(("row", "seq"), "head"),
            P(("row", "seq"), "head"),
            P(("row", "seq"), "head"),
            P("head", ("row", "seq")),
            P(("row", "seq"), "head"),
            P(("row", "seq"), "head"),
            P("head", ("row", "seq")),
            P(),
            P(None, "head"),
            P(),
            P(None, "head"),
            P(),
            P(None, "head"),
            P("head", None),
            P(),
            P("head", None, None),
            P("head", None, None),
        ),
        out_specs=(
            P("row", ("seq", "head"), None),
            P("row", ("seq", "head"), None),
            P(("row", "seq", "head"), None),
            P(None, "head"),
            P(("row", "seq", "head"), None),
            P(None, "head"),
            P(("row", "seq", "head"), None),
            P(None, "head"),
            P("head", None),
            P(None, ("row", "seq", "head")),
            P("head", None, None),
            P("head", None, None),
        ),
        check_vma=False,
    )
```

time: 1540 us -> 850 us (0.55)
  Pallas kernels: 167 us -> 571 us
  local copies, waits for them, and re-layouts: 422 us -> 67.1 us
  waiting for transfers between devices: 381 us -> 65.2 us
  matrix products: 238 us -> 41.6 us
  other arithmetic: 187 us -> 52.7 us
  starting transfers between devices: 133 us -> 29.2 us
    pallas_call x10 -> x19, Pallas kernels: 167 us -> 571 us  [the longest x18 341 us: kernel_call(): pl.pallas_call(body, grid_spec=pltpu.PrefetchScalarGridSpec(num_scalar_pr...]
    dynamic_update_slice x60 -> x0, local copies, waits for them, and re-layouts: 185 us -> none  [assemble(): whole = lax.dynamic_update_slice(whole, block, (place * depth, column))]
    ppermute x53 -> x11, waiting for transfers between devices: 199 us -> 23.7 us  [shift(): lax.ppermute(block, axis, [(i, (i + distance) % size) for i in range(size)])]
    dot_general x24 -> x0, matrix products: 168 us -> none  [the longest x1 30.1 us: local(): jnp.einsum('rbe,rbegf->regf', state_mask, via_phi, precision=HIGHEST)]
    ppermute x34 -> x6, waiting for transfers between devices: 162 us -> 23.4 us  [flip_x(): lax.ppermute(block, 'head', [(i, i ^ 2) for i in range(lax.axis_size('hea...]
    convert_element_type x15 -> x2, local copies, waits for them, and re-layouts: 62.6 us -> 3.5 us  [the longest x1 2.56 us: local(): grad_attn = (branch_out + dot(grad_low_mix, o_in, NT)).astype(BF16)]
    ppermute x53 -> x11, starting transfers between devices: 55.9 us -> 12.3 us  [shift(): lax.ppermute(block, axis, [(i, (i + distance) % size) for i in range(size)])]
    sub x4 -> x0, other arithmetic: 40.7 us -> none  [the longest x2 27.7 us: hedgehog(): jax.nn.softmax(-values, axis=-1)]
  transfers between devices with their start and end apart: 123 -> 37, of which waited for: 43 -> 20; matrix products, arithmetic and copies ran while one was open for 45% -> 16% of each run, Pallas kernels for 5% -> 63%
where the time goes in v1:
time: 850 us; the launch traced here: 843 us
  Pallas kernels  571 us (67%)
  local copies, waits for them, and re-layouts  67.1 us (8%)
  waiting for transfers between devices  65.2 us (8%)
  other arithmetic  52.7 us (6%)
  matrix products  41.6 us (5%)
  starting transfers between devices  29.2 us (3%)
  between operations  16.2 us (2%)
    pallas_call x18, Pallas kernels, kernel_call(): pl.pallas_call(body, grid_spec=pltpu.PrefetchScalarGridSpec(num_scalar_pr...  341 us
    pallas_call x1, Pallas kernels, gather(): pl.pallas_call(functools.partial(gather_kernel, plan, rows, seqs, parts,...  230 us
    dot_general x18, matrix products, dot(): return lax.dot_general(a, b, (dims, ((), ())), preferred_element_type=F32)  41.6 us
    ppermute x11, waiting for transfers between devices, shift(): lax.ppermute(block, axis, [(i, (i + distance) % size) for i in range(size)])  23.7 us
    unnamed x171, local copies, waits for them, and re-layouts  23.7 us
    ppermute x6, waiting for transfers between devices, flip_x(): lax.ppermute(block, 'head', [(i, i ^ 2) for i in range(lax.axis_size('hea...  23.4 us
  transfers between devices with their start and end apart: 37, of which 20 were waited for; matrix products, arithmetic and copies ran while one was open for 16% of the time, Pallas kernels for 63%

profile of v1, /device:TPU:0, one launch (start us, length us, event | category | flops | bytes accessed | tf_op | source)
XLA Modules:
  0.0 843.2 jit_solution(8383926441283395598)
XLA Ops:
  16.9 229.9 %gather.1 = (bf16[2,2048,768]{2,1,0:T(8,128)(2,1)}, bf16[2,2048,512]{2,1,0:T(8,128)(2,1)}, bf16[2048,1536]{1,0:T(8,128)(2,1)}, bf16[8,64,64]{2,1,0:T(8,128)(2,1)...) custom-call(bf16[256,768]{1,0:T(8,128)(2,1)} %pad_maximum_fusion.6.r, ...), custom_call_target="tpu_custom_call" | custom-call | tf_op jit(solution)/shard_map/gather/pallas_call | solution.py:266
  256.8 15.2 %project.1 = (bf16[2,16,512,64]{3,2,1,0:T(8,128)(2,1)}, bf16[2,4,512,128]{3,2,1,0:T(8,128)(2,1)}, bf16[2,512,24]{2,1,0:T(8,128)(2,1)}) custom-call(bf16[2,512,2048]{2,1,0:T(8,128)(2,1)} %pad_maximum_fusion.refs_0_, bf16[2,2048,768]{2,1,0:T(8,128)(2,1)} %get-tuple-element.65.refs_1_, bf16[2048,24]{1,0:T(8,128)(2,1)} %copy.76.refs_2_, ...), custom_call_target="tpu_custom_call" | custom-call | flops 6442450944 | bytes 10485760 | tf_op jit(solution)/shard_map/project/pallas_call | solution.py:44
  272.9 4.9 collective-permute-start
  285.6 8.7 %key_state.1 = (bf16[2,4,576,128]{3,2,1,0:T(8,128)(2,1)}, bf16[2,4,128,128]{3,2,1,0:T(8,128)(2,1)}) custom-call(s32[2,9]{1,0:T(2,128)} %bitcast.259, bf16[2,4,576,128]{3,2,1,0:T(8,128)(2,1)} %copy-done.7, bf16[4,64,128]{2,1,0:T(8,128)(2,1)} %pad_maximum_fusion.10.refs_2_.refs_3_, s32[2,576,128]{2,1,0:T(8,128)} %broadcast_in_dim.81.refs_3_.refs_7_.refs_8_.refs_5_), custom_call_target="tpu_custom_call" | custom-call | tf_op jit(solution)/shard_map/key_state/pallas_call | solution.py:44
  304.8 5.6 collective-permute-done.3
  312.5 22.7 %attend.1 = (bf16[2,512,1024]{2,1,0:T(8,128)(2,1)}, bf16[2,16,512,128]{3,2,1,0:T(8,128)(2,1)}) custom-call(s32[2,9]{1,0:T(2,128)} %bitcast.260, bf16[2,16,512,64]{3,2,1,0:T(8,128)(2,1)} %get-tuple-element.70.refs_1_, bf16[2,4,576,128]{3,2,1,0:T(8,128)(2,1)} %copy-done.7, bf16[2,4,576,128]{3,2,1,0:T(8,128)(2,1)} %get-tuple-element.73.refs_3_.refs_2_, ...), custom_call_target="tpu_custom_call" | custom-call | tf_op jit(solution)/shard_map/attend/pallas_call | solution.py:44
  335.2 4.4 fusion.31
  363.1 12.4 %ffn_pre.8 = (bf16[1024,512]{1,0:T(8,128)(2,1)}, bf16[1024,512]{1,0:T(8,128)(2,1)}, bf16[1024,512]{1,0:T(8,128)(2,1)}) custom-call(s32[1]{0:T(128)} %copy.145.refs_0_, bf16[512,2048]{1,0:T(8,128)(2,1)} %bitcast.240, bf16[512,2048]{1,0:T(8,128)(2,1)} %bitcast.273, bf16[1024,2048]{1,0:T(8,128)(2,1)} %bitcast.265, ...), custom_call_target="tpu_custom_call" | custom-call | flops 6442450944 | bytes 17825792 | tf_op jit(solution)/shard_map/ffn_pre/pallas_call | solution.py:44
  375.5 12.3 %ffn_pre.9 = (bf16[1024,512]{1,0:T(8,128)(2,1)}, bf16[1024,512]{1,0:T(8,128)(2,1)}, bf16[1024,512]{1,0:T(8,128)(2,1)}) custom-call(s32[1]{0:T(128)} %copy.145.refs_0_, bf16[512,2048]{1,0:T(8,128)(2,1)} %bitcast.241, bf16[512,2048]{1,0:T(8,128)(2,1)} %bitcast.274, bf16[1024,2048]{1,0:T(8,128)(2,1)} %bitcast.266, ...), custom_call_target="tpu_custom_call" | custom-call | flops 6442450944 | bytes 17825792 | tf_op jit(solution)/shard_map/ffn_pre/pallas_call | solution.py:44
  387.8 17.9 %collective-permute-done.7 = bf16[2,256,2048]{2,1,0:T(8,128)(2,1)} collective-permute-done((bf16[2,256,2048]{2,1,0:T(8,128)(2,1)S(1)}, bf16[2,256,2048]{2,1,0:T(8,128)(2,1)}, u32[]{:S(2)}, u32[]{:S(2)}) %collective-permute-start.7) | collective-permute-done | bytes 2097184 | tf_op jit(solution)/shard_map/ppermute | solution.py:33
  408.4 12.2 %ffn_pre.10 = (bf16[1024,512]{1,0:T(8,128)(2,1)}, bf16[1024,512]{1,0:T(8,128)(2,1)}, bf16[1024,512]{1,0:T(8,128)(2,1)}) custom-call(s32[1]{0:T(128)} %copy.145.refs_0_, bf16[512,2048]{1,0:T(8,128)(2,1)} %bitcast.242, bf16[512,2048]{1,0:T(8,128)(2,1)} %bitcast.275, bf16[1024,2048]{1,0:T(8,128)(2,1)} %bitcast.267, ...), custom_call_target="tpu_custom_call" | custom-call | flops 6442450944 | bytes 17825792 | tf_op jit(solution)/shard_map/ffn_pre/pallas_call | solution.py:44
  422.0 12.2 %ffn_pre.11 = (bf16[1024,512]{1,0:T(8,128)(2,1)}, bf16[1024,512]{1,0:T(8,128)(2,1)}, bf16[1024,512]{1,0:T(8,128)(2,1)}) custom-call(s32[1]{0:T(128)} %copy.145.refs_0_, bf16[512,2048]{1,0:T(8,128)(2,1)} %hold.1.refs_1_, bf16[512,2048]{1,0:T(8,128)(2,1)} %bitcast.277, bf16[1024,2048]{1,0:T(8,128)(2,1)} %bitcast.269, ...), custom_call_target="tpu_custom_call" | custom-call | flops 6442450944 | bytes 17825792 | tf_op jit(solution)/shard_map/ffn_pre/pallas_call | solution.py:44
  434.2 12.3 %ffn_pre.12 = (bf16[1024,512]{1,0:T(8,128)(2,1)}, bf16[1024,512]{1,0:T(8,128)(2,1)}, bf16[1024,512]{1,0:T(8,128)(2,1)}) custom-call(s32[1]{0:T(128)} %copy.145.refs_0_, bf16[512,2048]{1,0:T(8,128)(2,1)} %hold.1.refs_1_, bf16[512,2048]{1,0:T(8,128)(2,1)} %bitcast.278, bf16[1024,2048]{1,0:T(8,128)(2,1)} %bitcast.270, ...), custom_call_target="tpu_custom_call" | custom-call | flops 6442450944 | bytes 17825792 | tf_op jit(solution)/shard_map/ffn_pre/pallas_call | solution.py:44
  446.4 12.2 %ffn_pre.13 = (bf16[1024,512]{1,0:T(8,128)(2,1)}, bf16[1024,512]{1,0:T(8,128)(2,1)}, bf16[1024,512]{1,0:T(8,128)(2,1)}) custom-call(s32[1]{0:T(128)} %copy.145.refs_0_, bf16[512,2048]{1,0:T(8,128)(2,1)} %hold.1.refs_1_, bf16[512,2048]{1,0:T(8,128)(2,1)} %bitcast.279, bf16[1024,2048]{1,0:T(8,128)(2,1)} %bitcast.271, ...), custom_call_target="tpu_custom_call" | custom-call | flops 6442450944 | bytes 17825792 | tf_op jit(solution)/shard_map/ffn_pre/pallas_call | solution.py:44
  458.7 12.3 %ffn_pre.14 = (bf16[1024,512]{1,0:T(8,128)(2,1)}, bf16[1024,512]{1,0:T(8,128)(2,1)}, bf16[1024,512]{1,0:T(8,128)(2,1)}) custom-call(s32[1]{0:T(128)} %copy.145.refs_0_, bf16[512,2048]{1,0:T(8,128)(2,1)} %hold.1.refs_1_, bf16[512,2048]{1,0:T(8,128)(2,1)} %bitcast.280, bf16[1024,2048]{1,0:T(8,128)(2,1)} %bitcast.272, ...), custom_call_target="tpu_custom_call" | custom-call | flops 6442450944 | bytes 17825792 | tf_op jit(solution)/shard_map/ffn_pre/pallas_call | solution.py:44
  470.9 30.4 %ffn_gn.2 = bf16[1024,2048]{1,0:T(8,128)(2,1)} custom-call(bf16[1024,512]{1,0:T(8,128)(2,1)} %get-tuple-element.85.refs_0_, bf16[1024,512]{1,0:T(8,128)(2,1)} %get-tuple-element.86.refs_1_, bf16[1024,512]{1,0:T(8,128)(2,1)} %get-tuple-element.88.refs_2_, bf16[1024,512]{1,0:T(8,128)(2,1)} %get-tuple-element.89.refs_3_, ...), custom_call_target="tpu_custom_call" | custom-call | flops 17179869184 | bytes 37748736 | tf_op jit(solution)/shard_map/ffn_gn/pallas_call | solution.py:44
  512.0 12.2 %ffn_pre.15 = (bf16[1024,512]{1,0:T(8,128)(2,1)}, bf16[1024,512]{1,0:T(8,128)(2,1)}, bf16[1024,512]{1,0:T(8,128)(2,1)}) custom-call(s32[1]{0:T(128)} %copy.145.refs_0_, bf16[512,2048]{1,0:T(8,128)(2,1)} %bitcast.243, bf16[512,2048]{1,0:T(8,128)(2,1)} %bitcast.276, bf16[1024,2048]{1,0:T(8,128)(2,1)} %bitcast.268, ...), custom_call_target="tpu_custom_call" | custom-call | flops 6442450944 | bytes 17825792 | tf_op jit(solution)/shard_map/ffn_pre/pallas_call | solution.py:44
  524.2 30.0 %ffn_gn.3.refs_8_ = bf16[1024,2048]{1,0:T(8,128)(2,1)} custom-call(bf16[1024,512]{1,0:T(8,128)(2,1)} %get-tuple-element.98.refs_0_, bf16[1024,512]{1,0:T(8,128)(2,1)} %get-tuple-element.99.refs_1_, bf16[1024,512]{1,0:T(8,128)(2,1)} %get-tuple-element.100.refs_2_, bf16[1024,512]{1,0:T(8,128)(2,1)} %get-tuple-element.101.refs_3_, ...), custom_call_target="tpu_custom_call" | custom-call | flops 17179869184 | bytes 37748736 | tf_op jit(solution)/shard_map/ffn_gn/pallas_call | solution.py:44
  554.2 4.9 fusion.82
  559.2 22.2 %ffn_y.2 = bf16[1024,2048]{1,0:T(8,128)(2,1)} custom-call(bf16[1024,512]{1,0:T(8,128)(2,1)} %get-tuple-element.87.refs_5_.refs_0_, bf16[1024,512]{1,0:T(8,128)(2,1)} %get-tuple-element.90.refs_5_.refs_1_, bf16[1024,512]{1,0:T(8,128)(2,1)} %get-tuple-element.93.refs_5_.refs_2_, bf16[1024,512]{1,0:T(8,128)(2,1)} %get-tuple-element.106.refs_3_, ...), custom_call_target="tpu_custom_call" | custom-call | flops 8589934592 | bytes 33554432 | tf_op jit(solution)/shard_map/ffn_y/pallas_call | solution.py:44
  581.4 4.9 fusion.81
  591.0 5.1 fusion.79
  600.3 4.4 fusion.16.refs_11_
  619.7 79.9 %attend_back.1 = (bf16[2,512,1024]{2,1,0:T(8,128)(2,1)}, f32[2,8,64,128]{3,2,1,0:T(8,128)}, f32[2,4,576,128]{3,2,1,0:T(8,128)}, f32[2,4,576,128]{3,2,1,0:T(8,128)}, bf16[2,4,128,128]{3,2,1,0:T(8,128)(2,1)}) custom-call(s32[2,9]{1,0:T(2,128)} %bitcast.261, bf16[2,16,512,64]{3,2,1,0:T(8,128)(2,1)} %get-tuple-element.70.refs_1_, ...), custom_call_target="tpu_custom_call" | custom-call | tf_op jit(solution)/shard_map/attend_back/pallas_call | solution.py:44
  702.0 22.2 %ffn_y.3.refs_8_ = bf16[1024,2048]{1,0:T(8,128)(2,1)} custom-call(bf16[1024,512]{1,0:T(8,128)(2,1)} %get-tuple-element.81.refs_5_.refs_0_, bf16[1024,512]{1,0:T(8,128)(2,1)} %get-tuple-element.82.refs_5_.refs_1_, bf16[1024,512]{1,0:T(8,128)(2,1)} %get-tuple-element.83.refs_5_.refs_2_, bf16[1024,512]{1,0:T(8,128)(2,1)} %get-tuple-element.96.refs_3_, ...), custom_call_target="tpu_custom_call" | custom-call | flops 8589934592 | bytes 33554432 | tf_op jit(solution)/shard_map/ffn_y/pallas_call | solution.py:44
  724.2 5.0 fusion.80
  732.8 6.4 collective-permute-done.18
  740.2 9.1 %key_back.1 = (f32[2,576,256]{2,1,0:T(8,128)}, f32[2,576,256]{2,1,0:T(8,128)}, f32[2,2,64,128]{3,2,1,0:T(8,128)}) custom-call(s32[2,9]{1,0:T(2,128)} %bitcast.262, bf16[2,4,576,128]{3,2,1,0:T(8,128)(2,1)} %copy-done.7, bf16[2,4,576,128]{3,2,1,0:T(8,128)(2,1)} %get-tuple-element.73.refs_3_.refs_2_, bf16[4,64,128]{2,1,0:T(8,128)(2,1)} %pad_maximum_fusion.10.refs_2_.refs_3_, ...), custom_call_target="tpu_custom_call" | custom-call | tf_op jit(solution)/shard_map/key_back/pallas_call | solution.py:44
  768.8 5.5 fusion.21
  774.3 5.3 convolution_add_fusion.1
  814.4 5.3 collective-permute-done.33
  822.6 7.0 fusion.15
  (362 shorter events, 171.8 us)
Async XLA Ops:
  7.2 368.3 %all-gather.4.cloned.1.call-start = ((), (), s32[]{:S(2)}) async-start(), calls=%async_computation | async-start | bytes 7077888 | tf_op jit(solution)/shard_map/all_gather | solution.py:837
  11.6 396.8 %all-gather.6.cloned.1.call-start = ((), (), s32[]{:S(2)}) async-start(), calls=%async_computation.1 | async-start | bytes 7077888 | tf_op jit(solution)/shard_map/all_gather | solution.py:837
  12.6 446.1 %all-gather.8.cloned.1.call-start = ((), (), s32[]{:S(2)}) async-start(), calls=%async_computation.2 | async-start | bytes 7077888 | tf_op jit(solution)/shard_map/all_gather | solution.py:837
  272.9 9.1 %collective-permute-start = (bf16[2,4,64,128]{3,2,1,0:T(8,128)(2,1)S(1)}, bf16[2,4,64,128]{3,2,1,0:T(8,128)(2,1)}, u32[]{:S(2)}, u32[]{:S(2)}) collective-permute-start(bf16[2,4,64,128]{3,2,1,0:T(8,128)(2,1)S(1)} %slice.214), channel_id=1, source_target_pairs={{0,2},{1,3},{2,4},{3,5},{4,6},{5,7},{8,10},{9,11},{10,12},{11,13},... | collective-permute-start | bytes 393224 | tf_op jit(solution)/shard_map/ppermute | solution.py:935
  294.3 8.5 %collective-permute-start.2 = (bf16[2,4,128,128]{3,2,1,0:T(8,128)(2,1)}, bf16[2,4,128,128]{3,2,1,0:T(8,128)(2,1)S(1)}, u32[]{:S(2)}, u32[]{:S(2)}) collective-permute-start(bf16[2,4,128,128]{3,2,1,0:T(8,128)(2,1)} %get-tuple-element.75), channel_id=1, source_target_pairs={{0,2},{1,3},{2,0},{3,1},{4,6},{5,7},{6,4},{7,5},{8,10},{9,11},{10,... | collective-permute-start | bytes 786440 | tf_op jit(solution)/shard_map/ppermute | solution.py:33
  296.7 8.2 collective-permute-start.1
  302.9 7.6 collective-permute-start.3
  346.9 4.5 collective-permute-start.4
  357.8 47.9 %collective-permute-start.7 = (bf16[2,256,2048]{2,1,0:T(8,128)(2,1)S(1)}, bf16[2,256,2048]{2,1,0:T(8,128)(2,1)}, u32[]{:S(2)}, u32[]{:S(2)}) collective-permute-start(bf16[2,256,2048]{2,1,0:T(8,128)(2,1)S(1)} %multiply_convert_fusion), channel_id=1, source_target_pairs={{0,2},{1,3},{2,0},{3,1},{4,6},{5,7},{6,4},{7,5},{8,10},{9,11},{10,... | collective-permute-start | bytes 6291464 | tf_op jit(solution)/shard_map/ppermute | solution.py:33
  408.4 12.3 %collective-permute-start.8 = (bf16[2,256,2048]{2,1,0:T(8,128)(2,1)}, bf16[2,256,2048]{2,1,0:T(8,128)(2,1)S(1)}, u32[]{:S(2)}, u32[]{:S(2)}) collective-permute-start(bf16[2,256,2048]{2,1,0:T(8,128)(2,1)} %bitcast.244), channel_id=1, source_target_pairs={{0,1},{1,0},{2,3},{3,2},{4,5},{5,4},{6,7},{7,6},{8,9},{9,8},{10,11... | collective-permute-start | bytes 6291464 | tf_op jit(solution)/shard_map/ppermute | solution.py:29
  510.5 76.2 %collective-permute-start.11 = (bf16[2,256,2048]{2,1,0:T(8,128)(2,1)}, bf16[2,256,2048]{2,1,0:T(8,128)(2,1)S(1)}, u32[]{:S(2)}, u32[]{:S(2)}) collective-permute-start(bf16[2,256,2048]{2,1,0:T(8,128)(2,1)} %fusion.19.refs_5_), channel_id=1, source_target_pairs={{0,2},{1,3},{2,0},{3,1},{4,6},{5,7},{6,4},{7,5},{8,10},{9,11},{10,... | collective-permute-start | bytes 6291464 | tf_op jit(solution)/shard_map/ppermute | solution.py:33
  559.1 27.7 %collective-permute-start.10 = (bf16[2,256,2048]{2,1,0:T(8,128)(2,1)}, bf16[2,256,2048]{2,1,0:T(8,128)(2,1)}, u32[]{:S(2)}, u32[]{:S(2)}) collective-permute-start(bf16[2,256,2048]{2,1,0:T(8,128)(2,1)} %bitcast.19), channel_id=1, source_target_pairs={{0,1},{1,0},{2,3},{3,2},{4,5},{5,4},{6,7},{7,6},{8,9},{9,8},{10,11... | collective-permute-start | bytes 6291464 | tf_op jit(solution)/shard_map/ppermute | solution.py:29
  586.3 13.9 %collective-permute-start.13 = (bf16[2,256,2048]{2,1,0:T(8,128)(2,1)}, bf16[2,256,2048]{2,1,0:T(8,128)(2,1)}, u32[]{:S(2)}, u32[]{:S(2)}) collective-permute-start(bf16[2,256,2048]{2,1,0:T(8,128)(2,1)} %bitcast.23), channel_id=1, source_target_pairs={{0,1},{1,0},{2,3},{3,2},{4,5},{5,4},{6,7},{7,6},{8,9},{9,8},{10,11... | collective-permute-start | bytes 6291464 | tf_op jit(solution)/shard_map/ppermute | solution.py:29
  596.1 10.2 %collective-permute-start.12 = (bf16[2,256,2048]{2,1,0:T(8,128)(2,1)S(1)}, bf16[2,256,2048]{2,1,0:T(8,128)(2,1)}, u32[]{:S(2)}, u32[]{:S(2)}) collective-permute-start(bf16[2,256,2048]{2,1,0:T(8,128)(2,1)S(1)} %get-tuple-element.146), channel_id=1, source_target_pairs={{0,1},{1,0},{2,3},{3,2},{4,5},{5,4},{6,7},{7,6},{8,9},{9,8},{10,11... | collective-permute-start | bytes 6291464 | tf_op jit(solution)/shard_map/ppermute | solution.py:29
  604.7 217.9 %collective-permute-start.15 = (bf16[2,256,2048]{2,1,0:T(8,128)(2,1)}, bf16[2,256,2048]{2,1,0:T(8,128)(2,1)}, u32[]{:S(2)}, u32[]{:S(2)}) collective-permute-start(bf16[2,256,2048]{2,1,0:T(8,128)(2,1)} %fusion.16.refs_11_), channel_id=1, source_target_pairs={{0,2},{1,3},{2,0},{3,1},{4,6},{5,7},{6,4},{7,5},{8,10},{9,11},{10,... | collective-permute-start | bytes 6291464 | tf_op jit(solution)/shard_map/ppermute | solution.py:33
  699.6 30.9 %collective-permute-start.17 = (bf16[2,4,128,128]{3,2,1,0:T(8,128)(2,1)}, bf16[2,4,128,128]{3,2,1,0:T(8,128)(2,1)S(1)}, u32[]{:S(2)}, u32[]{:S(2)}) collective-permute-start(bf16[2,4,128,128]{3,2,1,0:T(8,128)(2,1)} %get-tuple-element.107.refs_8_), channel_id=1, source_target_pairs={{0,2},{1,3},{2,0},{3,1},{4,6},{5,7},{6,4},{7,5},{8,10},{9,11},{10,... | collective-permute-start | bytes 786440 | tf_op jit(solution)/shard_map/ppermute | solution.py:33
  701.1 31.7 %collective-permute-start.16 = (bf16[2,4,128,128]{3,2,1,0:T(8,128)(2,1)}, bf16[2,4,128,128]{3,2,1,0:T(8,128)(2,1)S(1)}, u32[]{:S(2)}, u32[]{:S(2)}) collective-permute-start(bf16[2,4,128,128]{3,2,1,0:T(8,128)(2,1)} %get-tuple-element.107.refs_8_), channel_id=1, source_target_pairs={{0,4},{4,0},{1,5},{5,1},{2,6},{6,2},{3,7},{7,3},{8,12},{12,8},{9,1... | collective-permute-start | bytes 786440 | tf_op jit(solution)/shard_map/ppermute | solution.py:25
  729.2 93.4 %collective-permute-start.14 = (bf16[2,256,2048]{2,1,0:T(8,128)(2,1)}, bf16[2,256,2048]{2,1,0:T(8,128)(2,1)}, u32[]{:S(2)}, u32[]{:S(2)}) collective-permute-start(bf16[2,256,2048]{2,1,0:T(8,128)(2,1)} %bitcast.25), channel_id=1, source_target_pairs={{0,1},{1,0},{2,3},{3,2},{4,5},{5,4},{6,7},{7,6},{8,9},{9,8},{10,11... | collective-permute-start | bytes 6291464 | tf_op jit(solution)/shard_map/ppermute | solution.py:29
  730.5 8.7 %collective-permute-start.18 = (bf16[2,4,128,128]{3,2,1,0:T(8,128)(2,1)S(1)}, bf16[2,4,128,128]{3,2,1,0:T(8,128)(2,1)S(1)}, u32[]{:S(2)}, u32[]{:S(2)}) collective-permute-start(bf16[2,4,128,128]{3,2,1,0:T(8,128)(2,1)S(1)} %collective-permute-done.17), channel_id=1, source_target_pairs={{0,4},{4,0},{1,5},{5,1},{2,6},{6,2},{3,7},{7,3},{8,12},{12,8},{9,1... | collective-permute-start | bytes 786440 | tf_op jit(solution)/shard_map/ppermute | solution.py:25
  750.2 6.2 collective-permute-start.19
  753.1 6.9 collective-permute-start.20
  768.7 16.3 %collective-permute-start.22 = (f32[2,256,24]{1,2,0:T(8,128)S(1)}, f32[2,256,24]{1,2,0:T(8,128)S(1)}, u32[]{:S(2)}, u32[]{:S(2)}) collective-permute-start(f32[2,256,24]{1,2,0:T(8,128)S(1)} %copy.95), channel_id=1, source_target_pairs={{0,1},{1,0},{2,3},{3,2},{4,5},{5,4},{6,7},{7,6},{8,9},{9,8},{10,11... | collective-permute-start | bytes 147464 | tf_op jit(solution)/shard_map/ppermute | solution.py:29
  787.3 6.9 collective-permute-start.25
  790.4 7.0 collective-permute-start.24
  790.5 6.8 collective-permute-start.23
  794.2 5.6 collective-permute-start.30
  799.9 4.8 collective-permute-start.31
  804.0 4.8 collective-permute-start.28
  804.7 5.8 collective-permute-start.27
  805.6 24.0 %collective-permute-start.21 = (bf16[2,256,2048]{2,1,0:T(8,128)(2,1)}, bf16[2,256,2048]{2,1,0:T(8,128)(2,1)}, u32[]{:S(2)}, u32[]{:S(2)}) collective-permute-start(bf16[2,256,2048]{2,1,0:T(8,128)(2,1)} %dynamic-slice_convert_fusion), channel_id=1, source_target_pairs={{0,1},{1,0},{2,3},{3,2},{4,5},{5,4},{6,7},{7,6},{8,9},{9,8},{10,11... | collective-permute-start | bytes 6291464 | tf_op jit(solution)/shard_map/ppermute | solution.py:29
  808.8 4.7 collective-permute-start.32
  813.5 6.2 collective-permute-start.33
  (77 other events, 2335.3 us)
Sparse Core Ops, SparseCore 0:
  11.7 179.1 all-gather.3
  193.1 110.4 all-gather.5
  305.7 99.0 all-gather.7

commit v2 on v1

--- a/solution.py
+++ b/solution.py
@@ -27,6 +27,13 @@
 
 def flip_core(block):
     return lax.ppermute(block, "head", [(i, i ^ 1) for i in range(lax.axis_size("head"))])
+
+
+def flip_core_parts(block, parts):
+    size = block.shape[0] // parts
+    return jnp.concatenate(
+        [flip_core(block[i * size : (i + 1) * size]) for i in range(parts)], axis=0
+    )
 
 
 def flip_x(block):
@@ -52,7 +59,9 @@
         ),
         out_shape=out_shape,
         compiler_params=pltpu.CompilerParams(vmem_limit_bytes=60 * 2**20),
-        cost_estimate=cost,
+        cost_estimate=cost and pl.CostEstimate(
+            flops=cost.flops // 4, bytes_accessed=cost.bytes_accessed // 4, transcendentals=0
+        ),
         name=name,
     )(*args, *after)
 
@@ -282,88 +291,87 @@
     return outs[:n], outs[n : n + len(smalls)], outs[-3:]
 
 
-def ffn_pre_kernel(
-    share_len, slots, live_ref, x_ref, more_ref, cot_ref, w_ref, mixed_ref, gg_ref, gu_ref
-):
-    tile, width = mixed_ref.shape
-    first = pl.program_id(0) < pl.num_programs(0) // 2
-    slot = lax.rem(pl.program_id(0) * tile // share_len, slots)
-    live = (slot < live_ref[0]).astype(F32)
+def ffn_kernel(chunks, before, share_len, slots, live_ref, x_ref, more_ref, cot_ref, *refs):
+    weights, refs = refs[:chunks], refs[chunks:]
+    earlier, refs = refs[: 4 * before], refs[4 * before :]
+    outs, (held, sem) = refs[:4], refs[4:]
+    step = pl.program_id(0)
+    tile = x_ref.shape[0]
+    width = held.shape[2] // 3
+    copies = [pltpu.make_async_copy(weights[c], held.at[c], sem.at[c]) for c in range(chunks)]
+
+    @pl.when(step == 0)
+    def _():
+        for copy in copies:
+            copy.start()
+
+    first = step < pl.num_programs(0) // 2
+    live = (lax.rem(step * tile // share_len, slots) < live_ref[0]).astype(F32)
     x, cot = jnp.where(first, x_ref[...], more_ref[...]), cot_ref[...]
-    gate = dot(x, w_ref[:, :width])
-    up = dot(x, w_ref[:, width : 2 * width])
-    gm = dot(cot, w_ref[:, 2 * width :]) * live
-    sig = jax.nn.sigmoid(gate)
-    silu = gate * sig
-    mixed_ref[...] = (silu * up).astype(BF16)
-    gg_ref[...] = (gm * up * (sig + silu * (1.0 - sig))).astype(BF16)
-    gu_ref[...] = (gm * silu).astype(BF16)
-
-
-def ffn_pre(x, cot, w, live_rows, share_len, slots, after=()):
+    sums = [None, None]
+    if before:
+        sums = [jnp.where(first, earlier[i][...], earlier[i + 1][...]).astype(F32) for i in (0, 2)]
+    for c in range(chunks):
+
+        @pl.when(step == 0)
+        def _():
+            copies[c].wait()
+
+        gate = dot(x, held[c, :, :width])
+        up = dot(x, held[c, :, width : 2 * width])
+        gm = dot(cot, held[c, :, 2 * width :]) * live
+        sig = jax.nn.sigmoid(gate)
+        silu = gate * sig
+        mixed = (silu * up).astype(BF16)
+        g_gate = (gm * up * (sig + silu * (1.0 - sig))).astype(BF16)
+        g_up = (gm * silu).astype(BF16)
+        parts = (
+            dot(jnp.concatenate([g_gate, g_up], axis=1), held[c, :, : 2 * width], NT),
+            dot(mixed, held[c, :, 2 * width :], NT),
+        )
+        sums = [p if t is None else t + p for t, p in zip(sums, parts)]
+
+    @pl.when(first)
+    def _():
+        outs[0][...] = sums[0].astype(BF16)
+        outs[2][...] = sums[1].astype(BF16)
+
+    @pl.when(jnp.logical_not(first))
+    def _():
+        outs[1][...] = sums[0].astype(BF16)
+        outs[3][...] = sums[1].astype(BF16)
+
+
+def ffn(x, cot, weights, live_rows, share_len, slots, before=(), after=()):
     tokens, depth = cot.shape
-    width = w.shape[1] // 3
+    chunks = len(weights)
+    width = weights[0].shape[1] // 3
     tile = min(256, share_len)
     half = tokens // tile // 2
-    out = jax.ShapeDtypeStruct((tokens, width), BF16)
+    lower = pl.BlockSpec((tile, depth), lambda i, *_: (jnp.minimum(i, half - 1), 0))
+    upper = pl.BlockSpec((tile, depth), lambda i, *_: (jnp.maximum(i - half, 0), 0))
+    out = jax.ShapeDtypeStruct((tokens // 2, depth), BF16)
     return kernel_call(
-        functools.partial(ffn_pre_kernel, share_len, slots),
-        [live_rows, x[0], x[1], cot, w],
+        functools.partial(ffn_kernel, chunks, len(before) // 4, share_len, slots),
+        [live_rows, x[0], x[1], cot, *weights, *before],
         after,
         prefetch=1,
         grid=(tokens // tile,),
-        in_specs=[
-            pl.BlockSpec((tile, depth), lambda i, *_: (jnp.minimum(i, half - 1), 0)),
-            pl.BlockSpec((tile, depth), lambda i, *_: (jnp.maximum(i - half, 0), 0)),
-            pl.BlockSpec((tile, depth), lambda i, *_: (i, 0)),
-            pl.BlockSpec((depth, 3 * width), lambda i, *_: (0, 0)),
-        ],
-        out_specs=[pl.BlockSpec((tile, width), lambda i, *_: (i, 0))] * 3,
-        out_shape=[out, out, out],
+        in_specs=[lower, upper, pl.BlockSpec((tile, depth), lambda i, *_: (i, 0))]
+        + [pl.BlockSpec(memory_space=pl.ANY)] * chunks
+        + [lower, upper] * (len(before) // 2),
+        out_specs=[lower, upper, lower, upper],
+        out_shape=[out] * 4,
+        scratch=[
+            pltpu.VMEM((chunks, depth, 3 * width), BF16),
+            pltpu.SemaphoreType.DMA((chunks,)),
+        ],
         cost=pl.CostEstimate(
-            flops=6 * tokens * depth * width,
-            bytes_accessed=4 * tokens * depth + 6 * depth * width + 6 * tokens * width,
-            transcendentals=tokens * width,
-        ),
-        name="ffn_pre",
-    )
-
-
-def ffn_post_kernel(chunks, start, lhs_count, *refs):
-    out_ref = refs[-1]
-    weights = refs[lhs_count * chunks : -1]
-    width = refs[0].shape[1]
-    total = None
-    for j in range(chunks):
-        for i in range(lhs_count):
-            at = (start + i) * width
-            part = dot(refs[lhs_count * j + i][...], weights[j][:, at : at + width], ((1,), (1,)))
-            total = part if total is None else total + part
-    out_ref[...] = total.astype(BF16)
-
-
-def ffn_post(acts, weights, start, name, after=()):
-    chunks, lhs_count = len(weights), len(acts[0])
-    tokens, width = acts[0][0].shape
-    depth = weights[0].shape[0]
-    tile = min(512, tokens)
-    cols = min(512, depth)
-    return kernel_call(
-        functools.partial(ffn_post_kernel, chunks, start, lhs_count),
-        [*[a for group in acts for a in group], *weights],
-        after,
-        grid=(depth // cols, tokens // tile),
-        in_specs=[pl.BlockSpec((tile, width), lambda d, i: (i, 0))] * (lhs_count * chunks)
-        + [pl.BlockSpec((cols, 3 * width), lambda d, i: (d, 0))] * chunks,
-        out_specs=pl.BlockSpec((tile, cols), lambda d, i: (i, d)),
-        out_shape=jax.ShapeDtypeStruct((tokens, depth), BF16),
-        cost=pl.CostEstimate(
-            flops=2 * lhs_count * tokens * depth * width * chunks,
-            bytes_accessed=(6 * depth * width + 2 * lhs_count * tokens * width) * chunks
-            + 2 * tokens * depth,
+            flops=12 * tokens * depth * width * chunks,
+            bytes_accessed=8 * tokens * depth + 6 * depth * width * chunks,
             transcendentals=0,
         ),
-        name=name,
+        name="ffn",
     )
 
 
@@ -556,7 +564,7 @@
 def attend_back_kernel(
     ends_ref, q_ref, kv_ref, phi_ref, phiq_ref, feat_ref, carry_ref, qdoc_ref, kdoc_ref, pdoc_ref,
     g_ref, gq_ref, gfeat_ref, gphi_ref, gkv_ref, gcarry_ref, vx_ref, gstate_ref, gphiq_ref, gk_ref,
-    gv_ref,
+    gv_ref, gqs_ref, gl_ref,
 ):
     r = pl.program_id(0)
     heads, length = q_ref.shape[1], q_ref.shape[2]
@@ -601,17 +609,16 @@
         from_state = dot(gx, state_low, NT)
         gstate_ref[b] = dot(phi_valid, gx, TN)
         for h in range(heads):
-            g_phi = part(from_lin, h) + jnp.where(valid, part(from_state, h), 0.0)
-            g_logit = features_back(part(phi_query, h), g_phi)
-            gphiq_ref[h, rows] = g_logit
-        pieces = []
-        for h in range(heads):
-            g_logit = gphiq_ref[h, rows]
-            pieces.append(part(g_query, h) + dot(g_logit, feat_ref[h][:, :HD], NT))
-        gq_ref[0, rows] = jnp.concatenate(pieces, axis=1).astype(BF16)
+            gphiq_ref[h, rows] = part(from_lin, h) + jnp.where(valid, part(from_state, h), 0.0)
+            gqs_ref[h, rows] = part(g_query, h)
+    for h in range(heads):
+        g_logit = features_back(phiq_ref[0, h], gphiq_ref[h])
+        gl_ref[h] = g_logit
+        gqs_ref[h] += dot(g_logit, feat_ref[h][:, :HD], NT)
+    gq_ref[0] = jnp.concatenate([gqs_ref[h] for h in range(heads)], axis=1).astype(BF16)
     for h in range(0, heads, 2):
         gfeat_ref[0, h // 2] = jnp.concatenate(
-            [dot(q_ref[0, i], gphiq_ref[i], TN) for i in (h, h + 1)], axis=1
+            [dot(q_ref[0, i], gl_ref[i], TN) for i in (h, h + 1)], axis=1
         )
     later = gstate_ref[blocks - 1]
     for b in range(blocks - 1, 0, -1):
@@ -648,9 +655,11 @@
         scratch=[
             pltpu.VMEM((ext, 2 * HD), BF16),
             pltpu.VMEM((length // WIN, 2 * HD, 2 * HD), F32),
-            pltpu.VMEM((heads, length, HD), BF16),
+            pltpu.VMEM((heads, length, 2 * HD), F32),
             pltpu.VMEM((ext, HD), F32),
             pltpu.VMEM((ext, 2 * HD), F32),
+            pltpu.VMEM((heads, length, HD), F32),
+            pltpu.VMEM((heads, length, HD), BF16),
         ],
         out_shape=[
             jax.ShapeDtypeStruct((slots, length, all_heads * HD), BF16),
@@ -665,7 +674,7 @@
 
 def key_back_kernel(
     ends_ref, kv_ref, phi_ref, feat_ref, later_ref, kdoc_ref, gphi_ref, gkv_ref,
-    gk_ref, gv_ref, gfeat_ref,
+    body_ref, edge_ref, gfeat_ref,
 ):
     r = pl.program_id(0)
     ext = kv_ref.shape[2]
@@ -686,16 +695,18 @@
         vals.append(gkv[:, HD:] + jnp.concatenate([more_v, tail], axis=0)[:, :HD])
         feats.append(dot(kv[:, :HD], g_logit, TN))
     gfeat_ref[0, 0] = jnp.concatenate(feats, axis=1)
-    gk_ref[0] = jnp.concatenate(keys, axis=1)
-    gv_ref[0] = jnp.concatenate(vals, axis=1)
+    both = jnp.concatenate(keys + vals, axis=1)
+    body_ref[0, 0] = both[WIN:]
+    edge_ref[0, 0] = both[:WIN].astype(BF16)
 
 
 def key_back(ends, kv, phi, feat, later, kdoc, gphi, gkv, after=()):
     slots, groups, ext, _ = kv.shape
     four = lambda r, s, *_: (r, s, 0, 0)
     wide = pl.BlockSpec((1, 2, ext, 2 * HD), four)
-    out = pl.BlockSpec((1, ext, 2 * HD), lambda r, s, *_: (r, 0, s))
-    flat = jax.ShapeDtypeStruct((slots, ext, groups * HD), F32)
+    body = pl.BlockSpec((1, 1, ext - WIN, 4 * HD), four)
+    edge = pl.BlockSpec((1, 1, WIN, 4 * HD), four)
+    sets = groups // 2
     return kernel_call(
         key_back_kernel,
         [ends, kv, phi, feat, later, kdoc, gphi, gkv],
@@ -711,14 +722,30 @@
             wide,
             wide,
         ],
-        out_specs=[out, out, pl.BlockSpec((1, 1, HD, 2 * HD), four)],
-        out_shape=[flat, flat, jax.ShapeDtypeStruct((slots, groups // 2, HD, 2 * HD), F32)],
+        out_specs=[body, edge, pl.BlockSpec((1, 1, HD, 2 * HD), four)],
+        out_shape=[
+            jax.ShapeDtypeStruct((slots, sets, ext - WIN, 4 * HD), F32),
+            jax.ShapeDtypeStruct((slots, sets, WIN, 4 * HD), BF16),
+            jax.ShapeDtypeStruct((slots, sets, HD, 2 * HD), F32),
+        ],
         name="key_back",
     )
 
 
-def project_kernel(sets, q_cols, k_cols, x_ref, w_ref, a_ref, b_ref, q_ref, kv_ref, small_ref):
-    x = x_ref[0]
+LOW = 128
+
+
+def normalize(values, gain):
+    scale = lax.rsqrt(jnp.mean(values * values, axis=-1, keepdims=True) + NORM_EPS)
+    return (values * scale * gain).astype(BF16)
+
+
+def project_kernel(
+    sets, q_cols, k_cols, shares, core_ref, own_ref, other_ref, gain_ref, w_ref, a_ref, b_ref, q_ref,
+    kv_ref, small_ref
+):
+    own = pl.program_id(1) // shares == core_ref[0]
+    x = normalize(jnp.where(own, own_ref[0], other_ref[0]).astype(F32), gain_ref[...])
     width = q_cols + 2 * k_cols
     small = dot(x, a_ref[...]).astype(BF16)
     small_ref[0] = small
@@ -737,32 +764,37 @@
             kv_ref[0, s * groups + g + 1] = jnp.where(low, swap(k), v).astype(BF16)
 
 
-def project(x, w, a, b, q_cols, k_cols, after=()):
-    slots, length, depth = x.shape
+def project(core, own, other, gain, w, a, b, q_cols, k_cols, after=()):
+    slots, share, depth = own.shape
+    length = 2 * share
     sets = w.shape[0]
     heads, groups = sets * q_cols // HD, sets * k_cols // HD
-    tile = min(256, length)
-    ranks = a.shape[1]
+    tile = min(256, share)
+    shares = share // tile
+    token = pl.BlockSpec((1, tile, depth), lambda r, i, *_: (r, lax.rem(i, shares), 0))
     return kernel_call(
-        functools.partial(project_kernel, sets, q_cols, k_cols),
-        [x, w, a, b],
+        functools.partial(project_kernel, sets, q_cols, k_cols, shares),
+        [core, own, other, gain, w, a, b],
         after,
+        prefetch=1,
         grid=(slots, length // tile),
         in_specs=[
-            pl.BlockSpec((1, tile, depth), lambda r, i: (r, i, 0)),
-            pl.BlockSpec(w.shape, lambda r, i: (0, 0, 0)),
-            pl.BlockSpec(a.shape, lambda r, i: (0, 0)),
-            pl.BlockSpec(b.shape, lambda r, i: (0, 0)),
+            token,
+            token,
+            pl.BlockSpec(gain.shape, lambda r, i, *_: (0, 0)),
+            pl.BlockSpec(w.shape, lambda r, i, *_: (0, 0, 0)),
+            pl.BlockSpec(a.shape, lambda r, i, *_: (0, 0)),
+            pl.BlockSpec(b.shape, lambda r, i, *_: (0, 0)),
         ],
         out_specs=[
-            pl.BlockSpec((1, heads, tile, HD), lambda r, i: (r, 0, i, 0)),
-            pl.BlockSpec((1, groups, tile, 2 * HD), lambda r, i: (r, 0, i, 0)),
-            pl.BlockSpec((1, tile, ranks), lambda r, i: (r, i, 0)),
+            pl.BlockSpec((1, heads, tile, HD), lambda r, i, *_: (r, 0, i, 0)),
+            pl.BlockSpec((1, groups, tile, 2 * HD), lambda r, i, *_: (r, 0, i, 0)),
+            pl.BlockSpec((1, tile, LOW), lambda r, i, *_: (r, i, 0)),
         ],
         out_shape=[
             jax.ShapeDtypeStruct((slots, heads, length, HD), BF16),
             jax.ShapeDtypeStruct((slots, groups, length, 2 * HD), BF16),
-            jax.ShapeDtypeStruct((slots, length, ranks), BF16),
+            jax.ShapeDtypeStruct((slots, length, LOW), BF16),
         ],
         cost=pl.CostEstimate(
             flops=2 * slots * length * w.size,
@@ -771,6 +803,229 @@
         ),
         name="project",
     )
+
+
+def halves(share, tile):
+    shares = share // tile
+    own = lambda r, i, core: (r, core[0] * shares + i, 0)
+    other = lambda r, i, core: (r, (1 - core[0]) * shares + i, 0)
+    return own, other
+
+
+def out_project_kernel(core_ref, own_ref, other_ref, w_ref, low_ref, keep_ref, away_ref):
+    depth = w_ref.shape[1]
+    half = w_ref.shape[2]
+    for src, dst in ((own_ref, keep_ref), (other_ref, away_ref)):
+        attn = src[0]
+        full = dot(attn[:, :half], w_ref[0], NT) + dot(attn[:, half:], w_ref[1], NT)
+        dst[0, :, :depth] = full.astype(BF16)
+        dst[0, :, depth:] = dot(attn, low_ref[...]).astype(BF16)
+
+
+def out_project(core, attn, w, low, share):
+    slots, length, width = attn.shape
+    depth = w.shape[1]
+    tile = min(256, share)
+    own, other = halves(share, tile)
+    out = pl.BlockSpec((1, tile, depth + LOW), lambda r, i, *_: (r, i, 0))
+    shape = jax.ShapeDtypeStruct((slots, share, depth + LOW), BF16)
+    return kernel_call(
+        out_project_kernel,
+        [core, attn, attn, w, low],
+        (),
+        prefetch=1,
+        grid=(slots, share // tile),
+        in_specs=[
+            pl.BlockSpec((1, tile, width), own),
+            pl.BlockSpec((1, tile, width), other),
+            pl.BlockSpec(w.shape, lambda r, i, *_: (0, 0, 0)),
+            pl.BlockSpec(low.shape, lambda r, i, *_: (0, 0)),
+        ],
+        out_specs=[out, out],
+        out_shape=[shape, shape],
+        name="out_project",
+    )
+
+
+def middle_kernel(hidden_ref, keep_ref, got_ref, second_ref, gain_ref, mid_ref, normed_ref, low_ref):
+    depth = hidden_ref.shape[1]
+    total = keep_ref[...].astype(F32) + got_ref[...].astype(F32)
+    low = total[:, depth:].astype(BF16)
+    low_ref[...] = low
+    mid = hidden_ref[...].astype(F32) + total[:, :depth]
+    mid = mid + ADAPTER_SCALE * dot(low, second_ref[...])
+    mid_ref[...] = mid
+    normed_ref[...] = normalize(mid, gain_ref[...])
+
+
+def tokens_call(kernel, tiled, whole, outs, name, prefetch=(), sums=()):
+    tokens = tiled[0].shape[0]
+    tile = min(256, tokens)
+    rows = lambda v: pl.BlockSpec((tile, v.shape[1]), lambda i, *_: (i, 0))
+    full = lambda v: pl.BlockSpec(v.shape, lambda i, *_: (0, 0))
+    shapes = [jax.ShapeDtypeStruct((tokens, width), kind) for width, kind in outs]
+    totals = [jax.ShapeDtypeStruct(v, F32) for v in sums]
+    return kernel_call(
+        kernel,
+        [*prefetch, *tiled, *whole],
+        (),
+        prefetch=len(prefetch),
+        grid=(tokens // tile,),
+        in_specs=[rows(v) for v in tiled] + [full(v) for v in whole],
+        out_specs=[rows(v) for v in shapes] + [full(v) for v in totals],
+        out_shape=shapes + totals,
+        name=name,
+    )
+
+
+def norm_back(values, gain, grad):
+    scale = lax.rsqrt(jnp.mean(values * values, axis=-1, keepdims=True) + NORM_EPS)
+    scaled = gain * grad
+    shared = scale * scale * scale * jnp.mean(values * scaled, axis=-1, keepdims=True)
+    return scale, scale * scaled - values * shared
+
+
+def sum_kernel(*refs):
+    refs[-1][...] = sum(r[...].astype(F32) for r in refs[:-1]).astype(BF16)
+
+
+def branch_kernel(slot_len, live_ref, mid_ref, a_ref, b_ref, c_ref, cot_ref, gain_ref, grad_ref, low_ref):
+    grad = a_ref[...].astype(F32) + b_ref[...].astype(F32) + c_ref[...].astype(F32)
+    tile = mid_ref.shape[0]
+    token = pl.program_id(0) * tile + lax.broadcasted_iota(jnp.int32, (tile, 1), 0)
+    live = token < live_ref[0] * slot_len
+    cot = jnp.where(live, cot_ref[...].astype(F32), 0.0)
+    total = cot + norm_back(mid_ref[...], gain_ref[...], grad)[1]
+    grad_ref[...] = total
+    low_ref[...] = total.astype(BF16)
+
+
+def attn_grad_kernel(
+    shares, core_ref, own_ref, other_ref, attn_ref, w_ref, second_ref, first_ref, grad_ref, sum_ref
+):
+    own = pl.program_id(1) // shares == core_ref[0]
+    x = jnp.where(own, own_ref[0], other_ref[0])
+    low = (ADAPTER_SCALE * dot(x, second_ref[...], NT)).astype(BF16)
+    half = w_ref.shape[2]
+    first = first_ref[...]
+    for s in range(2):
+        cols = slice(s * half, (s + 1) * half)
+        grad_ref[0, :, cols] = (dot(x, w_ref[s]) + dot(low, first[cols], NT)).astype(BF16)
+
+    @pl.when((pl.program_id(0) == 0) & (pl.program_id(1) == 0))
+    def _():
+        sum_ref[...] = jnp.zeros_like(sum_ref)
+
+    sum_ref[...] += dot(low, attn_ref[0], TN)
+
+
+def attn_grad(core, own, other, attn, w, second, first):
+    slots, share, depth = own.shape
+    length = 2 * share
+    width = attn.shape[2]
+    tile = min(256, share)
+    shares = share // tile
+    token = pl.BlockSpec((1, tile, depth), lambda r, i, *_: (r, lax.rem(i, shares), 0))
+    wide = pl.BlockSpec((1, tile, width), lambda r, i, *_: (r, i, 0))
+    full = lambda v: pl.BlockSpec(v.shape, lambda r, i, *_: (0,) * v.ndim)
+    total = jax.ShapeDtypeStruct((LOW, width), F32)
+    return kernel_call(
+        functools.partial(attn_grad_kernel, shares),
+        [core, own, other, attn, w, second, first],
+        (),
+        prefetch=1,
+        grid=(slots, length // tile),
+        in_specs=[token, token, wide, full(w), full(second), full(first)],
+        out_specs=[wide, full(total)],
+        out_shape=[jax.ShapeDtypeStruct(attn.shape, BF16), total],
+        name="attn_grad",
+    )
+
+
+def normed_grad_kernel(
+    q_cols, shares, core_ref, q_own_ref, q_other_ref, kv_own_ref, kv_other_ref, s_own_ref, s_other_ref,
+    back_ref, w_ref, b_ref, keep_ref, away_ref, sum_ref
+):
+    depth, width = w_ref.shape[1:]
+    core, step = core_ref[0], pl.program_id(1)
+
+    @pl.when((pl.program_id(0) == 0) & (step == 0))
+    def _():
+        sum_ref[...] = jnp.zeros_like(sum_ref)
+
+    sides = (
+        (q_own_ref, kv_own_ref, s_own_ref, keep_ref, core),
+        (q_other_ref, kv_other_ref, s_other_ref, away_ref, 1 - core),
+    )
+    for q_ref, kv_ref, s_ref, out_ref, share in sides:
+        tile = q_ref.shape[1]
+        last = (share * shares + step == 2 * shares - 1).astype(F32)
+        full = low = None
+        for s in range(2):
+            kv = kv_ref[0, s]
+            edge = back_ref[0, s].astype(F32) * last
+            if tile > WIN:
+                edge = jnp.concatenate([jnp.zeros((tile - WIN, kv.shape[1]), F32), edge], axis=0)
+            kv = (kv + edge).astype(BF16)
+            q = q_ref[0, :, s * q_cols : (s + 1) * q_cols]
+            grads = jnp.concatenate([q, kv], axis=1)
+            part = dot(grads, w_ref[s], NT)
+            small = dot(grads, b_ref[:, s * width : (s + 1) * width], NT)
+            full = part if full is None else full + part
+            low = small if low is None else low + small
+            sum_ref[s] += dot(s_ref[0], grads, TN)
+        out_ref[0, :, :depth] = full.astype(BF16)
+        out_ref[0, :, depth:] = (ADAPTER_SCALE * low).astype(BF16)
+
+
+def normed_grad(core, q, kv, small, back, w, b, q_cols, share):
+    slots, length, q_width = q.shape
+    sets, depth, width = w.shape
+    tile = min(256, share)
+    shares = share // tile
+    own, other = halves(share, tile)
+    four = lambda f: (lambda r, i, core: (r, 0, f(r, i, core)[1], 0))
+    out = pl.BlockSpec((1, tile, depth + LOW), lambda r, i, *_: (r, i, 0))
+    shape = jax.ShapeDtypeStruct((slots, share, depth + LOW), BF16)
+    total = jax.ShapeDtypeStruct((sets, LOW, width), F32)
+    kv_block = (1, sets, tile, kv.shape[3])
+    return kernel_call(
+        functools.partial(normed_grad_kernel, q_cols, shares),
+        [core, q, q, kv, kv, small, small, back, w, b],
+        (),
+        prefetch=1,
+        grid=(slots, shares),
+        in_specs=[
+            pl.BlockSpec((1, tile, q_width), own),
+            pl.BlockSpec((1, tile, q_width), other),
+            pl.BlockSpec(kv_block, four(own)),
+            pl.BlockSpec(kv_block, four(other)),
+            pl.BlockSpec((1, tile, LOW), own),
+            pl.BlockSpec((1, tile, LOW), other),
+            pl.BlockSpec((1, sets, WIN, kv.shape[3]), lambda r, i, *_: (r, 0, 0, 0)),
+            pl.BlockSpec(w.shape, lambda r, i, *_: (0, 0, 0)),
+            pl.BlockSpec(b.shape, lambda r, i, *_: (0, 0)),
+        ],
+        out_specs=[out, out, pl.BlockSpec(total.shape, lambda r, i, *_: (0, 0, 0))],
+        out_shape=[shape, shape, total],
+        name="normed_grad",
+    )
+
+
+def finish_kernel(keep_ref, got_ref, hidden_ref, mid_ref, gain_ref, first_ref, out_ref, sum_ref):
+    depth = hidden_ref.shape[1]
+    total = keep_ref[...].astype(F32) + got_ref[...].astype(F32)
+    low = total[:, depth:].astype(BF16)
+    grad = total[:, :depth] + dot(low, first_ref[...])
+    values, gain = hidden_ref[...].astype(F32), gain_ref[...]
+    scale, back = norm_back(values, gain, grad)
+    out_ref[...] = (mid_ref[...] + back).astype(BF16)
+
+    @pl.when(pl.program_id(0) == 0)
+    def _():
+        sum_ref[...] = jnp.zeros_like(sum_ref)
+
+    sum_ref[...] += dot(low, (values * scale * gain).astype(BF16), TN)
 
 
 def local(
@@ -836,7 +1091,6 @@
     ffn_later = [
         lax.all_gather(v, ("row", "seq"), axis=0, tiled=True) for v in ffn_shards[1:]
     ]
-    half_chunk = ffn_shards[0].shape[1] // 2
     own_smalls = [
         query_feature, key_feature, query_adapt_out, key_adapt_out, value_adapt_out, outproj_adapt_in
     ]
@@ -846,8 +1100,7 @@
         [
             (0, (0, qkv_shard.shape[1]), True, 0),
             (1, (0, out_shard.shape[1]), True, 0),
-            (2, (0, half_chunk), True, rows * seqs),
-            (2, (half_chunk, half_chunk), False, rows * seqs),
+            (2, (0, ffn_shards[0].shape[1]), True, rows * seqs),
         ],
         own_smalls,
         hidden_in,
@@ -893,17 +1146,11 @@
                 held.append((source, start))
         return held[1:]
 
-    gain_attn = norm_attn.astype(F32)
-    gain_ffn = norm_ffn.astype(F32)
-    slot_live = (jnp.arange(slots) < live_rows[0])[:, None, None]
-    grad_low = jnp.where(slot_live, grad_out, jnp.zeros_like(grad_out))
-    grad_share = grad_low.astype(F32)
-    rows_float = hidden_in.astype(F32)
-    normed_share = rms_scaled(rows_float, gain_attn).astype(BF16)
-    normed_other = rms_scaled(tie(hidden_other, qkv_mat).astype(F32), gain_attn).astype(BF16)
-    normed = in_order(normed_share, normed_other)
-
-    flat = normed.reshape(slots * piece_len, model_dim)
+    gain_attn = norm_attn.astype(F32)[None]
+    gain_ffn = norm_ffn.astype(F32)[None]
+    core_index = core.astype(jnp.int32).reshape(1)
+    flat_tokens = lambda v: v.reshape(-1, v.shape[-1])
+
     set_cols = q_cols + 2 * k_cols
     adapt_in_all = jnp.concatenate([query_adapt_in, key_adapt_in, value_adapt_in], axis=1)
 
@@ -920,9 +1167,15 @@
         ]
         return jnp.concatenate([by_sets(r) for r in rows], axis=0)
 
-    adapt_out_all = diagonal([q_out, k_out, v_out])
+    pad_rows = lambda v: jnp.pad(v, ((0, LOW - v.shape[0]), (0, 0)))
+    pad_cols = lambda v: jnp.pad(v, ((0, 0), (0, LOW - v.shape[1])))
+    adapt_in_all = pad_cols(adapt_in_all)
+    adapt_out_all = pad_rows(diagonal([q_out, k_out, v_out]))
+    second = pad_rows(projection_adapter_second)
+    o_in = pad_cols(o_in)
     query, kv_own, small = project(
-        normed, qkv_mat, adapt_in_all, adapt_out_all, q_cols, k_cols
+        core_index, hidden_in, hidden_other, gain_attn, qkv_mat, adapt_in_all, adapt_out_all, q_cols,
+        k_cols,
     )
 
     def along_pieces(block, distance):
@@ -946,117 +1199,94 @@
     attn, phi_query = attend(
         end_docs, query, kv, phi_key, query_feat, carry, query_doc_lanes, key_doc_lanes, pair_docs
     )
-    attn = attn.reshape(slots * piece_len, -1)
-
-    half_q = q_cols
-    proj_part = dot(attn[:, :half_q], out_mat[0], NT) + dot(attn[:, half_q:], out_mat[1], NT)
-    proj_part = proj_part.reshape(slots, piece_len, model_dim)
-    low_part = dot(attn, o_in).reshape(slots, piece_len, RANK)
-    proj_sum = own_half(proj_part) + flip_core(other_half(proj_part).astype(BF16)).astype(F32)
-    low_mix = (own_half(low_part) + flip_core(other_half(low_part))).astype(BF16)
-    mid_rows = (
-        rows_float
-        + proj_sum
-        + ADAPTER_SCALE
-        * dot(low_mix.reshape(-1, RANK), projection_adapter_second).reshape(rows_float.shape)
-    )
-
-    nmid = rms_scaled(mid_rows, gain_ffn).astype(BF16)
+
+    keep, away = out_project(core_index, attn, out_mat, o_in, share_len)
+    mid_rows, nmid, low_mix = tokens_call(
+        middle_kernel,
+        [flat_tokens(v) for v in (hidden_in, keep, flip_core(away))],
+        [second, gain_ffn],
+        [(model_dim, F32), (model_dim, BF16), (LOW, BF16)],
+        "middle",
+    )
+
     nmid_x = flip_x(nmid)
 
     def chip_tokens(own):
-        return own.reshape(-1, model_dim), flip_core(own).reshape(-1, model_dim)
-
-    def sum_away(away):
-        away = away.reshape(2, slots, share_len, model_dim)
-        return (away[0].astype(F32) + flip_core(away[1]).astype(F32)).astype(BF16)
-
-    def sum_mine(mine, back):
-        mine = mine.reshape(2, slots, share_len, model_dim)
-        return mine[0].astype(F32) + flip_core(mine[1]).astype(F32) + back.astype(F32)
-
-    flat_tokens = lambda v: v.reshape(-1, model_dim)
+        return own, flip_core(own)
+
+    def sum_away(own, other):
+        return (own.astype(F32) + flip_core(other).astype(F32)).astype(BF16)
+
     x_mine = chip_tokens(nmid)
     c_mine, c_away = flat_tokens(cot_mine), flat_tokens(cot_away)
-    pre = lambda x, c, w, after: ffn_pre(x, c, w, live_rows, share_len, slots, after)
-    acts_mine, acts_away, after = [], [], ()
-    for w in ffn_mats[:-1]:
-        acts_mine.append(pre(x_mine, c_mine, w, after))
-        after = (acts_mine[-1][0],)
-    x_away = chip_tokens(hold(nmid_x, (acts_mine[1][0],)))
-    for w in ffn_mats:
-        acts_away.append(pre(x_away, c_away, w, after))
-        after = (acts_away[-1][0],)
-    gn_away = ffn_post([v[1:] for v in acts_away], ffn_mats, 0, "ffn_gn")
-    gn_there = sum_away(gn_away)
+    run = lambda x, c, w, before=(), after=(): ffn(
+        x, c, w, live_rows, share_len, slots, before, after
+    )
+    mine = run(x_mine, c_mine, ffn_mats[:-1])
+    x_away = chip_tokens(hold(nmid_x, (mine[0],)))
+    away = run(x_away, c_away, ffn_mats[:-1])
+    away = run(x_away, c_away, ffn_mats[-1:], away)
+    gn_there = sum_away(*away[:2])
     gn_back = flip_x(gn_there)
-    acts_mine.append(pre(x_mine, c_mine, ffn_mats[-1], (gn_there,)))
-    gn_mine = ffn_post([v[1:] for v in acts_mine], ffn_mats, 0, "ffn_gn")
-    y_away = ffn_post([v[:1] for v in acts_away], ffn_mats, 2, "ffn_y", (gn_mine,))
-    y_there = sum_away(y_away)
+    gn_own, gn_other, y_own, y_other = run(
+        x_mine, c_mine, ffn_mats[-1:], mine, (gn_there,)
+    )
+    y_there = sum_away(*away[2:])
     y_back = flip_x(y_there)
-    grad_nmid = sum_mine(gn_mine, gn_back)
-    grad_mid = grad_share + rms_back(mid_rows, gain_ffn, grad_nmid)
-
-    branch_share = grad_mid.astype(BF16)
-    branch = in_order(branch_share, flip_core(branch_share)).reshape(-1, model_dim)
-    grad_low_mix = (
-        ADAPTER_SCALE * dot(branch, projection_adapter_second, ((1,), (1,)))
-    ).astype(BF16)
-    sum_o_in = dot(grad_low_mix, attn, TN)
-    sum_o_out = ADAPTER_SCALE * dot(
-        low_mix.reshape(-1, RANK), branch_share.reshape(-1, model_dim), ((0,), (0,))
-    )
-    branch_out = jnp.concatenate([dot(branch, out_mat[0]), dot(branch, out_mat[1])], axis=1)
-    grad_attn = (branch_out + dot(grad_low_mix, o_in, NT)).astype(BF16)
+    grad_mid, branch = tokens_call(
+        functools.partial(branch_kernel, share_len),
+        [mid_rows, gn_own, flip_core_parts(gn_other, 4), gn_back, flat_tokens(grad_out)],
+        [gain_ffn],
+        [(model_dim, F32), (model_dim, BF16)],
+        "branch",
+        prefetch=[live_rows],
+    )
+
+    shaped = lambda v: v.reshape(slots, share_len, -1)
+    grad_attn, sum_o_in = attn_grad(
+        core_index, shaped(branch), shaped(flip_core(branch)), attn, out_mat, second, o_in
+    )
+    sum_o_in = sum_o_in[:RANK]
+    sum_o_out = ADAPTER_SCALE * dot(low_mix, branch, TN)[:RANK]
 
     grad_query, feat_query, gphi, gkv, grad_carry = attend_back(
         end_docs, query, kv, phi_key, phi_query, query_feat, carry, query_doc_lanes, key_doc_lanes,
-        pair_docs, grad_attn.reshape(slots, piece_len, -1), (y_there,),
-    )
-    y_mine = ffn_post([v[:1] for v in acts_mine], ffn_mats, 2, "ffn_y", (grad_carry,))
-    block_out = (mid_rows + sum_mine(y_mine, y_back)).astype(BF16)
+        pair_docs, grad_attn, (y_there,),
+    )
+    block_out = tokens_call(
+        sum_kernel, [mid_rows, y_own, flip_core(y_other), y_back], [], [(model_dim, BF16)], "sum_y"
+    )[0].reshape(hidden_in.shape)
     later = jnp.zeros(grad_carry.shape, F32)
     for source, part in from_pieces(grad_carry):
         start = lax.dynamic_index_in_dim(piece_docs, source, 1, keepdims=False)
         keep = (source > piece) & (start == next_doc)
         later = later + jnp.where(keep[:, None, None, None], part.astype(F32), 0.0)
-    grad_key_ext, grad_value_ext, feat_key = key_back(
-        end_docs, kv, phi_key, key_feat, later, key_doc_lanes, gphi, gkv, (y_mine,)
+    grad_body, grad_edge, feat_key = key_back(
+        end_docs, kv, phi_key, key_feat, later, key_doc_lanes, gphi, gkv, (y_back,)
     )
     sum_q_feat = jnp.sum(feat_query, axis=0).reshape(2, -1, 2 * HD)
     sum_k_feat = jnp.sum(feat_key, axis=0).reshape(2, -1, 2 * HD)
-    tail_pad = ((0, 0), (piece_len - WIN, 0), (0, 0))
-
-    def fold_back(ext):
-        back = along_pieces(ext[:, :WIN].astype(BF16), -1).astype(F32)
-        return (ext[:, WIN:] + jnp.pad(back, tail_pad)).astype(BF16)
-
-    grad_key_low = fold_back(grad_key_ext).reshape(slots * piece_len, -1)
-    grad_value_low = fold_back(grad_value_ext).reshape(slots * piece_len, -1)
-    grad_query_low = grad_query.reshape(slots * piece_len, -1)
-
-    nt = ((1,), (1,))
-    stacked = by_sets([grad_query_low, grad_key_low, grad_value_low])
-    grad_normed_part = dot(stacked[:, :set_cols], qkv_mat[0], nt) + dot(
-        stacked[:, set_cols:], qkv_mat[1], nt
-    )
-    small_part = ADAPTER_SCALE * dot(stacked, adapt_out_all, nt)
-    small = small.reshape(slots * piece_len, 3 * RANK)
+
+    keep, away, outs = normed_grad(
+        core_index, grad_query, grad_body, small, along_pieces(grad_edge, -1), qkv_mat, adapt_out_all,
+        q_cols, share_len,
+    )
+    outs = ADAPTER_SCALE * outs
     outs = [
-        ADAPTER_SCALE * dot(small[:, i * RANK : (i + 1) * RANK], g, ((0,), (0,)))
-        for i, g in enumerate((grad_query_low, grad_key_low, grad_value_low))
+        outs[:, :RANK, :q_cols],
+        outs[:, RANK : 2 * RANK, q_cols : q_cols + k_cols],
+        outs[:, 2 * RANK : 3 * RANK, q_cols + k_cols :],
     ]
-    grad_normed_part = grad_normed_part.reshape(slots, piece_len, model_dim)
-    small_part = small_part.reshape(slots, piece_len, 3 * RANK)
-    grad_normed = own_half(grad_normed_part) + flip_core(
-        other_half(grad_normed_part).astype(BF16)
-    ).astype(F32)
-    small_low = (own_half(small_part) + flip_core(other_half(small_part))).astype(BF16)
-    small_low = small_low.reshape(-1, 3 * RANK)
-    grad_normed = grad_normed + dot(small_low, adapt_in_all, nt).reshape(rows_float.shape)
-    sum_in = dot(small_low, normed_share.reshape(-1, model_dim), ((0,), (0,)))
-    grad_hidden = (grad_mid + rms_back(rows_float, gain_attn, grad_normed)).astype(BF16)
+    grad_hidden, sum_in = tokens_call(
+        finish_kernel,
+        [flat_tokens(keep), flat_tokens(flip_core(away)), flat_tokens(hidden_in), grad_mid],
+        [gain_attn, adapt_in_all.T],
+        [(model_dim, BF16)],
+        "finish",
+        sums=[(LOW, model_dim)],
+    )
+    grad_hidden = grad_hidden.reshape(hidden_in.shape)
+    sum_in = sum_in[: 3 * RANK]
 
     by_rows = jnp.concatenate([sum_in, sum_o_out], axis=0)
     width = model_dim // (rows * seqs * heads)
@@ -1066,10 +1296,11 @@
     in_parts = by_rows.reshape(4, RANK, width)
 
     def lanes_of(v):
-        v = v.reshape(RANK, 2, -1, 2 * HD).transpose(1, 2, 0, 3)
+        v = v.reshape(2, RANK, -1, 2 * HD).transpose(0, 2, 1, 3)
         return v.reshape(2, -1, 2 * HD)
 
-    packed = [lanes_of(v) for v in outs + [sum_o_in]] + [sum_q_feat, sum_k_feat]
+    o_sets = jnp.stack([sum_o_in[:, :q_cols], sum_o_in[:, q_cols:]])
+    packed = [lanes_of(v) for v in outs + [o_sets]] + [sum_q_feat, sum_k_feat]
     sizes = [v.shape[1] for v in packed]
     packed = jnp.concatenate(packed, axis=1)
     kept = lax.dynamic_index_in_dim(packed, x_place, 0, keepdims=False)

time: 850 us -> 725 us (0.85)
  local copies, waits for them, and re-layouts: 67.1 us -> 24.8 us
  matrix products: 41.6 us -> 0.42 us
  other arithmetic: 52.7 us -> 27.2 us
  Pallas kernels: 571 us -> 546 us
    dot_general x18 -> x1, matrix products: 41.6 us -> 0.42 us  [dot(): return lax.dot_general(a, b, (dims, ((), ())), preferred_element_type=F32)]
    pallas_call x1, Pallas kernels: 230 us -> 207 us  [gather(): pl.pallas_call(functools.partial(gather_kernel, plan, rows, seqs, parts,...]
    convert_element_type x12 -> x2, other arithmetic: 23.9 us -> 6.17 us  [sum_away(): return (own.astype(F32) + flip_core(other).astype(F32)).astype(BF16)]
    slice x7 -> x3, local copies, waits for them, and re-layouts: 19.6 us -> 2.78 us  [the longest x1 1.66 us: flip_core_parts(): block[i * size:(i + 1) * size]]
    unnamed x171 -> x95, local copies, waits for them, and re-layouts: 23.7 us -> 10.7 us
    ppermute x11 -> x12, waiting for transfers between devices: 6.73 us -> 18 us  [flip_core(): lax.ppermute(block, 'head', [(i, i ^ 1) for i in range(lax.axis_size('hea...]
    pallas_call x18 -> x17, Pallas kernels: 341 us -> 339 us  [kernel_call(): pl.pallas_call(body, grid_spec=pltpu.PrefetchScalarGridSpec(num_scalar_pr...]
  transfers between devices with their start and end apart: 37 -> 37, of which waited for: 20 -> 20; matrix products, arithmetic and copies ran while one was open for 16% -> 6% of each run, Pallas kernels for 63% -> 72%
where the time goes in v2:
time: 725 us; the launch traced here: 720 us
  Pallas kernels  546 us (75%)
  waiting for transfers between devices  69.2 us (10%)
  starting transfers between devices  37.2 us (5%)
  other arithmetic  27.2 us (4%)
  local copies, waits for them, and re-layouts  24.8 us (3%)
  between operations  15.5 us (2%)
    pallas_call x17, Pallas kernels, kernel_call(): pl.pallas_call(body, grid_spec=pltpu.PrefetchScalarGridSpec(num_scalar_pr...  339 us
    pallas_call x1, Pallas kernels, gather(): pl.pallas_call(functools.partial(gather_kernel, plan, rows, seqs, parts,...  207 us
    ppermute x6, waiting for transfers between devices, flip_x(): lax.ppermute(block, 'head', [(i, i ^ 2) for i in range(lax.axis_size('hea...  27.3 us
    ppermute x12, waiting for transfers between devices, flip_core(): lax.ppermute(block, 'head', [(i, i ^ 1) for i in range(lax.axis_size('hea...  18 us
    ppermute x11, waiting for transfers between devices, shift(): lax.ppermute(block, axis, [(i, (i + distance) % size) for i in range(size)])  16.7 us
    ppermute x11, starting transfers between devices, shift(): lax.ppermute(block, axis, [(i, (i + distance) % size) for i in range(size)])  15.3 us
  transfers between devices with their start and end apart: 37, of which 20 were waited for; matrix products, arithmetic and copies ran while one was open for 6% of the time, Pallas kernels for 72%

profile of v2, /device:TPU:0, one launch (start us, length us, event | category | flops | bytes accessed | tf_op | source)
XLA Modules:
  0.0 720.3 jit_solution(8022993659460979341)
XLA Ops:
  18.4 206.6 %gather.1 = (bf16[2,2048,768]{2,1,0:T(8,128)(2,1)}, bf16[2,2048,512]{2,1,0:T(8,128)(2,1)}, bf16[2048,1536]{1,0:T(8,128)(2,1)}, bf16[8,64,64]{2,1,0:T(8,128)(2,1)...) custom-call(bf16[256,768]{1,0:T(8,128)(2,1)} %pad_maximum_fusion.5.r, ...), custom_call_target="tpu_custom_call" | custom-call | tf_op jit(solution)/shard_map/gather/pallas_call | solution.py:275
  228.1 17.5 %project.1 = (bf16[2,16,512,64]{3,2,1,0:T(8,128)(2,1)}, bf16[2,4,512,128]{3,2,1,0:T(8,128)(2,1)}, bf16[2,512,128]{2,1,0:T(8,128)(2,1)}) custom-call(s32[1]{0:T(128)} %bitcast.1.refs_0_, bf16[2,256,2048]{2,1,0:T(8,128)(2,1)} %refs_1_.1, bf16[2,256,2048]{2,1,0:T(8,128)(2,1)} %get-tuple-element.69.refs_2_, f32[1,2048]{1,0:T(1,128)} %bitcast.149, ...), custom_call_target="tpu_custom_call" | custom-call | flops 1610612736 | bytes 2621440 | tf_op jit(solution)/shard_map/project/pallas_call | solution.py:51
  254.0 8.7 %key_state.1 = (bf16[2,4,576,128]{3,2,1,0:T(8,128)(2,1)}, bf16[2,4,128,128]{3,2,1,0:T(8,128)(2,1)}) custom-call(s32[2,9]{1,0:T(2,128)} %bitcast.154, bf16[2,4,576,128]{3,2,1,0:T(8,128)(2,1)} %copy-done, bf16[4,64,128]{2,1,0:T(8,128)(2,1)} %pad_maximum_fusion.8.refs_2_.refs_3_, s32[2,576,128]{2,1,0:T(8,128)} %broadcast_in_dim.69.refs_3_.refs_7_.refs_8_.refs_5_), custom_call_target="tpu_custom_call" | custom-call | tf_op jit(solution)/shard_map/key_state/pallas_call | solution.py:51
  267.0 4.4 collective-permute-done.2
  275.7 3.7 collective-permute-done.3
  281.5 22.5 %attend.1 = (bf16[2,512,1024]{2,1,0:T(8,128)(2,1)}, bf16[2,16,512,128]{3,2,1,0:T(8,128)(2,1)}) custom-call(s32[2,9]{1,0:T(2,128)} %bitcast.155, bf16[2,16,512,64]{3,2,1,0:T(8,128)(2,1)} %get-tuple-element.74.refs_1_, bf16[2,4,576,128]{3,2,1,0:T(8,128)(2,1)} %copy-done, bf16[2,4,576,128]{3,2,1,0:T(8,128)(2,1)} %get-tuple-element.77.refs_3_.refs_2_, ...), custom_call_target="tpu_custom_call" | custom-call | tf_op jit(solution)/shard_map/attend/pallas_call | solution.py:51
  304.0 8.9 %out_project.1 = (bf16[2,256,2176]{2,1,0:T(8,128)(2,1)}, bf16[2,256,2176]{2,1,0:T(8,128)(2,1)}) custom-call(s32[1]{0:T(128)} %bitcast.1.refs_0_, bf16[2,512,1024]{2,1,0:T(8,128)(2,1)} %get-tuple-element.80.refs_1_.refs_2_.refs_3_, bf16[2,512,1024]{2,1,0:T(8,128)(2,1)} %get-tuple-element.80.refs_1_.refs_2_.refs_3_, ...), custom_call_target="tpu_custom_call" | custom-call | tf_op jit(solution)/shard_map/out_project/pallas_call | solution.py:51
  314.4 3.1 collective-permute-done.4
  318.8 5.8 middle.1
  329.2 52.7 %ffn.4 = (bf16[512,2048]{1,0:T(8,128)(2,1)}, bf16[512,2048]{1,0:T(8,128)(2,1)}, bf16[512,2048]{1,0:T(8,128)(2,1)}, bf16[512,2048]{1,0:T(8,128)(2,1)}) custom-call(s32[1]{0:T(128)S(6)} %copy.123.refs_0_, bf16[512,2048]{1,0:T(8,128)(2,1)} %get-tuple-element.86.refs_1_, bf16[512,2048]{1,0:T(8,128)(2,1)} %collective-permute-done.5.refs_2_, ...), custom_call_target="tpu_custom_call" | custom-call | flops 9663676416 | bytes 8912896 | tf_op jit(solution)/shard_map/ffn/pallas_call | solution.py:51
  386.1 4.1 collective-permute-done.7.refs_2_
  391.6 52.4 %ffn.5 = (bf16[512,2048]{1,0:T(8,128)(2,1)}, bf16[512,2048]{1,0:T(8,128)(2,1)}, bf16[512,2048]{1,0:T(8,128)(2,1)}, bf16[512,2048]{1,0:T(8,128)(2,1)}) custom-call(s32[1]{0:T(128)S(6)} %copy.123.refs_0_, bf16[512,2048]{1,0:T(8,128)(2,1)} %hold.1.refs_1_, bf16[512,2048]{1,0:T(8,128)(2,1)} %copy-done.6, bf16[1024,2048]{1,0:T(8,128)(2,1)} %bitcast.129, ...), custom_call_target="tpu_custom_call" | custom-call | flops 9663676416 | bytes 8912896 | tf_op jit(solution)/shard_map/ffn/pallas_call | solution.py:51
  444.1 25.5 %ffn.6 = (bf16[512,2048]{1,0:T(8,128)(2,1)}, bf16[512,2048]{1,0:T(8,128)(2,1)}, bf16[512,2048]{1,0:T(8,128)(2,1)}, bf16[512,2048]{1,0:T(8,128)(2,1)}) custom-call(s32[1]{0:T(128)S(6)} %copy.123.refs_0_, bf16[512,2048]{1,0:T(8,128)(2,1)} %hold.1.refs_1_, bf16[512,2048]{1,0:T(8,128)(2,1)} %copy-done.6, bf16[1024,2048]{1,0:T(8,128)(2,1)} %bitcast.130, ...), custom_call_target="tpu_custom_call" | custom-call | flops 3221225472 | bytes 5767168 | tf_op jit(solution)/shard_map/ffn/pallas_call | solution.py:51
  470.2 4.5 collective-permute-done.8
  479.0 25.4 %ffn.7 = (bf16[512,2048]{1,0:T(8,128)(2,1)}, bf16[512,2048]{1,0:T(8,128)(2,1)}, bf16[512,2048]{1,0:T(8,128)(2,1)}, bf16[512,2048]{1,0:T(8,128)(2,1)}) custom-call(s32[1]{0:T(128)S(6)} %copy.123.refs_0_, bf16[512,2048]{1,0:T(8,128)(2,1)} %get-tuple-element.86.refs_1_, bf16[512,2048]{1,0:T(8,128)(2,1)} %collective-permute-done.5.refs_2_, ...), custom_call_target="tpu_custom_call" | custom-call | flops 3221225472 | bytes 5767168 | tf_op jit(solution)/shard_map/ffn/pallas_call | solution.py:51
  511.9 13.1 %collective-permute-done.16.refs_4_ = bf16[512,2048]{1,0:T(8,128)(2,1)} collective-permute-done((bf16[512,2048]{1,0:T(8,128)(2,1)S(1)}, bf16[512,2048]{1,0:T(8,128)(2,1)}, u32[]{:S(2)}, u32[]{:S(2)}) %collective-permute-start.16) | collective-permute-done | bytes 2097184 | tf_op jit(solution)/shard_map/ppermute | solution.py:40
  525.1 8.6 %branch.1 = (f32[512,2048]{1,0:T(8,128)}, bf16[512,2048]{1,0:T(8,128)(2,1)}) custom-call(s32[1]{0:T(128)S(6)} %copy.123.refs_0_, f32[512,2048]{1,0:T(8,128)} %get-tuple-element.85.refs_0_.refs_1_, bf16[512,2048]{1,0:T(8,128)(2,1)} %get-tuple-element.105.refs_2_, bf16[512,2048]{1,0:T(8,128)(2,1)} %pad_maximum_fusion.refs_3_, ...), custom_call_target="tpu_custom_call" | custom-call | tf_op jit(solution)/shard_map/branch/pallas_call | solution.py:51
  533.7 3.8 add_convert_fusion.refs_11_
  539.3 12.7 %attn_grad.1 = (bf16[2,512,1024]{2,1,0:T(8,128)(2,1)}, f32[128,1024]{1,0:T(8,128)}) custom-call(s32[1]{0:T(128)} %bitcast.1.refs_0_, bf16[2,256,2048]{2,1,0:T(8,128)(2,1)} %bitcast.128, bf16[2,256,2048]{2,1,0:T(8,128)(2,1)} %bitcast.13.refs_2_, bf16[2,512,1024]{2,1,0:T(8,128)(2,1)} %get-tuple-element.80.refs_1_.refs_2_.refs_3_, ...), custom_call_target="tpu_custom_call" | custom-call | tf_op jit(solution)/shard_map/attn_grad/pallas_call | solution.py:51
  552.0 60.2 %attend_back.1 = (bf16[2,512,1024]{2,1,0:T(8,128)(2,1)}, f32[2,8,64,128]{3,2,1,0:T(8,128)}, f32[2,4,576,128]{3,2,1,0:T(8,128)}, f32[2,4,576,128]{3,2,1,0:T(8,128)}, bf16[2,4,128,128]{3,2,1,0:T(8,128)(2,1)}) custom-call(s32[2,9]{1,0:T(2,128)} %bitcast.156, bf16[2,16,512,64]{3,2,1,0:T(8,128)(2,1)} %get-tuple-element.74.refs_1_, ...), custom_call_target="tpu_custom_call" | custom-call | tf_op jit(solution)/shard_map/attend_back/pallas_call | solution.py:51
  614.8 6.1 collective-permute-done.19
  623.7 4.8 collective-permute-done.20
  630.9 9.1 %key_back.1 = (f32[2,2,512,256]{3,2,1,0:T(8,128)}, bf16[2,2,64,256]{3,2,1,0:T(8,128)(2,1)}, f32[2,2,64,128]{3,2,1,0:T(8,128)}) custom-call(s32[2,9]{1,0:T(2,128)} %bitcast.157, bf16[2,4,576,128]{3,2,1,0:T(8,128)(2,1)} %copy-done, bf16[2,4,576,128]{3,2,1,0:T(8,128)(2,1)} %get-tuple-element.77.refs_3_.refs_2_, ...), custom_call_target="tpu_custom_call" | custom-call | tf_op jit(solution)/shard_map/key_back/pallas_call | solution.py:51
  643.0 4.1 collective-permute-done.21.refs_7_
  647.8 13.6 %normed_grad.1 = (bf16[2,256,2176]{2,1,0:T(8,128)(2,1)}, bf16[2,256,2176]{2,1,0:T(8,128)(2,1)}, f32[2,128,768]{2,1,0:T(8,128)}) custom-call(s32[1]{0:T(128)} %bitcast.1.refs_0_, bf16[2,512,1024]{2,1,0:T(8,128)(2,1)} %get-tuple-element.109.refs_1_.refs_2_, bf16[2,512,1024]{2,1,0:T(8,128)(2,1)} %get-tuple-element.109.refs_1_.refs_2_, ...), custom_call_target="tpu_custom_call" | custom-call | tf_op jit(solution)/shard_map/normed_grad/pallas_call | solution.py:51
  664.6 3.6 collective-permute-done.30
  669.9 3.0 collective-permute-done.31
  674.5 5.7 sum_y.1
  680.3 4.8 collective-permute-start.33
  685.0 7.2 finish.1
  703.0 3.7 collective-permute-done.26
  706.9 3.7 collective-permute-start.29
  (239 shorter events, 90.7 us)
Async XLA Ops:
  7.2 322.0 %all-gather.6.cloned.1.call-start = ((), (), s32[]{:S(2)}) async-start(), calls=%async_computation.1 | async-start | bytes 7077888 | tf_op jit(solution)/shard_map/all_gather | solution.py:1092
  11.4 317.8 %all-gather.8.cloned.1.call-start = ((), (), s32[]{:S(2)}) async-start(), calls=%async_computation.2 | async-start | bytes 7077888 | tf_op jit(solution)/shard_map/all_gather | solution.py:1092
  12.4 431.6 %all-gather.4.cloned.1.call-start = ((), (), s32[]{:S(2)}) async-start(), calls=%async_computation | async-start | bytes 7077888 | tf_op jit(solution)/shard_map/all_gather | solution.py:1092
  246.6 6.0 collective-permute-start
  262.7 8.7 %collective-permute-start.2 = (bf16[2,4,128,128]{3,2,1,0:T(8,128)(2,1)}, bf16[2,4,128,128]{3,2,1,0:T(8,128)(2,1)S(1)}, u32[]{:S(2)}, u32[]{:S(2)}) collective-permute-start(bf16[2,4,128,128]{3,2,1,0:T(8,128)(2,1)} %get-tuple-element.79), channel_id=1, source_target_pairs={{0,2},{1,3},{2,0},{3,1},{4,6},{5,7},{6,4},{7,5},{8,10},{9,11},{10,... | collective-permute-start | bytes 786440 | tf_op jit(solution)/shard_map/ppermute | solution.py:40
  265.4 10.3 %collective-permute-start.1 = (bf16[2,4,128,128]{3,2,1,0:T(8,128)(2,1)}, bf16[2,4,128,128]{3,2,1,0:T(8,128)(2,1)S(1)}, u32[]{:S(2)}, u32[]{:S(2)}) collective-permute-start(bf16[2,4,128,128]{3,2,1,0:T(8,128)(2,1)} %get-tuple-element.79), channel_id=1, source_target_pairs={{0,4},{4,0},{1,5},{5,1},{2,6},{6,2},{3,7},{7,3},{8,12},{12,8},{9,1... | collective-permute-start | bytes 786440 | tf_op jit(solution)/shard_map/ppermute | solution.py:25
  271.5 8.0 %collective-permute-start.3 = (bf16[2,4,128,128]{3,2,1,0:T(8,128)(2,1)S(1)}, bf16[2,4,128,128]{3,2,1,0:T(8,128)(2,1)S(1)}, u32[]{:S(2)}, u32[]{:S(2)}) collective-permute-start(bf16[2,4,128,128]{3,2,1,0:T(8,128)(2,1)S(1)} %collective-permute-done.2), channel_id=1, source_target_pairs={{0,4},{4,0},{1,5},{5,1},{2,6},{6,2},{3,7},{7,3},{8,12},{12,8},{9,1... | collective-permute-start | bytes 786440 | tf_op jit(solution)/shard_map/ppermute | solution.py:25
  312.9 4.6 collective-permute-start.4
  324.6 4.5 collective-permute-start.5
  324.8 57.1 %collective-permute-start.6 = (bf16[512,2048]{1,0:T(8,128)(2,1)}, bf16[512,2048]{1,0:T(8,128)(2,1)S(1)}, u32[]{:S(2)}, u32[]{:S(2)}) collective-permute-start(bf16[512,2048]{1,0:T(8,128)(2,1)} %get-tuple-element.86.refs_1_), channel_id=1, source_target_pairs={{0,2},{1,3},{2,0},{3,1},{4,6},{5,7},{6,4},{7,5},{8,10},{9,11},{10,... | collective-permute-start | bytes 6291464 | tf_op jit(solution)/shard_map/ppermute | solution.py:40
  469.6 5.1 collective-permute-start.8
  469.9 63.8 %collective-permute-start.10 = (bf16[512,2048]{1,0:T(8,128)(2,1)}, bf16[512,2048]{1,0:T(8,128)(2,1)}, u32[]{:S(2)}, u32[]{:S(2)}) collective-permute-start(bf16[512,2048]{1,0:T(8,128)(2,1)} %get-tuple-element.103), channel_id=1, source_target_pairs={{0,1},{1,0},{2,3},{3,2},{4,5},{5,4},{6,7},{7,6},{8,9},{9,8},{10,11... | collective-permute-start | bytes 6291464 | tf_op jit(solution)/shard_map/ppermute | solution.py:29
  477.1 48.0 %collective-permute-start.16 = (bf16[512,2048]{1,0:T(8,128)(2,1)S(1)}, bf16[512,2048]{1,0:T(8,128)(2,1)}, u32[]{:S(2)}, u32[]{:S(2)}) collective-permute-start(bf16[512,2048]{1,0:T(8,128)(2,1)S(1)} %add_convert_fusion.1.refs_9_), channel_id=1, source_target_pairs={{0,2},{1,3},{2,0},{3,1},{4,6},{5,7},{6,4},{7,5},{8,10},{9,11},{10,... | collective-permute-start | bytes 6291464 | tf_op jit(solution)/shard_map/ppermute | solution.py:40
  533.6 5.7 collective-permute-start.17
  537.6 92.0 %collective-permute-start.11 = (bf16[512,2048]{1,0:T(8,128)(2,1)}, bf16[512,2048]{1,0:T(8,128)(2,1)S(1)}, u32[]{:S(2)}, u32[]{:S(2)}) collective-permute-start(bf16[512,2048]{1,0:T(8,128)(2,1)} %add_convert_fusion.refs_11_), channel_id=1, source_target_pairs={{0,2},{1,3},{2,0},{3,1},{4,6},{5,7},{6,4},{7,5},{8,10},{9,11},{10,... | collective-permute-start | bytes 6291464 | tf_op jit(solution)/shard_map/ppermute | solution.py:40
  612.2 8.7 %collective-permute-start.19 = (bf16[2,4,128,128]{3,2,1,0:T(8,128)(2,1)}, bf16[2,4,128,128]{3,2,1,0:T(8,128)(2,1)S(1)}, u32[]{:S(2)}, u32[]{:S(2)}) collective-permute-start(bf16[2,4,128,128]{3,2,1,0:T(8,128)(2,1)} %get-tuple-element.110), channel_id=1, source_target_pairs={{0,2},{1,3},{2,0},{3,1},{4,6},{5,7},{6,4},{7,5},{8,10},{9,11},{10,... | collective-permute-start | bytes 786440 | tf_op jit(solution)/shard_map/ppermute | solution.py:40
  612.9 10.8 %collective-permute-start.18 = (bf16[2,4,128,128]{3,2,1,0:T(8,128)(2,1)}, bf16[2,4,128,128]{3,2,1,0:T(8,128)(2,1)S(1)}, u32[]{:S(2)}, u32[]{:S(2)}) collective-permute-start(bf16[2,4,128,128]{3,2,1,0:T(8,128)(2,1)} %get-tuple-element.110), channel_id=1, source_target_pairs={{0,4},{4,0},{1,5},{5,1},{2,6},{6,2},{3,7},{7,3},{8,12},{12,8},{9,1... | collective-permute-start | bytes 786440 | tf_op jit(solution)/shard_map/ppermute | solution.py:25
  620.9 7.6 %collective-permute-start.20 = (bf16[2,4,128,128]{3,2,1,0:T(8,128)(2,1)S(1)}, bf16[2,4,128,128]{3,2,1,0:T(8,128)(2,1)S(1)}, u32[]{:S(2)}, u32[]{:S(2)}) collective-permute-start(bf16[2,4,128,128]{3,2,1,0:T(8,128)(2,1)S(1)} %collective-permute-done.19), channel_id=1, source_target_pairs={{0,4},{4,0},{1,5},{5,1},{2,6},{6,2},{3,7},{7,3},{8,12},{12,8},{9,1... | collective-permute-start | bytes 786440 | tf_op jit(solution)/shard_map/ppermute | solution.py:25
  622.6 51.9 %collective-permute-start.9 = (bf16[512,2048]{1,0:T(8,128)(2,1)}, bf16[512,2048]{1,0:T(8,128)(2,1)}, u32[]{:S(2)}, u32[]{:S(2)}) collective-permute-start(bf16[512,2048]{1,0:T(8,128)(2,1)} %get-tuple-element.101), channel_id=1, source_target_pairs={{0,1},{1,0},{2,3},{3,2},{4,5},{5,4},{6,7},{7,6},{8,9},{9,8},{10,11... | collective-permute-start | bytes 6291464 | tf_op jit(solution)/shard_map/ppermute | solution.py:29
  640.0 7.1 collective-permute-start.21
  662.7 22.4 %collective-permute-start.22 = (bf16[2,256,2176]{2,1,0:T(8,128)(2,1)}, bf16[2,256,2176]{2,1,0:T(8,128)(2,1)}, u32[]{:S(2)}, u32[]{:S(2)}) collective-permute-start(bf16[2,256,2176]{2,1,0:T(8,128)(2,1)} %get-tuple-element.117), channel_id=1, source_target_pairs={{0,1},{1,0},{2,3},{3,2},{4,5},{5,4},{6,7},{7,6},{8,9},{9,8},{10,11... | collective-permute-start | bytes 6684680 | tf_op jit(solution)/shard_map/ppermute | solution.py:29
  662.9 5.3 collective-permute-start.30
  668.2 4.7 collective-permute-start.31
  673.0 7.2 %collective-permute-start.32 = (bf16[400,128]{1,0:T(8,128)(2,1)S(1)}, bf16[400,128]{1,0:T(8,128)(2,1)S(1)}, u32[]{:S(2)}, u32[]{:S(2)}) collective-permute-start(bf16[400,128]{1,0:T(8,128)(2,1)S(1)} %add_convert_fusion.3), channel_id=1, source_target_pairs={{0,8},{8,0},{16,24},{24,16},{1,9},{9,1},{17,25},{25,17},{2,10},{10... | collective-permute-start | bytes 307208 | tf_op jit(solution)/shard_map/ppermute | solution.py:118
  680.3 17.2 %collective-permute-start.33 = (bf16[400,128]{1,0:T(8,128)(2,1)S(1)}, bf16[400,128]{1,0:T(8,128)(2,1)S(1)}, u32[]{:S(2)}, u32[]{:S(2)}) collective-permute-start(bf16[400,128]{1,0:T(8,128)(2,1)S(1)} %add_convert_fusion.2), channel_id=1, source_target_pairs={{0,16},{8,24},{16,0},{24,8},{1,17},{9,25},{17,1},{25,9},{2,18},{10... | collective-permute-start | bytes 307208 | tf_op jit(solution)/shard_map/ppermute | solution.py:118
  694.1 5.2 collective-permute-start.23
  694.2 6.4 collective-permute-start.24
  696.0 6.0 collective-permute-start.25
  702.0 4.7 collective-permute-start.26
  706.8 6.2 collective-permute-start.27
  706.8 6.1 collective-permute-start.28
  706.9 6.0 collective-permute-start.29
  (42 other events, 799.6 us)
Sparse Core Ops, SparseCore 0:
  11.5 171.9 all-gather.5
  185.7 101.0 all-gather.7
  289.0 99.0 all-gather.3

commit v3 on v2

--- a/solution.py
+++ b/solution.py
@@ -10,7 +10,7 @@
 HD = 64
 RANK = 8
 WIN = 64
-FF_CHUNKS = 4
+FF_CHUNKS = (1, 2, 3, 2)
 
 NORM_EPS = 1e-05
 ADAPTER_SCALE = 2.0
@@ -294,11 +294,10 @@
 def ffn_kernel(chunks, before, share_len, slots, live_ref, x_ref, more_ref, cot_ref, *refs):
     weights, refs = refs[:chunks], refs[chunks:]
     earlier, refs = refs[: 4 * before], refs[4 * before :]
-    outs, (held, sem) = refs[:4], refs[4:]
+    outs, held, sem = refs[:4], refs[4:-1], refs[-1]
     step = pl.program_id(0)
     tile = x_ref.shape[0]
-    width = held.shape[2] // 3
-    copies = [pltpu.make_async_copy(weights[c], held.at[c], sem.at[c]) for c in range(chunks)]
+    copies = [pltpu.make_async_copy(weights[c], held[c], sem.at[c]) for c in range(chunks)]
 
     @pl.when(step == 0)
     def _():
@@ -317,17 +316,18 @@
         def _():
             copies[c].wait()
 
-        gate = dot(x, held[c, :, :width])
-        up = dot(x, held[c, :, width : 2 * width])
-        gm = dot(cot, held[c, :, 2 * width :]) * live
+        w, width = held[c], held[c].shape[1] // 3
+        gate = dot(x, w[:, :width])
+        up = dot(x, w[:, width : 2 * width])
+        gm = dot(cot, w[:, 2 * width :]) * live
         sig = jax.nn.sigmoid(gate)
         silu = gate * sig
         mixed = (silu * up).astype(BF16)
         g_gate = (gm * up * (sig + silu * (1.0 - sig))).astype(BF16)
         g_up = (gm * silu).astype(BF16)
         parts = (
-            dot(jnp.concatenate([g_gate, g_up], axis=1), held[c, :, : 2 * width], NT),
-            dot(mixed, held[c, :, 2 * width :], NT),
+            dot(jnp.concatenate([g_gate, g_up], axis=1), w[:, : 2 * width], NT),
+            dot(mixed, w[:, 2 * width :], NT),
         )
         sums = [p if t is None else t + p for t, p in zip(sums, parts)]
 
@@ -345,7 +345,7 @@
 def ffn(x, cot, weights, live_rows, share_len, slots, before=(), after=()):
     tokens, depth = cot.shape
     chunks = len(weights)
-    width = weights[0].shape[1] // 3
+    units = sum(w.shape[1] for w in weights) // 3
     tile = min(256, share_len)
     half = tokens // tile // 2
     lower = pl.BlockSpec((tile, depth), lambda i, *_: (jnp.minimum(i, half - 1), 0))
@@ -363,12 +363,12 @@
         out_specs=[lower, upper, lower, upper],
         out_shape=[out] * 4,
         scratch=[
-            pltpu.VMEM((chunks, depth, 3 * width), BF16),
+            *[pltpu.VMEM(w.shape, BF16) for w in weights],
             pltpu.SemaphoreType.DMA((chunks,)),
         ],
         cost=pl.CostEstimate(
-            flops=12 * tokens * depth * width * chunks,
-            bytes_accessed=8 * tokens * depth + 6 * depth * width * chunks,
+            flops=12 * tokens * depth * units,
+            bytes_accessed=8 * tokens * depth + 6 * depth * units,
             transcendentals=0,
         ),
         name="ffn",
@@ -495,15 +495,33 @@
             window, linear, valid)
 
 
+def query_feature_kernel(q_ref, feat_ref, phi_ref):
+    for h in range(q_ref.shape[1]):
+        phi_ref[0, h] = features(q_ref[0, h], feat_ref[h]).astype(BF16)
+
+
+def query_features(q, feat, groups):
+    slots, all_heads, length, _ = q.shape
+    sp = attention_specs(slots, groups, all_heads // groups, length)
+    return kernel_call(
+        query_feature_kernel,
+        [q, feat],
+        (),
+        grid=(slots, groups),
+        in_specs=[sp["q"], sp["feat"]],
+        out_specs=sp["phiq"],
+        out_shape=jax.ShapeDtypeStruct((slots, all_heads, length, 2 * HD), BF16),
+        name="query_features",
+    )
+
+
 def attend_kernel(
-    ends_ref, q_ref, kv_ref, phi_ref, feat_ref, carry_ref, qdoc_ref, kdoc_ref, pdoc_ref,
-    attn_ref, phiq_ref, vx_ref,
+    ends_ref, q_ref, kv_ref, phi_ref, phiq_ref, carry_ref, qdoc_ref, kdoc_ref, pdoc_ref,
+    attn_ref, vx_ref,
 ):
     r = pl.program_id(0)
     heads, length = q_ref.shape[1], q_ref.shape[2]
     vx_ref[...] = values_ones(kv_ref[0, 0])
-    for h in range(heads):
-        phiq_ref[0, h] = features(q_ref[0, h], feat_ref[h]).astype(BF16)
     state = carry_ref[0, 0]
     for b in range(length // WIN):
         if b:
@@ -539,24 +557,21 @@
     )
 
 
-def attend(ends, q, kv, phi, feat, carry, qdoc, kdoc, pdoc, after=()):
+def attend(ends, q, kv, phi, phiq, carry, qdoc, kdoc, pdoc, after=()):
     slots, all_heads, length, _ = q.shape
     groups = kv.shape[1]
     heads = all_heads // groups
     sp = attention_specs(slots, groups, heads, length)
     return kernel_call(
         attend_kernel,
-        [ends, q, kv, phi, feat, carry, qdoc, kdoc, pdoc],
+        [ends, q, kv, phi, phiq, carry, qdoc, kdoc, pdoc],
         after,
         prefetch=1,
         grid=(slots, groups),
-        in_specs=[sp[n] for n in ("q", "kv", "kv", "feat", "state", "qdoc", "kdoc", "pdoc")],
-        out_specs=[sp["tokens"], sp["phiq"]],
+        in_specs=[sp[n] for n in ("q", "kv", "kv", "phiq", "state", "qdoc", "kdoc", "pdoc")],
+        out_specs=sp["tokens"],
         scratch=[pltpu.VMEM((length + WIN, 2 * HD), BF16)],
-        out_shape=[
-            jax.ShapeDtypeStruct((slots, length, all_heads * HD), BF16),
-            jax.ShapeDtypeStruct((slots, all_heads, length, 2 * HD), BF16),
-        ],
+        out_shape=jax.ShapeDtypeStruct((slots, length, all_heads * HD), BF16),
         name="attend",
     )
 
@@ -858,9 +873,9 @@
     normed_ref[...] = normalize(mid, gain_ref[...])
 
 
-def tokens_call(kernel, tiled, whole, outs, name, prefetch=(), sums=()):
+def tokens_call(kernel, tiled, whole, outs, name, prefetch=(), sums=(), tile=256, after=()):
     tokens = tiled[0].shape[0]
-    tile = min(256, tokens)
+    tile = min(tile, tokens)
     rows = lambda v: pl.BlockSpec((tile, v.shape[1]), lambda i, *_: (i, 0))
     full = lambda v: pl.BlockSpec(v.shape, lambda i, *_: (0, 0))
     shapes = [jax.ShapeDtypeStruct((tokens, width), kind) for width, kind in outs]
@@ -868,7 +883,7 @@
     return kernel_call(
         kernel,
         [*prefetch, *tiled, *whole],
-        (),
+        after,
         prefetch=len(prefetch),
         grid=(tokens // tile,),
         in_specs=[rows(v) for v in tiled] + [full(v) for v in whole],
@@ -883,6 +898,10 @@
     scaled = gain * grad
     shared = scale * scale * scale * jnp.mean(values * scaled, axis=-1, keepdims=True)
     return scale, scale * scaled - values * shared
+
+
+def pair_kernel(a_ref, b_ref, out_ref):
+    out_ref[...] = a_ref[...] + b_ref[...].astype(F32)
 
 
 def sum_kernel(*refs):
@@ -1026,6 +1045,107 @@
         sum_ref[...] = jnp.zeros_like(sum_ref)
 
     sum_ref[...] += dot(low, (values * scale * gain).astype(BF16), TN)
+
+
+def sums_kernel(rows, seqs, heads, part_ref, pack_ref, out_ref, cols_ref, *scratch):
+    a1, a2, a3, c2, c3, b1, b2, b3, e2, e3, send_sem, recv_sem = scratch
+    place = {a: lax.axis_index(a) for a in ("row", "seq", "head")}
+    counts = {"row": rows, "seq": seqs, "head": heads}
+    x_place = place["head"] // 2
+    peers = [
+        (a, {a: lax.rem(place[a] + d, counts[a])}) for a in counts for d in range(1, counts[a])
+    ]
+    barrier = pltpu.get_barrier_semaphore()
+    for _, peer in peers:
+        pl.semaphore_signal(barrier, inc=1, device_id=peer, device_id_type=pl.DeviceIdType.MESH)
+    pl.semaphore_wait(barrier, len(peers))
+    used = [0]
+
+    def remote(src, dst, device):
+        n = used[0]
+        used[0] += 1
+        return pltpu.make_async_remote_copy(
+            src_ref=src, dst_ref=dst, send_sem=send_sem.at[n], recv_sem=recv_sem.at[n],
+            device_id=device, device_id_type=pl.DeviceIdType.MESH,
+        )
+
+    def exchange(axis, parts, slots, packs, pack_slots):
+        me, size = place[axis], counts[axis]
+        copies = []
+        for d in range(1, size):
+            to = lax.rem(me + d, size)
+            copies.append(remote(parts.at[to], slots.at[me], {axis: to}))
+            if pack_slots is not None:
+                copies.append(remote(packs, pack_slots.at[me], {axis: to}))
+        return copies
+
+    def add_up(ref, size):
+        total = ref[0].astype(F32)
+        for i in range(1, size):
+            total = total + ref[i].astype(F32)
+        return total
+
+    b1[0] = pack_ref[1 - x_place].astype(BF16)
+    copies = exchange("head", part_ref, a1, None, None)
+    copies.append(remote(b1.at[0], b1.at[1], {"head": lax.rem(place["head"] + 2, heads)}))
+    for copy in copies:
+        copy.start()
+    a1[place["head"]] = part_ref[place["head"]]
+    for copy in copies:
+        copy.wait()
+    stages = (
+        ("seq", add_up(a1, heads), pack_ref[x_place] + b1[1].astype(F32), c2, a2, e2, b2),
+        ("row", None, None, c3, a3, e3, b3),
+    )
+    for axis, part, pack, held, slots, pack_held, pack_slots in stages:
+        if part is None:
+            part, pack = add_up(a2, seqs), add_up(b2, seqs)
+        held[...] = part
+        pack_held[...] = pack.astype(BF16)
+        copies = exchange(axis, held, slots, pack_held, pack_slots)
+        for copy in copies:
+            copy.start()
+        slots[place[axis]] = held[place[axis]]
+        pack_slots[place[axis]] = pack_held[...]
+        for copy in copies:
+            copy.wait()
+    out_ref[...] = add_up(a3, rows)
+    cols_ref[...] = add_up(b3, rows)
+
+
+def final_sums(part, pack):
+    rows, seqs, heads = (lax.axis_size(a) for a in ("row", "seq", "head"))
+    low, width = part.shape[3:]
+    count, lanes = pack.shape[1:]
+    place = pl.BlockSpec(memory_space=pltpu.VMEM)
+    copies = heads + 2 * (seqs - 1) + 2 * (rows - 1)
+    return pl.pallas_call(
+        functools.partial(sums_kernel, rows, seqs, heads),
+        in_specs=[place, place],
+        out_specs=[place, place],
+        out_shape=[
+            jax.ShapeDtypeStruct((low, width), F32),
+            jax.ShapeDtypeStruct((count, lanes), F32),
+        ],
+        scratch_shapes=[
+            pltpu.VMEM((heads, seqs, rows, low, width), F32),
+            pltpu.VMEM((seqs, rows, low, width), F32),
+            pltpu.VMEM((rows, low, width), F32),
+            pltpu.VMEM((seqs, rows, low, width), F32),
+            pltpu.VMEM((rows, low, width), F32),
+            pltpu.VMEM((2, count, lanes), BF16),
+            pltpu.VMEM((seqs, count, lanes), BF16),
+            pltpu.VMEM((rows, count, lanes), BF16),
+            pltpu.VMEM((count, lanes), BF16),
+            pltpu.VMEM((count, lanes), BF16),
+            pltpu.SemaphoreType.DMA((copies,)),
+            pltpu.SemaphoreType.DMA((copies,)),
+        ],
+        compiler_params=pltpu.CompilerParams(
+            collective_id=1, has_side_effects=True, vmem_limit_bytes=32 * 2**20
+        ),
+        name="final_sums",
+    )(part, pack)
 
 
 def local(
@@ -1081,12 +1201,11 @@
     qkv_shard = jnp.concatenate([query_weight, key_weight, value_weight], axis=1)
     out_shard = out_weight.T
     down_shard = down_weight.T
-    chunk = ff_cols // FF_CHUNKS
+    unit = ff_cols // sum(FF_CHUNKS)
+    bounds = [unit * sum(FF_CHUNKS[:j]) for j in range(len(FF_CHUNKS) + 1)]
     ffn_shards = [
-        jnp.concatenate(
-            [w[:, j * chunk : (j + 1) * chunk] for w in (gate_weight, up_weight, down_shard)], axis=1
-        )
-        for j in range(FF_CHUNKS)
+        jnp.concatenate([w[:, lo:hi] for w in (gate_weight, up_weight, down_shard)], axis=1)
+        for lo, hi in zip(bounds[:-1], bounds[1:])
     ]
     ffn_later = [
         lax.all_gather(v, ("row", "seq"), axis=0, tiled=True) for v in ffn_shards[1:]
@@ -1196,8 +1315,9 @@
         after = lax.dynamic_index_in_dim(piece_docs, source + 1, 1, keepdims=False)
         keep = (source < piece) & (after == carry_doc)
         carry = carry + jnp.where(keep[:, None, None, None], part.astype(F32), 0.0)
-    attn, phi_query = attend(
-        end_docs, query, kv, phi_key, query_feat, carry, query_doc_lanes, key_doc_lanes, pair_docs
+    phi_query = query_features(query, query_feat, kv.shape[1])
+    attn = attend(
+        end_docs, query, kv, phi_key, phi_query, carry, query_doc_lanes, key_doc_lanes, pair_docs
     )
 
     keep, away = out_project(core_index, attn, out_mat, o_in, share_len)
@@ -1222,14 +1342,14 @@
     run = lambda x, c, w, before=(), after=(): ffn(
         x, c, w, live_rows, share_len, slots, before, after
     )
-    mine = run(x_mine, c_mine, ffn_mats[:-1])
+    mine = run(x_mine, c_mine, ffn_mats[:2])
     x_away = chip_tokens(hold(nmid_x, (mine[0],)))
     away = run(x_away, c_away, ffn_mats[:-1])
     away = run(x_away, c_away, ffn_mats[-1:], away)
     gn_there = sum_away(*away[:2])
     gn_back = flip_x(gn_there)
     gn_own, gn_other, y_own, y_other = run(
-        x_mine, c_mine, ffn_mats[-1:], mine, (gn_there,)
+        x_mine, c_mine, ffn_mats[2:], mine, (gn_there,)
     )
     y_there = sum_away(*away[2:])
     y_back = flip_x(y_there)
@@ -1254,15 +1374,16 @@
         pair_docs, grad_attn, (y_there,),
     )
     block_out = tokens_call(
-        sum_kernel, [mid_rows, y_own, flip_core(y_other), y_back], [], [(model_dim, BF16)], "sum_y"
-    )[0].reshape(hidden_in.shape)
+        sum_kernel, [mid_rows, y_own, flip_core(y_other), y_back], [], [(model_dim, BF16)], "sum_y",
+        after=(grad_carry,),
+    )[0]
     later = jnp.zeros(grad_carry.shape, F32)
     for source, part in from_pieces(grad_carry):
         start = lax.dynamic_index_in_dim(piece_docs, source, 1, keepdims=False)
         keep = (source > piece) & (start == next_doc)
         later = later + jnp.where(keep[:, None, None, None], part.astype(F32), 0.0)
     grad_body, grad_edge, feat_key = key_back(
-        end_docs, kv, phi_key, key_feat, later, key_doc_lanes, gphi, gkv, (y_back,)
+        end_docs, kv, phi_key, key_feat, later, key_doc_lanes, gphi, gkv, (block_out,)
     )
     sum_q_feat = jnp.sum(feat_query, axis=0).reshape(2, -1, 2 * HD)
     sum_k_feat = jnp.sum(feat_key, axis=0).reshape(2, -1, 2 * HD)
@@ -1291,9 +1412,6 @@
     by_rows = jnp.concatenate([sum_in, sum_o_out], axis=0)
     width = model_dim // (rows * seqs * heads)
     by_rows = by_rows.reshape(4 * RANK, rows, seqs, heads, width).transpose(3, 2, 1, 0, 4)
-    for axis in ("head", "seq", "row"):
-        by_rows = scatter_sum(by_rows, axis)
-    in_parts = by_rows.reshape(4, RANK, width)
 
     def lanes_of(v):
         v = v.reshape(2, RANK, -1, 2 * HD).transpose(0, 2, 1, 3)
@@ -1303,11 +1421,8 @@
     packed = [lanes_of(v) for v in outs + [o_sets]] + [sum_q_feat, sum_k_feat]
     sizes = [v.shape[1] for v in packed]
     packed = jnp.concatenate(packed, axis=1)
-    kept = lax.dynamic_index_in_dim(packed, x_place, 0, keepdims=False)
-    sent = lax.dynamic_index_in_dim(packed, 1 - x_place, 0, keepdims=False)
-    packed = kept + flip_x(sent.astype(BF16)).astype(F32)
-    for axis in ("seq", "row"):
-        packed = full_sum(packed, axis)
+    in_parts, packed = final_sums(by_rows, packed)
+    in_parts = in_parts.reshape(4, RANK, width)
     cols, at = [], 0
     for size in sizes:
         cols.append(packed[at : at + size])
@@ -1318,7 +1433,7 @@
     cols[3] = cols[3].T
 
     return (
-        block_out,
+        block_out.reshape(hidden_in.shape),
         grad_hidden,
         in_parts[0].T,
         cols[0],

time: 725 us -> 715 us (0.986)
  Pallas kernels: 546 us -> 567 us
  waiting for transfers between devices: 69.2 us -> 53.2 us
  starting transfers between devices: 37.2 us -> 22.8 us
    pallas_call x0 -> x1, Pallas kernels: none -> 25.3 us  [final_sums(): pl.pallas_call(functools.partial(sums_kernel, rows, seqs, heads), in_spec...]
    pallas_call x1, Pallas kernels: 207 us -> 191 us  [gather(): pl.pallas_call(functools.partial(gather_kernel, plan, rows, seqs, parts,...]
    pallas_call x17 -> x18, Pallas kernels: 339 us -> 351 us  [kernel_call(): pl.pallas_call(body, grid_spec=pltpu.PrefetchScalarGridSpec(num_scalar_pr...]
    ppermute x11 -> x4, waiting for transfers between devices: 16.7 us -> 6.04 us  [shift(): lax.ppermute(block, axis, [(i, (i + distance) % size) for i in range(size)])]
    ppermute x6 -> x5, waiting for transfers between devices: 27.3 us -> 19.7 us  [flip_x(): lax.ppermute(block, 'head', [(i, i ^ 2) for i in range(lax.axis_size('hea...]
    ppermute x3 -> x0, starting transfers between devices: 7.53 us -> none  [full_sum(): got = lax.ppermute(sent, axis, [(i, i ^ step) for i in range(size)])]
    ppermute x11 -> x4, starting transfers between devices: 15.3 us -> 8.75 us  [shift(): lax.ppermute(block, axis, [(i, (i + distance) % size) for i in range(size)])]
  transfers between devices with their start and end apart: 37 -> 26, of which waited for: 20 -> 15; matrix products, arithmetic and copies ran while one was open for 6% -> 5% of each run, Pallas kernels for 72% -> 69%
where the time goes in v3:
time: 715 us; the launch traced here: 710 us
  Pallas kernels  567 us (79%)
  waiting for transfers between devices  53.2 us (7%)
  local copies, waits for them, and re-layouts  26.3 us (4%)
  other arithmetic  24.5 us (3%)
  starting transfers between devices  22.8 us (3%)
  between operations  15.6 us (2%)
    pallas_call x18, Pallas kernels, kernel_call(): pl.pallas_call(body, grid_spec=pltpu.PrefetchScalarGridSpec(num_scalar_pr...  351 us
    pallas_call x1, Pallas kernels, gather(): pl.pallas_call(functools.partial(gather_kernel, plan, rows, seqs, parts,...  191 us
    pallas_call x1, Pallas kernels, final_sums(): pl.pallas_call(functools.partial(sums_kernel, rows, seqs, heads), in_spec...  25.3 us
    ppermute x12, waiting for transfers between devices, flip_core(): lax.ppermute(block, 'head', [(i, i ^ 1) for i in range(lax.axis_size('hea...  21.5 us
    ppermute x5, waiting for transfers between devices, flip_x(): lax.ppermute(block, 'head', [(i, i ^ 2) for i in range(lax.axis_size('hea...  19.7 us
  transfers between devices with their start and end apart: 26, of which 15 were waited for; matrix products, arithmetic and copies ran while one was open for 5% of the time, Pallas kernels for 69%

profile of v3, /device:TPU:0, one launch (start us, length us, event | category | flops | bytes accessed | tf_op | source)
XLA Modules:
  0.0 710.1 jit_solution(4438258227057023915)
XLA Ops:
  21.1 191.1 %gather.1 = (bf16[2,2048,768]{2,1,0:T(8,128)(2,1)}, bf16[2,2048,512]{2,1,0:T(8,128)(2,1)}, bf16[2048,768]{1,0:T(8,128)(2,1)}, bf16[8,64,64]{2,1,0:T(8,128)(2,1)}...) custom-call(bf16[256,768]{1,0:T(8,128)(2,1)} %pad_maximum_fusion.4.r, ...), custom_call_target="tpu_custom_call" | custom-call | tf_op jit(solution)/shard_map/gather/pallas_call | solution.py:275
  217.1 16.8 %project.1 = (bf16[2,16,512,64]{3,2,1,0:T(8,128)(2,1)}, bf16[2,4,512,128]{3,2,1,0:T(8,128)(2,1)}, bf16[2,512,128]{2,1,0:T(8,128)(2,1)}) custom-call(s32[1]{0:T(128)} %bitcast.1.refs_0_, bf16[2,256,2048]{2,1,0:T(8,128)(2,1)} %refs_1_.1, bf16[2,256,2048]{2,1,0:T(8,128)(2,1)} %get-tuple-element.69.refs_2_, f32[1,2048]{1,0:T(1,128)} %bitcast.106, ...), custom_call_target="tpu_custom_call" | custom-call | flops 1610612736 | bytes 2621440 | tf_op jit(solution)/shard_map/project/pallas_call | solution.py:51
  235.0 3.9 collective-permute-start
  244.0 8.7 %key_state.1 = (bf16[2,4,576,128]{3,2,1,0:T(8,128)(2,1)}, bf16[2,4,128,128]{3,2,1,0:T(8,128)(2,1)}) custom-call(s32[2,9]{1,0:T(2,128)} %bitcast.112, bf16[2,4,576,128]{3,2,1,0:T(8,128)(2,1)} %copy-done, bf16[4,64,128]{2,1,0:T(8,128)(2,1)} %pad_maximum_fusion.8.refs_2_.refs_3_, s32[2,576,128]{2,1,0:T(8,128)} %broadcast_in_dim.69.refs_3_.refs_7_.refs_8_.refs_5_), custom_call_target="tpu_custom_call" | custom-call | tf_op jit(solution)/shard_map/key_state/pallas_call | solution.py:51
  256.8 4.5 collective-permute-done.2
  261.4 2.6 collective-permute-start.3
  264.2 10.2 %query_features.1.refs_4_ = bf16[2,16,512,128]{3,2,1,0:T(8,128)(2,1)} custom-call(bf16[2,16,512,64]{3,2,1,0:T(8,128)(2,1)} %get-tuple-element.74.refs_0_.refs_1_, bf16[16,64,128]{2,1,0:T(8,128)(2,1)} %pad_maximum_fusion.6.refs_1_.refs_5_), custom_call_target="tpu_custom_call" | custom-call | tf_op jit(solution)/shard_map/query_features/pallas_call | solution.py:51
  275.5 5.7 collective-permute-done.3
  283.2 16.2 %attend.1.refs_1_.refs_2_.refs_3_ = bf16[2,512,1024]{2,1,0:T(8,128)(2,1)} custom-call(s32[2,9]{1,0:T(2,128)} %bitcast.113, bf16[2,16,512,64]{3,2,1,0:T(8,128)(2,1)} %get-tuple-element.74.refs_0_.refs_1_, bf16[2,4,576,128]{3,2,1,0:T(8,128)(2,1)} %copy-done, bf16[2,4,576,128]{3,2,1,0:T(8,128)(2,1)} %get-tuple-element.77.refs_3_.refs_2_, ...), custom_call_target="tpu_custom_call" | custom-call | tf_op jit(solution)/shard_map/attend/pallas_call | solution.py:51
  299.3 9.0 %out_project.1 = (bf16[2,256,2176]{2,1,0:T(8,128)(2,1)}, bf16[2,256,2176]{2,1,0:T(8,128)(2,1)}) custom-call(s32[1]{0:T(128)} %bitcast.1.refs_0_, bf16[2,512,1024]{2,1,0:T(8,128)(2,1)} %attend.1.refs_1_.refs_2_.refs_3_, bf16[2,512,1024]{2,1,0:T(8,128)(2,1)} %attend.1.refs_1_.refs_2_.refs_3_, bf16[2,2048,512]{2,1,0:T(8,128)(2,1)} %get-tuple-element.80.refs_3_.refs_4_, ...), custom_call_target="tpu_custom_call" | custom-call | tf_op jit(solution)/shard_map/out_project/pallas_call | solution.py:51
  309.8 3.1 collective-permute-done.4
  314.2 5.8 middle.1
  325.7 33.0 %ffn.4 = (bf16[512,2048]{1,0:T(8,128)(2,1)}, bf16[512,2048]{1,0:T(8,128)(2,1)}, bf16[512,2048]{1,0:T(8,128)(2,1)}, bf16[512,2048]{1,0:T(8,128)(2,1)}) custom-call(s32[1]{0:T(128)S(6)} %copy.99.refs_0_, bf16[512,2048]{1,0:T(8,128)(2,1)} %get-tuple-element.85.refs_1_, bf16[512,2048]{1,0:T(8,128)(2,1)} %copy-done.5, bf16[1024,2048]{1,0:T(8,128)(2,1)} %bitcast.88, ...), custom_call_target="tpu_custom_call" | custom-call | flops 4831838208 | bytes 6553600 | tf_op jit(solution)/shard_map/ffn/pallas_call | solution.py:51
  358.7 9.7 %collective-permute-done.6.refs_0_ = bf16[512,2048]{1,0:T(8,128)(2,1)} collective-permute-done((bf16[512,2048]{1,0:T(8,128)(2,1)}, bf16[512,2048]{1,0:T(8,128)(2,1)}, u32[]{:S(2)}, u32[]{:S(2)}) %collective-permute-start.6) | collective-permute-done | bytes 2097184 | tf_op jit(solution)/shard_map/ppermute | solution.py:40
  368.4 2.7 hold.1.refs_1_
  371.1 4.4 collective-permute-done.7.refs_2_
  376.8 56.8 %ffn.5 = (bf16[512,2048]{1,0:T(8,128)(2,1)}, bf16[512,2048]{1,0:T(8,128)(2,1)}, bf16[512,2048]{1,0:T(8,128)(2,1)}, bf16[512,2048]{1,0:T(8,128)(2,1)}) custom-call(s32[1]{0:T(128)S(6)} %copy.99.refs_0_, bf16[512,2048]{1,0:T(8,128)(2,1)} %hold.1.refs_1_, bf16[512,2048]{1,0:T(8,128)(2,1)} %copy-done.6, bf16[1024,2048]{1,0:T(8,128)(2,1)} %bitcast.90, ...), custom_call_target="tpu_custom_call" | custom-call | flops 9663676416 | bytes 8912896 | tf_op jit(solution)/shard_map/ffn/pallas_call | solution.py:51
  433.6 25.5 %ffn.6 = (bf16[512,2048]{1,0:T(8,128)(2,1)}, bf16[512,2048]{1,0:T(8,128)(2,1)}, bf16[512,2048]{1,0:T(8,128)(2,1)}, bf16[512,2048]{1,0:T(8,128)(2,1)}) custom-call(s32[1]{0:T(128)S(6)} %copy.99.refs_0_, bf16[512,2048]{1,0:T(8,128)(2,1)} %hold.1.refs_1_, bf16[512,2048]{1,0:T(8,128)(2,1)} %copy-done.6, bf16[1024,2048]{1,0:T(8,128)(2,1)} %bitcast.91, ...), custom_call_target="tpu_custom_call" | custom-call | flops 3221225472 | bytes 5767168 | tf_op jit(solution)/shard_map/ffn/pallas_call | solution.py:51
  459.7 5.6 collective-permute-done.8
  469.0 49.1 %ffn.7 = (bf16[512,2048]{1,0:T(8,128)(2,1)}, bf16[512,2048]{1,0:T(8,128)(2,1)}, bf16[512,2048]{1,0:T(8,128)(2,1)}, bf16[512,2048]{1,0:T(8,128)(2,1)}) custom-call(s32[1]{0:T(128)S(6)} %copy.99.refs_0_, bf16[512,2048]{1,0:T(8,128)(2,1)} %get-tuple-element.85.refs_1_, bf16[512,2048]{1,0:T(8,128)(2,1)} %copy-done.5, bf16[1024,2048]{1,0:T(8,128)(2,1)} %bitcast.89, ...), custom_call_target="tpu_custom_call" | custom-call | flops 8053063680 | bytes 8126464 | tf_op jit(solution)/shard_map/ffn/pallas_call | solution.py:51
  525.5 8.4 %branch.1 = (f32[512,2048]{1,0:T(8,128)}, bf16[512,2048]{1,0:T(8,128)(2,1)}) custom-call(s32[1]{0:T(128)S(6)} %copy.99.refs_0_, f32[512,2048]{1,0:T(8,128)} %get-tuple-element.84.refs_1_.refs_0_, bf16[512,2048]{1,0:T(8,128)(2,1)} %get-tuple-element.103.refs_2_, bf16[512,2048]{1,0:T(8,128)(2,1)} %pad_maximum_fusion.refs_3_, ...), custom_call_target="tpu_custom_call" | custom-call | tf_op jit(solution)/shard_map/branch/pallas_call | solution.py:51
  534.0 3.1 add_convert_fusion.refs_11_
  538.6 12.9 %attn_grad.1 = (bf16[2,512,1024]{2,1,0:T(8,128)(2,1)}, f32[128,1024]{1,0:T(8,128)}) custom-call(s32[1]{0:T(128)} %bitcast.1.refs_0_, bf16[2,256,2048]{2,1,0:T(8,128)(2,1)} %bitcast.87, bf16[2,256,2048]{2,1,0:T(8,128)(2,1)} %bitcast.12.refs_2_, bf16[2,512,1024]{2,1,0:T(8,128)(2,1)} %attend.1.refs_1_.refs_2_.refs_3_, ...), custom_call_target="tpu_custom_call" | custom-call | tf_op jit(solution)/shard_map/attn_grad/pallas_call | solution.py:51
  551.5 60.3 %attend_back.1 = (bf16[2,512,1024]{2,1,0:T(8,128)(2,1)}, f32[2,8,64,128]{3,2,1,0:T(8,128)}, f32[2,4,576,128]{3,2,1,0:T(8,128)}, f32[2,4,576,128]{3,2,1,0:T(8,128)}, bf16[2,4,128,128]{3,2,1,0:T(8,128)(2,1)}) custom-call(s32[2,9]{1,0:T(2,128)} %bitcast.114, bf16[2,16,512,64]{3,2,1,0:T(8,128)(2,1)} %get-tuple-element.74.refs_0_.refs_1_, ...), custom_call_target="tpu_custom_call" | custom-call | tf_op jit(solution)/shard_map/attend_back/pallas_call | solution.py:51
  615.1 5.6 collective-permute-done.19
  623.0 5.7 sum_y.1.refs_8_
  630.1 9.1 %key_back.1 = (f32[2,2,512,256]{3,2,1,0:T(8,128)}, bf16[2,2,64,256]{3,2,1,0:T(8,128)(2,1)}, f32[2,2,64,128]{3,2,1,0:T(8,128)}) custom-call(s32[2,9]{1,0:T(2,128)} %bitcast.115, bf16[2,4,576,128]{3,2,1,0:T(8,128)(2,1)} %copy-done, bf16[2,4,576,128]{3,2,1,0:T(8,128)(2,1)} %get-tuple-element.77.refs_3_.refs_2_, ...), custom_call_target="tpu_custom_call" | custom-call | tf_op jit(solution)/shard_map/key_back/pallas_call | solution.py:51
  640.5 5.8 collective-permute-done.21.refs_7_
  646.9 13.7 %normed_grad.1 = (bf16[2,256,2176]{2,1,0:T(8,128)(2,1)}, bf16[2,256,2176]{2,1,0:T(8,128)(2,1)}, f32[2,128,768]{2,1,0:T(8,128)}) custom-call(s32[1]{0:T(128)} %bitcast.1.refs_0_, bf16[2,512,1024]{2,1,0:T(8,128)(2,1)} %get-tuple-element.108.refs_1_.refs_2_, bf16[2,512,1024]{2,1,0:T(8,128)(2,1)} %get-tuple-element.108.refs_1_.refs_2_, ...), custom_call_target="tpu_custom_call" | custom-call | tf_op jit(solution)/shard_map/normed_grad/pallas_call | solution.py:51
  662.7 2.8 collective-permute-done.22
  665.5 7.2 %finish.1 = (bf16[512,2048]{1,0:T(8,128)(2,1)}, f32[128,2048]{1,0:T(8,128)}) custom-call(bf16[512,2176]{1,0:T(8,128)(2,1)} %bitcast.95, bf16[512,2176]{1,0:T(8,128)(2,1)} %bitcast.15.refs_1_, bf16[512,2048]{1,0:T(8,128)(2,1)} %bitcast.84, f32[512,2048]{1,0:T(8,128)} %get-tuple-element.116.refs_3_, f32[1,2048]{1,0:T(1,128)} %bitcast.107, ...), custom_call_target="tpu_custom_call" | custom-call | tf_op jit(solution)/shard_map/finish/pallas_call | solution.py:51
  674.3 25.3 %final_sums.1 = (f32[32,64]{1,0:T(8,128)S(1)}, f32[400,128]{1,0:T(8,128)S(1)}) custom-call(f32[4,2,4,32,64]{4,3,2,1,0:T(8,128)S(1)} %bitcast.82, f32[2,400,128]{2,1,0:T(8,128)S(1)} %constant_dynamic-update-slice_fusion.14.pack_ref), custom_call_target="tpu_custom_call" | custom-call | tf_op jit(solution)/shard_map/final_sums/pallas_call | solution.py:1122
  (209 shorter events, 70.5 us)
Async XLA Ops:
  7.2 317.2 %all-gather.8.cloned.1.call-start = ((), (), s32[]{:S(2)}) async-start(), calls=%async_computation.2 | async-start | bytes 7077888 | tf_op jit(solution)/shard_map/all_gather | solution.py:1211
  11.5 364.0 %all-gather.4.cloned.1.call-start = ((), (), s32[]{:S(2)}) async-start(), calls=%async_computation | async-start | bytes 10616832 | tf_op jit(solution)/shard_map/all_gather | solution.py:1211
  13.7 419.9 %all-gather.6.cloned.1.call-start = ((), (), s32[]{:S(2)}) async-start(), calls=%async_computation.1 | async-start | bytes 7077888 | tf_op jit(solution)/shard_map/all_gather | solution.py:1211
  21.0 191.2 %copy-start.29 = (bf16[8,128]{1,0:T(8,128)(2,1)S(1)}, bf16[8,128]{1,0:T(8,128)(2,1)}, u32[]{:S(2)}) copy-start(bf16[8,128]{1,0:T(8,128)(2,1)} %refs_7_.1) | copy-start | bytes 6148
  21.0 191.2 %copy-start.28 = (bf16[8,128]{1,0:T(8,128)(2,1)S(1)}, bf16[8,128]{1,0:T(8,128)(2,1)}, u32[]{:S(2)}) copy-start(bf16[8,128]{1,0:T(8,128)(2,1)} %refs_6_.1) | copy-start | bytes 6148
  21.1 192.0 %copy-start.22 = (bf16[8,512]{1,0:T(8,128)(2,1)S(1)}, bf16[8,512]{1,0:T(8,128)(2,1)}, u32[]{:S(2)}) copy-start(bf16[8,512]{1,0:T(8,128)(2,1)} %refs_5_.1) | copy-start | bytes 24580
  21.1 192.7 %copy-start.23 = (bf16[2048,8]{0,1:T(8,128)(2,1)S(1)}, bf16[2048,8]{0,1:T(8,128)(2,1)}, u32[]{:S(2)}) copy-start(bf16[2048,8]{0,1:T(8,128)(2,1)} %param.40) | copy-start | bytes 98308
  21.1 192.7 %copy-start.24 = (bf16[2048,8]{0,1:T(8,128)(2,1)S(1)}, bf16[2048,8]{0,1:T(8,128)(2,1)}, u32[]{:S(2)}) copy-start(bf16[2048,8]{0,1:T(8,128)(2,1)} %param.38) | copy-start | bytes 98308
  21.1 192.7 %copy-start.25 = (bf16[2048,8]{0,1:T(8,128)(2,1)S(1)}, bf16[2048,8]{0,1:T(8,128)(2,1)}, u32[]{:S(2)}) copy-start(bf16[2048,8]{0,1:T(8,128)(2,1)} %param.36) | copy-start | bytes 98308
  235.0 7.7 %collective-permute-start = (bf16[2,4,64,128]{3,2,1,0:T(8,128)(2,1)S(1)}, bf16[2,4,64,128]{3,2,1,0:T(8,128)(2,1)S(1)}, u32[]{:S(2)}, u32[]{:S(2)}) collective-permute-start(bf16[2,4,64,128]{3,2,1,0:T(8,128)(2,1)S(1)} %slice.153), channel_id=1, source_target_pairs={{0,2},{1,3},{2,4},{3,5},{4,6},{5,7},{8,10},{9,11},{10,12},{11,13},... | collective-permute-start | bytes 393224 | tf_op jit(solution)/shard_map/ppermute | solution.py:1307
  252.8 8.6 %collective-permute-start.2 = (bf16[2,4,128,128]{3,2,1,0:T(8,128)(2,1)}, bf16[2,4,128,128]{3,2,1,0:T(8,128)(2,1)S(1)}, u32[]{:S(2)}, u32[]{:S(2)}) collective-permute-start(bf16[2,4,128,128]{3,2,1,0:T(8,128)(2,1)} %get-tuple-element.79), channel_id=1, source_target_pairs={{0,2},{1,3},{2,0},{3,1},{4,6},{5,7},{6,4},{7,5},{8,10},{9,11},{10,... | collective-permute-start | bytes 786440 | tf_op jit(solution)/shard_map/ppermute | solution.py:40
  255.2 20.2 %collective-permute-start.1 = (bf16[2,4,128,128]{3,2,1,0:T(8,128)(2,1)}, bf16[2,4,128,128]{3,2,1,0:T(8,128)(2,1)S(1)}, u32[]{:S(2)}, u32[]{:S(2)}) collective-permute-start(bf16[2,4,128,128]{3,2,1,0:T(8,128)(2,1)} %get-tuple-element.79), channel_id=1, source_target_pairs={{0,4},{4,0},{1,5},{5,1},{2,6},{6,2},{3,7},{7,3},{8,12},{12,8},{9,1... | collective-permute-start | bytes 786440 | tf_op jit(solution)/shard_map/ppermute | solution.py:25
  261.4 19.8 %collective-permute-start.3 = (bf16[2,4,128,128]{3,2,1,0:T(8,128)(2,1)S(1)}, bf16[2,4,128,128]{3,2,1,0:T(8,128)(2,1)S(1)}, u32[]{:S(2)}, u32[]{:S(2)}) collective-permute-start(bf16[2,4,128,128]{3,2,1,0:T(8,128)(2,1)S(1)} %collective-permute-done.2), channel_id=1, source_target_pairs={{0,4},{4,0},{1,5},{5,1},{2,6},{6,2},{3,7},{7,3},{8,12},{12,8},{9,1... | collective-permute-start | bytes 786440 | tf_op jit(solution)/shard_map/ppermute | solution.py:25
  308.3 4.6 collective-permute-start.4
  320.0 4.4 collective-permute-start.5
  320.2 48.2 %collective-permute-start.6 = (bf16[512,2048]{1,0:T(8,128)(2,1)}, bf16[512,2048]{1,0:T(8,128)(2,1)}, u32[]{:S(2)}, u32[]{:S(2)}) collective-permute-start(bf16[512,2048]{1,0:T(8,128)(2,1)} %get-tuple-element.85.refs_1_), channel_id=1, source_target_pairs={{0,2},{1,3},{2,0},{3,1},{4,6},{5,7},{6,4},{7,5},{8,10},{9,11},{10,... | collective-permute-start | bytes 6291464 | tf_op jit(solution)/shard_map/ppermute | solution.py:40
  371.1 4.4 collective-permute-start.7
  459.1 6.2 collective-permute-start.8
  459.3 74.8 %collective-permute-start.10 = (bf16[512,2048]{1,0:T(8,128)(2,1)}, bf16[512,2048]{1,0:T(8,128)(2,1)}, u32[]{:S(2)}, u32[]{:S(2)}) collective-permute-start(bf16[512,2048]{1,0:T(8,128)(2,1)} %get-tuple-element.102), channel_id=1, source_target_pairs={{0,1},{1,0},{2,3},{3,2},{4,5},{5,4},{6,7},{7,6},{8,9},{9,8},{10,11... | collective-permute-start | bytes 6291464 | tf_op jit(solution)/shard_map/ppermute | solution.py:29
  467.6 57.9 %collective-permute-start.16 = (bf16[512,2048]{1,0:T(8,128)(2,1)S(1)}, bf16[512,2048]{1,0:T(8,128)(2,1)}, u32[]{:S(2)}, u32[]{:S(2)}) collective-permute-start(bf16[512,2048]{1,0:T(8,128)(2,1)S(1)} %add_convert_fusion.1.refs_10_), channel_id=1, source_target_pairs={{0,2},{1,3},{2,0},{3,1},{4,6},{5,7},{6,4},{7,5},{8,10},{9,11},{10,... | collective-permute-start | bytes 6291464 | tf_op jit(solution)/shard_map/ppermute | solution.py:40
  519.8 2.0 collective-permute-start.12
  519.9 2.5 collective-permute-start.13
  520.3 2.9 collective-permute-start.14
  521.7 2.2 collective-permute-start.15
  533.9 4.7 collective-permute-start.17
  537.2 85.8 %collective-permute-start.11 = (bf16[512,2048]{1,0:T(8,128)(2,1)S(1)}, bf16[512,2048]{1,0:T(8,128)(2,1)}, u32[]{:S(2)}, u32[]{:S(2)}) collective-permute-start(bf16[512,2048]{1,0:T(8,128)(2,1)S(1)} %add_convert_fusion.refs_11_), channel_id=1, source_target_pairs={{0,2},{1,3},{2,0},{3,1},{4,6},{5,7},{6,4},{7,5},{8,10},{9,11},{10,... | collective-permute-start | bytes 6291464 | tf_op jit(solution)/shard_map/ppermute | solution.py:40
  538.5 84.5 %collective-permute-start.9 = (bf16[512,2048]{1,0:T(8,128)(2,1)}, bf16[512,2048]{1,0:T(8,128)(2,1)}, u32[]{:S(2)}, u32[]{:S(2)}) collective-permute-start(bf16[512,2048]{1,0:T(8,128)(2,1)} %get-tuple-element.100), channel_id=1, source_target_pairs={{0,1},{1,0},{2,3},{3,2},{4,5},{5,4},{6,7},{7,6},{8,9},{9,8},{10,11... | collective-permute-start | bytes 6291464 | tf_op jit(solution)/shard_map/ppermute | solution.py:29
  611.8 8.9 %collective-permute-start.19 = (bf16[2,4,128,128]{3,2,1,0:T(8,128)(2,1)}, bf16[2,4,128,128]{3,2,1,0:T(8,128)(2,1)S(1)}, u32[]{:S(2)}, u32[]{:S(2)}) collective-permute-start(bf16[2,4,128,128]{3,2,1,0:T(8,128)(2,1)} %get-tuple-element.107.refs_4_), channel_id=1, source_target_pairs={{0,2},{1,3},{2,0},{3,1},{4,6},{5,7},{6,4},{7,5},{8,10},{9,11},{10,... | collective-permute-start | bytes 786440 | tf_op jit(solution)/shard_map/ppermute | solution.py:40
  612.9 15.8 %collective-permute-start.18 = (bf16[2,4,128,128]{3,2,1,0:T(8,128)(2,1)}, bf16[2,4,128,128]{3,2,1,0:T(8,128)(2,1)S(1)}, u32[]{:S(2)}, u32[]{:S(2)}) collective-permute-start(bf16[2,4,128,128]{3,2,1,0:T(8,128)(2,1)} %get-tuple-element.107.refs_4_), channel_id=1, source_target_pairs={{0,4},{4,0},{1,5},{5,1},{2,6},{6,2},{3,7},{7,3},{8,12},{12,8},{9,1... | collective-permute-start | bytes 786440 | tf_op jit(solution)/shard_map/ppermute | solution.py:25
  620.7 8.4 %collective-permute-start.20 = (bf16[2,4,128,128]{3,2,1,0:T(8,128)(2,1)S(1)}, bf16[2,4,128,128]{3,2,1,0:T(8,128)(2,1)S(1)}, u32[]{:S(2)}, u32[]{:S(2)}) collective-permute-start(bf16[2,4,128,128]{3,2,1,0:T(8,128)(2,1)S(1)} %collective-permute-done.19), channel_id=1, source_target_pairs={{0,4},{4,0},{1,5},{5,1},{2,6},{6,2},{3,7},{7,3},{8,12},{12,8},{9,1... | collective-permute-start | bytes 786440 | tf_op jit(solution)/shard_map/ppermute | solution.py:25
  639.2 7.1 collective-permute-start.21
  660.7 4.8 collective-permute-start.22
  (32 other events, 258.4 us)
Sparse Core Ops, SparseCore 0:
  11.6 161.1 all-gather.7
  175.0 147.5 all-gather.3
  324.8 99.0 all-gather.5

commit v4 on v3

--- a/solution.py
+++ b/solution.py
@@ -10,7 +10,7 @@
 HD = 64
 RANK = 8
 WIN = 64
-FF_CHUNKS = (1, 2, 3, 2)
+FF_CHUNKS = (3, 4, 6, 3)
 
 NORM_EPS = 1e-05
 ADAPTER_SCALE = 2.0
@@ -241,12 +241,11 @@
         for t in starts:
             transfer(t).start()
         if event is None:
-            for copy in early + own:
+            for copy in [cot_x] + early + own:
                 copy.start()
         if i == last_x:
-            cot_x.start()
-    cot_x.wait()
-    cot_last.start()
+            cot_x.wait()
+            cot_last.start()
     for t in number:
         transfer(t).wait_send()
     for copy in early + own + [cot_last]:
@@ -869,7 +868,7 @@
     low_ref[...] = low
     mid = hidden_ref[...].astype(F32) + total[:, :depth]
     mid = mid + ADAPTER_SCALE * dot(low, second_ref[...])
-    mid_ref[...] = mid
+    mid_ref[...] = mid.astype(BF16)
     normed_ref[...] = normalize(mid, gain_ref[...])
 
 
@@ -908,15 +907,18 @@
     refs[-1][...] = sum(r[...].astype(F32) for r in refs[:-1]).astype(BF16)
 
 
-def branch_kernel(slot_len, live_ref, mid_ref, a_ref, b_ref, c_ref, cot_ref, gain_ref, grad_ref, low_ref):
-    grad = a_ref[...].astype(F32) + b_ref[...].astype(F32) + c_ref[...].astype(F32)
+def branch_kernel(slot_len, slots, live_ref, mid_ref, a_ref, c_ref, cot_ref, *refs):
+    parts, (gain_ref, grad_ref) = refs[:slots], refs[slots:]
+    part = parts[0][...]
+    for r in range(1, slots):
+        part = jnp.where(pl.program_id(0) == r, parts[r][...], part)
+    grad = a_ref[...].astype(F32) + part.astype(F32) + c_ref[...].astype(F32)
     tile = mid_ref.shape[0]
     token = pl.program_id(0) * tile + lax.broadcasted_iota(jnp.int32, (tile, 1), 0)
     live = token < live_ref[0] * slot_len
     cot = jnp.where(live, cot_ref[...].astype(F32), 0.0)
-    total = cot + norm_back(mid_ref[...], gain_ref[...], grad)[1]
-    grad_ref[...] = total
-    low_ref[...] = total.astype(BF16)
+    mid = mid_ref[...].astype(F32)
+    grad_ref[...] = (cot + norm_back(mid, gain_ref[...], grad)[1]).astype(BF16)
 
 
 def attn_grad_kernel(
@@ -1038,7 +1040,7 @@
     grad = total[:, :depth] + dot(low, first_ref[...])
     values, gain = hidden_ref[...].astype(F32), gain_ref[...]
     scale, back = norm_back(values, gain, grad)
-    out_ref[...] = (mid_ref[...] + back).astype(BF16)
+    out_ref[...] = (mid_ref[...].astype(F32) + back).astype(BF16)
 
     @pl.when(pl.program_id(0) == 0)
     def _():
@@ -1325,7 +1327,7 @@
         middle_kernel,
         [flat_tokens(v) for v in (hidden_in, keep, flip_core(away))],
         [second, gain_ffn],
-        [(model_dim, F32), (model_dim, BF16), (LOW, BF16)],
+        [(model_dim, BF16), (model_dim, BF16), (LOW, BF16)],
         "middle",
     )
 
@@ -1353,13 +1355,14 @@
     )
     y_there = sum_away(*away[2:])
     y_back = flip_x(y_there)
-    grad_mid, branch = tokens_call(
-        functools.partial(branch_kernel, share_len),
-        [mid_rows, gn_own, flip_core_parts(gn_other, 4), gn_back, flat_tokens(grad_out)],
-        [gain_ffn],
-        [(model_dim, F32), (model_dim, BF16)],
+    branch, = tokens_call(
+        functools.partial(branch_kernel, share_len, slots),
+        [mid_rows, gn_own, gn_back, flat_tokens(grad_out)],
+        [flip_core(gn_other[r * share_len : (r + 1) * share_len]) for r in range(slots)] + [gain_ffn],
+        [(model_dim, BF16)],
         "branch",
         prefetch=[live_rows],
+        tile=share_len,
     )
 
     shaped = lambda v: v.reshape(slots, share_len, -1)
@@ -1400,7 +1403,7 @@
     ]
     grad_hidden, sum_in = tokens_call(
         finish_kernel,
-        [flat_tokens(keep), flat_tokens(flip_core(away)), flat_tokens(hidden_in), grad_mid],
+        [flat_tokens(keep), flat_tokens(flip_core(away)), flat_tokens(hidden_in), branch],
         [gain_attn, adapt_in_all.T],
         [(model_dim, BF16)],
         "finish",

time: 715 us -> 695 us (0.972)
  Pallas kernels: 567 us -> 556 us
    pallas_call x1, Pallas kernels: 191 us -> 180 us  [gather(): pl.pallas_call(functools.partial(gather_kernel, plan, rows, seqs, parts,...]
    ppermute x4, starting transfers between devices: 8.75 us -> 0.08 us  [shift(): lax.ppermute(block, axis, [(i, (i + distance) % size) for i in range(size)])]
    ppermute x12 -> x10, waiting for transfers between devices: 21.5 us -> 21.2 us  [flip_core(): lax.ppermute(block, 'head', [(i, i ^ 1) for i in range(lax.axis_size('hea...]
  transfers between devices with their start and end apart: 26 -> 24, of which waited for: 15 -> 13; matrix products, arithmetic and copies ran while one was open for 5% -> 5% of each run, Pallas kernels for 69% -> 69%
where the time goes in v4:
time: 695 us; the launch traced here: 690 us
  Pallas kernels  556 us (80%)
  waiting for transfers between devices  55.4 us (8%)
  local copies, waits for them, and re-layouts  25.1 us (4%)
  other arithmetic  21.5 us (3%)
  starting transfers between devices  16.3 us (2%)
  between operations  15.6 us (2%)
    pallas_call x18, Pallas kernels, kernel_call(): pl.pallas_call(body, grid_spec=pltpu.PrefetchScalarGridSpec(num_scalar_pr...  351 us
    pallas_call x1, Pallas kernels, gather(): pl.pallas_call(functools.partial(gather_kernel, plan, rows, seqs, parts,...  180 us
    pallas_call x1, Pallas kernels, final_sums(): pl.pallas_call(functools.partial(sums_kernel, rows, seqs, heads), in_spec...  24.8 us
    ppermute x10, waiting for transfers between devices, flip_core(): lax.ppermute(block, 'head', [(i, i ^ 1) for i in range(lax.axis_size('hea...  21.2 us
    ppermute x5, waiting for transfers between devices, flip_x(): lax.ppermute(block, 'head', [(i, i ^ 2) for i in range(lax.axis_size('hea...  20.4 us
  transfers between devices with their start and end apart: 24, of which 13 were waited for; matrix products, arithmetic and copies ran while one was open for 5% of the time, Pallas kernels for 69%

profile of v4, /device:TPU:0, one launch (start us, length us, event | category | flops | bytes accessed | tf_op | source)
XLA Modules:
  0.0 690.2 jit_solution(6119006499523583271)
XLA Ops:
  18.5 179.8 %gather.1 = (bf16[2,2048,768]{2,1,0:T(8,128)(2,1)}, bf16[2,2048,512]{2,1,0:T(8,128)(2,1)}, bf16[2048,1152]{1,0:T(8,128)(2,1)}, bf16[8,64,64]{2,1,0:T(8,128)(2,1)...) custom-call(bf16[256,768]{1,0:T(8,128)(2,1)} %pad_maximum_fusion.4.r, ...), custom_call_target="tpu_custom_call" | custom-call | tf_op jit(solution)/shard_map/gather/pallas_call | solution.py:274
  201.3 16.8 %project.1 = (bf16[2,16,512,64]{3,2,1,0:T(8,128)(2,1)}, bf16[2,4,512,128]{3,2,1,0:T(8,128)(2,1)}, bf16[2,512,128]{2,1,0:T(8,128)(2,1)}) custom-call(s32[1]{0:T(128)} %bitcast.1.refs_0_, bf16[2,256,2048]{2,1,0:T(8,128)(2,1)} %refs_1_.1, bf16[2,256,2048]{2,1,0:T(8,128)(2,1)} %get-tuple-element.67.refs_2_, f32[1,2048]{1,0:T(1,128)} %bitcast.106, ...), custom_call_target="tpu_custom_call" | custom-call | flops 1610612736 | bytes 2621440 | tf_op jit(solution)/shard_map/project/pallas_call | solution.py:51
  219.1 7.3 %collective-permute-start = (bf16[2,4,64,128]{3,2,1,0:T(8,128)(2,1)S(1)}, bf16[2,4,64,128]{3,2,1,0:T(8,128)(2,1)S(1)}, u32[]{:S(2)}, u32[]{:S(2)}) collective-permute-start(bf16[2,4,64,128]{3,2,1,0:T(8,128)(2,1)S(1)} %slice.147), channel_id=1, source_target_pairs={{0,2},{1,3},{2,4},{3,5},{4,6},{5,7},{8,10},{9,11},{10,12},{11,13},... | collective-permute-start | bytes 393224 | tf_op jit(solution)/shard_map/ppermute | solution.py:1309
  232.7 8.8 %key_state.1 = (bf16[2,4,576,128]{3,2,1,0:T(8,128)(2,1)}, bf16[2,4,128,128]{3,2,1,0:T(8,128)(2,1)}) custom-call(s32[2,9]{1,0:T(2,128)} %bitcast.112, bf16[2,4,576,128]{3,2,1,0:T(8,128)(2,1)} %copy-done.1, bf16[4,64,128]{2,1,0:T(8,128)(2,1)} %pad_maximum_fusion.7.refs_2_.refs_3_, s32[2,576,128]{2,1,0:T(8,128)} %broadcast_in_dim.69.refs_3_.refs_7_.refs_8_.refs_5_), custom_call_target="tpu_custom_call" | custom-call | tf_op jit(solution)/shard_map/key_state/pallas_call | solution.py:51
  241.9 6.2 collective-permute-done.2
  248.7 10.2 %query_features.1.refs_4_ = bf16[2,16,512,128]{3,2,1,0:T(8,128)(2,1)} custom-call(bf16[2,16,512,64]{3,2,1,0:T(8,128)(2,1)} %get-tuple-element.72.refs_0_.refs_1_, bf16[16,64,128]{2,1,0:T(8,128)(2,1)} %pad_maximum_fusion.5.refs_1_.refs_5_), custom_call_target="tpu_custom_call" | custom-call | tf_op jit(solution)/shard_map/query_features/pallas_call | solution.py:51
  259.8 5.0 collective-permute-done.3
  266.8 16.1 %attend.1.refs_1_.refs_2_.refs_3_ = bf16[2,512,1024]{2,1,0:T(8,128)(2,1)} custom-call(s32[2,9]{1,0:T(2,128)} %bitcast.113, bf16[2,16,512,64]{3,2,1,0:T(8,128)(2,1)} %get-tuple-element.72.refs_0_.refs_1_, bf16[2,4,576,128]{3,2,1,0:T(8,128)(2,1)} %copy-done.1, bf16[2,4,576,128]{3,2,1,0:T(8,128)(2,1)} %get-tuple-element.75.refs_3_.refs_2_, ...), custom_call_target="tpu_custom_call" | custom-call | tf_op jit(solution)/shard_map/attend/pallas_call | solution.py:51
  283.0 8.9 %out_project.1 = (bf16[2,256,2176]{2,1,0:T(8,128)(2,1)}, bf16[2,256,2176]{2,1,0:T(8,128)(2,1)}) custom-call(s32[1]{0:T(128)} %bitcast.1.refs_0_, bf16[2,512,1024]{2,1,0:T(8,128)(2,1)} %attend.1.refs_1_.refs_2_.refs_3_, bf16[2,512,1024]{2,1,0:T(8,128)(2,1)} %attend.1.refs_1_.refs_2_.refs_3_, bf16[2,2048,512]{2,1,0:T(8,128)(2,1)} %get-tuple-element.78.refs_3_.refs_4_, ...), custom_call_target="tpu_custom_call" | custom-call | tf_op jit(solution)/shard_map/out_project/pallas_call | solution.py:51
  293.3 3.1 collective-permute-done.4
  297.8 5.4 middle.1
  308.9 36.2 %ffn.4 = (bf16[512,2048]{1,0:T(8,128)(2,1)}, bf16[512,2048]{1,0:T(8,128)(2,1)}, bf16[512,2048]{1,0:T(8,128)(2,1)}, bf16[512,2048]{1,0:T(8,128)(2,1)}) custom-call(s32[1]{0:T(128)S(6)} %copy.99.refs_0_, bf16[512,2048]{1,0:T(8,128)(2,1)} %get-tuple-element.83.refs_1_, bf16[512,2048]{1,0:T(8,128)(2,1)} %copy-done.5, bf16[1024,2048]{1,0:T(8,128)(2,1)} %bitcast.88, ...), custom_call_target="tpu_custom_call" | custom-call | flops 5637144576 | bytes 6946816 | tf_op jit(solution)/shard_map/ffn/pallas_call | solution.py:51
  345.2 6.4 collective-permute-done.6.refs_0_
  351.6 2.6 hold.1.refs_1_
  354.2 4.4 collective-permute-done.7.refs_2_
  359.9 59.4 %ffn.5 = (bf16[512,2048]{1,0:T(8,128)(2,1)}, bf16[512,2048]{1,0:T(8,128)(2,1)}, bf16[512,2048]{1,0:T(8,128)(2,1)}, bf16[512,2048]{1,0:T(8,128)(2,1)}) custom-call(s32[1]{0:T(128)S(6)} %copy.99.refs_0_, bf16[512,2048]{1,0:T(8,128)(2,1)} %hold.1.refs_1_, bf16[512,2048]{1,0:T(8,128)(2,1)} %copy-done.6, bf16[1024,2048]{1,0:T(8,128)(2,1)} %bitcast.93, ...), custom_call_target="tpu_custom_call" | custom-call | flops 10468982784 | bytes 9306112 | tf_op jit(solution)/shard_map/ffn/pallas_call | solution.py:51
  419.3 23.8 %ffn.6 = (bf16[512,2048]{1,0:T(8,128)(2,1)}, bf16[512,2048]{1,0:T(8,128)(2,1)}, bf16[512,2048]{1,0:T(8,128)(2,1)}, bf16[512,2048]{1,0:T(8,128)(2,1)}) custom-call(s32[1]{0:T(128)S(6)} %copy.99.refs_0_, bf16[512,2048]{1,0:T(8,128)(2,1)} %hold.1.refs_1_, bf16[512,2048]{1,0:T(8,128)(2,1)} %copy-done.6, bf16[1024,2048]{1,0:T(8,128)(2,1)} %bitcast.94, ...), custom_call_target="tpu_custom_call" | custom-call | flops 2415919104 | bytes 5373952 | tf_op jit(solution)/shard_map/ffn/pallas_call | solution.py:51
  443.8 5.5 collective-permute-done.8
  453.4 47.3 %ffn.7 = (bf16[512,2048]{1,0:T(8,128)(2,1)}, bf16[512,2048]{1,0:T(8,128)(2,1)}, bf16[512,2048]{1,0:T(8,128)(2,1)}, bf16[512,2048]{1,0:T(8,128)(2,1)}) custom-call(s32[1]{0:T(128)S(6)} %copy.99.refs_0_, bf16[512,2048]{1,0:T(8,128)(2,1)} %get-tuple-element.83.refs_1_, bf16[512,2048]{1,0:T(8,128)(2,1)} %copy-done.5, bf16[1024,2048]{1,0:T(8,128)(2,1)} %bitcast.89, ...), custom_call_target="tpu_custom_call" | custom-call | flops 7247757312 | bytes 7733248 | tf_op jit(solution)/shard_map/ffn/pallas_call | solution.py:51
  507.7 7.7 %branch.1.refs_3_ = bf16[512,2048]{1,0:T(8,128)(2,1)} custom-call(s32[1]{0:T(128)S(6)} %copy.99.refs_0_, bf16[512,2048]{1,0:T(8,128)(2,1)} %get-tuple-element.82.refs_1_.refs_0_, bf16[512,2048]{1,0:T(8,128)(2,1)} %get-tuple-element.101.refs_2_, bf16[512,2048]{1,0:T(8,128)(2,1)} %collective-permute-done.12.refs_3_, bf16[512,2048]{1,0:T(8,128)(2,1)} %bitcast.86, ...), custom_call_target="tpu_custom_call" | custom-call | tf_op jit(solution)/shard_map/branch/pallas_call | solution.py:51
  515.5 3.1 add_convert_fusion.refs_11_
  520.0 12.9 %attn_grad.1 = (bf16[2,512,1024]{2,1,0:T(8,128)(2,1)}, f32[128,1024]{1,0:T(8,128)}) custom-call(s32[1]{0:T(128)} %bitcast.1.refs_0_, bf16[2,256,2048]{2,1,0:T(8,128)(2,1)} %bitcast.85, bf16[2,256,2048]{2,1,0:T(8,128)(2,1)} %bitcast.12.refs_2_, bf16[2,512,1024]{2,1,0:T(8,128)(2,1)} %attend.1.refs_1_.refs_2_.refs_3_, ...), custom_call_target="tpu_custom_call" | custom-call | tf_op jit(solution)/shard_map/attn_grad/pallas_call | solution.py:51
  533.0 60.3 %attend_back.1 = (bf16[2,512,1024]{2,1,0:T(8,128)(2,1)}, f32[2,8,64,128]{3,2,1,0:T(8,128)}, f32[2,4,576,128]{3,2,1,0:T(8,128)}, f32[2,4,576,128]{3,2,1,0:T(8,128)}, bf16[2,4,128,128]{3,2,1,0:T(8,128)(2,1)}) custom-call(s32[2,9]{1,0:T(2,128)} %bitcast.114, bf16[2,16,512,64]{3,2,1,0:T(8,128)(2,1)} %get-tuple-element.72.refs_0_.refs_1_, ...), custom_call_target="tpu_custom_call" | custom-call | tf_op jit(solution)/shard_map/attend_back/pallas_call | solution.py:51
  594.3 7.8 %collective-permute-done.17 = bf16[2,4,128,128]{3,2,1,0:T(8,128)(2,1)S(1)} collective-permute-done((bf16[2,4,128,128]{3,2,1,0:T(8,128)(2,1)}, bf16[2,4,128,128]{3,2,1,0:T(8,128)(2,1)S(1)}, u32[]{:S(2)}, u32[]{:S(2)}) %collective-permute-start.17) | collective-permute-done | bytes 262176 | tf_op jit(solution)/shard_map/ppermute | solution.py:40
  602.2 4.9 sum_y.1.refs_8_
  607.1 2.9 collective-permute-done.18
  611.0 9.1 %key_back.1 = (f32[2,2,512,256]{3,2,1,0:T(8,128)}, bf16[2,2,64,256]{3,2,1,0:T(8,128)(2,1)}, f32[2,2,64,128]{3,2,1,0:T(8,128)}) custom-call(s32[2,9]{1,0:T(2,128)} %bitcast.115, bf16[2,4,576,128]{3,2,1,0:T(8,128)(2,1)} %copy-done.1, bf16[2,4,576,128]{3,2,1,0:T(8,128)(2,1)} %get-tuple-element.75.refs_3_.refs_2_, ...), custom_call_target="tpu_custom_call" | custom-call | tf_op jit(solution)/shard_map/key_back/pallas_call | solution.py:51
  621.4 5.8 collective-permute-done.19.refs_7_
  627.9 13.6 %normed_grad.1 = (bf16[2,256,2176]{2,1,0:T(8,128)(2,1)}, bf16[2,256,2176]{2,1,0:T(8,128)(2,1)}, f32[2,128,768]{2,1,0:T(8,128)}) custom-call(s32[1]{0:T(128)} %bitcast.1.refs_0_, bf16[2,512,1024]{2,1,0:T(8,128)(2,1)} %get-tuple-element.105.refs_1_.refs_2_, bf16[2,512,1024]{2,1,0:T(8,128)(2,1)} %get-tuple-element.105.refs_1_.refs_2_, ...), custom_call_target="tpu_custom_call" | custom-call | tf_op jit(solution)/shard_map/normed_grad/pallas_call | solution.py:51
  643.5 2.8 collective-permute-done.20
  646.3 7.0 %finish.1 = (bf16[512,2048]{1,0:T(8,128)(2,1)}, f32[128,2048]{1,0:T(8,128)}) custom-call(bf16[512,2176]{1,0:T(8,128)(2,1)} %bitcast.95, bf16[512,2176]{1,0:T(8,128)(2,1)} %bitcast.15.refs_1_, bf16[512,2048]{1,0:T(8,128)(2,1)} %bitcast.84, bf16[512,2048]{1,0:T(8,128)(2,1)} %branch.1.refs_3_, f32[1,2048]{1,0:T(1,128)} %bitcast.107, ...), custom_call_target="tpu_custom_call" | custom-call | tf_op jit(solution)/shard_map/finish/pallas_call | solution.py:51
  654.9 24.8 %final_sums.1 = (f32[32,64]{1,0:T(8,128)S(1)}, f32[400,128]{1,0:T(8,128)S(1)}) custom-call(f32[4,2,4,32,64]{4,3,2,1,0:T(8,128)S(1)} %bitcast.82, f32[2,400,128]{2,1,0:T(8,128)S(1)} %constant_dynamic-update-slice_fusion.14.pack_ref), custom_call_target="tpu_custom_call" | custom-call | tf_op jit(solution)/shard_map/final_sums/pallas_call | solution.py:1124
  (213 shorter events, 58.6 us)
Async XLA Ops:
  7.2 300.4 %all-gather.8.cloned.1.call-start = ((), (), s32[]{:S(2)}) async-start(), calls=%async_computation.2 | async-start | bytes 7077888 | tf_op jit(solution)/shard_map/all_gather | solution.py:1213
  9.9 348.7 %all-gather.4.cloned.1.call-start = ((), (), s32[]{:S(2)}) async-start(), calls=%async_computation | async-start | bytes 10616832 | tf_op jit(solution)/shard_map/all_gather | solution.py:1213
  11.4 407.9 %all-gather.6.cloned.1.call-start = ((), (), s32[]{:S(2)}) async-start(), calls=%async_computation.1 | async-start | bytes 5308416 | tf_op jit(solution)/shard_map/all_gather | solution.py:1213
  18.5 179.8 %copy-start.32 = (bf16[8,128]{1,0:T(8,128)(2,1)S(1)}, bf16[8,128]{1,0:T(8,128)(2,1)}, u32[]{:S(2)}) copy-start(bf16[8,128]{1,0:T(8,128)(2,1)} %refs_6_.1) | copy-start | bytes 6148
  18.5 180.6 %copy-start.33 = (bf16[8,128]{1,0:T(8,128)(2,1)S(1)}, bf16[8,128]{1,0:T(8,128)(2,1)}, u32[]{:S(2)}) copy-start(bf16[8,128]{1,0:T(8,128)(2,1)} %refs_7_.1) | copy-start | bytes 6148
  18.5 181.3 %copy-start.26 = (bf16[8,512]{1,0:T(8,128)(2,1)S(1)}, bf16[8,512]{1,0:T(8,128)(2,1)}, u32[]{:S(2)}) copy-start(bf16[8,512]{1,0:T(8,128)(2,1)} %refs_5_.1) | copy-start | bytes 24580
  201.3 26.0 %copy-start.18 = (bf16[2,64,64]{2,1,0:T(8,128)(2,1)S(1)}, bf16[2,64,64]{2,1,0:T(8,128)(2,1)}, u32[]{:S(2)}) copy-start(bf16[2,64,64]{2,1,0:T(8,128)(2,1)} %refs_4_.1) | copy-start | bytes 49156
  201.3 26.0 %copy-start.31 = (bf16[2,64,64]{2,1,0:T(8,128)(2,1)S(1)}, bf16[2,64,64]{2,1,0:T(8,128)(2,1)}, u32[]{:S(2)}) copy-start(bf16[2,64,64]{2,1,0:T(8,128)(2,1)} %get-tuple-element.74) | copy-start | bytes 49156
  219.1 12.2 %collective-permute-start = (bf16[2,4,64,128]{3,2,1,0:T(8,128)(2,1)S(1)}, bf16[2,4,64,128]{3,2,1,0:T(8,128)(2,1)S(1)}, u32[]{:S(2)}, u32[]{:S(2)}) collective-permute-start(bf16[2,4,64,128]{3,2,1,0:T(8,128)(2,1)S(1)} %slice.147), channel_id=1, source_target_pairs={{0,2},{1,3},{2,4},{3,5},{4,6},{5,7},{8,10},{9,11},{10,12},{11,13},... | collective-permute-start | bytes 393224 | tf_op jit(solution)/shard_map/ppermute | solution.py:1309
  241.5 6.6 collective-permute-start.2
  241.8 18.0 %collective-permute-start.1 = (bf16[2,4,128,128]{3,2,1,0:T(8,128)(2,1)}, bf16[2,4,128,128]{3,2,1,0:T(8,128)(2,1)S(1)}, u32[]{:S(2)}, u32[]{:S(2)}) collective-permute-start(bf16[2,4,128,128]{3,2,1,0:T(8,128)(2,1)} %get-tuple-element.77), channel_id=1, source_target_pairs={{0,4},{4,0},{1,5},{5,1},{2,6},{6,2},{3,7},{7,3},{8,12},{12,8},{9,1... | collective-permute-start | bytes 786440 | tf_op jit(solution)/shard_map/ppermute | solution.py:25
  248.0 16.7 %collective-permute-start.3 = (bf16[2,4,128,128]{3,2,1,0:T(8,128)(2,1)S(1)}, bf16[2,4,128,128]{3,2,1,0:T(8,128)(2,1)S(1)}, u32[]{:S(2)}, u32[]{:S(2)}) collective-permute-start(bf16[2,4,128,128]{3,2,1,0:T(8,128)(2,1)S(1)} %collective-permute-done.2), channel_id=1, source_target_pairs={{0,4},{4,0},{1,5},{5,1},{2,6},{6,2},{3,7},{7,3},{8,12},{12,8},{9,1... | collective-permute-start | bytes 786440 | tf_op jit(solution)/shard_map/ppermute | solution.py:25
  291.9 4.6 collective-permute-start.4
  303.2 4.4 collective-permute-start.5
  303.3 48.2 %collective-permute-start.6 = (bf16[512,2048]{1,0:T(8,128)(2,1)}, bf16[512,2048]{1,0:T(8,128)(2,1)}, u32[]{:S(2)}, u32[]{:S(2)}) collective-permute-start(bf16[512,2048]{1,0:T(8,128)(2,1)} %get-tuple-element.83.refs_1_), channel_id=1, source_target_pairs={{0,2},{1,3},{2,0},{3,1},{4,6},{5,7},{6,4},{7,5},{8,10},{9,11},{10,... | collective-permute-start | bytes 6291464 | tf_op jit(solution)/shard_map/ppermute | solution.py:40
  354.2 4.4 collective-permute-start.7
  443.2 6.0 collective-permute-start.8
  443.4 72.1 %collective-permute-start.10 = (bf16[512,2048]{1,0:T(8,128)(2,1)}, bf16[512,2048]{1,0:T(8,128)(2,1)}, u32[]{:S(2)}, u32[]{:S(2)}) collective-permute-start(bf16[512,2048]{1,0:T(8,128)(2,1)} %get-tuple-element.100), channel_id=1, source_target_pairs={{0,1},{1,0},{2,3},{3,2},{4,5},{5,4},{6,7},{7,6},{8,9},{9,8},{10,11... | collective-permute-start | bytes 6291464 | tf_op jit(solution)/shard_map/ppermute | solution.py:29
  451.6 55.1 %collective-permute-start.12 = (bf16[512,2048]{1,0:T(8,128)(2,1)S(1)}, bf16[512,2048]{1,0:T(8,128)(2,1)}, u32[]{:S(2)}, u32[]{:S(2)}) collective-permute-start(bf16[512,2048]{1,0:T(8,128)(2,1)S(1)} %add_convert_fusion.1.refs_10_), channel_id=1, source_target_pairs={{0,2},{1,3},{2,0},{3,1},{4,6},{5,7},{6,4},{7,5},{8,10},{9,11},{10,... | collective-permute-start | bytes 6291464 | tf_op jit(solution)/shard_map/ppermute | solution.py:40
  502.5 2.7 collective-permute-start.13
  502.5 4.1 collective-permute-start.14
  515.4 4.7 collective-permute-start.15
  518.6 14.3 %copy-start.3 = (bf16[512,2048]{1,0:T(8,128)(2,1)}, bf16[512,2048]{1,0:T(8,128)(2,1)S(1)}, u32[]{:S(2)}) copy-start(bf16[512,2048]{1,0:T(8,128)(2,1)S(1)} %add_convert_fusion.refs_11_) | copy-start | bytes 6291460
  518.7 83.5 %collective-permute-start.11 = (bf16[512,2048]{1,0:T(8,128)(2,1)S(1)}, bf16[512,2048]{1,0:T(8,128)(2,1)}, u32[]{:S(2)}, u32[]{:S(2)}) collective-permute-start(bf16[512,2048]{1,0:T(8,128)(2,1)S(1)} %add_convert_fusion.refs_11_), channel_id=1, source_target_pairs={{0,2},{1,3},{2,0},{3,1},{4,6},{5,7},{6,4},{7,5},{8,10},{9,11},{10,... | collective-permute-start | bytes 6291464 | tf_op jit(solution)/shard_map/ppermute | solution.py:40
  520.0 82.2 %collective-permute-start.9 = (bf16[512,2048]{1,0:T(8,128)(2,1)}, bf16[512,2048]{1,0:T(8,128)(2,1)}, u32[]{:S(2)}, u32[]{:S(2)}) collective-permute-start(bf16[512,2048]{1,0:T(8,128)(2,1)} %get-tuple-element.98), channel_id=1, source_target_pairs={{0,1},{1,0},{2,3},{3,2},{4,5},{5,4},{6,7},{7,6},{8,9},{9,8},{10,11... | collective-permute-start | bytes 6291464 | tf_op jit(solution)/shard_map/ppermute | solution.py:29
  593.2 8.9 %collective-permute-start.17 = (bf16[2,4,128,128]{3,2,1,0:T(8,128)(2,1)}, bf16[2,4,128,128]{3,2,1,0:T(8,128)(2,1)S(1)}, u32[]{:S(2)}, u32[]{:S(2)}) collective-permute-start(bf16[2,4,128,128]{3,2,1,0:T(8,128)(2,1)} %get-tuple-element.104.refs_4_), channel_id=1, source_target_pairs={{0,2},{1,3},{2,0},{3,1},{4,6},{5,7},{6,4},{7,5},{8,10},{9,11},{10,... | collective-permute-start | bytes 786440 | tf_op jit(solution)/shard_map/ppermute | solution.py:40
  594.3 12.8 %collective-permute-start.16 = (bf16[2,4,128,128]{3,2,1,0:T(8,128)(2,1)}, bf16[2,4,128,128]{3,2,1,0:T(8,128)(2,1)S(1)}, u32[]{:S(2)}, u32[]{:S(2)}) collective-permute-start(bf16[2,4,128,128]{3,2,1,0:T(8,128)(2,1)} %get-tuple-element.104.refs_4_), channel_id=1, source_target_pairs={{0,4},{4,0},{1,5},{5,1},{2,6},{6,2},{3,7},{7,3},{8,12},{12,8},{9,1... | collective-permute-start | bytes 786440 | tf_op jit(solution)/shard_map/ppermute | solution.py:25
  602.2 7.9 %collective-permute-start.18 = (bf16[2,4,128,128]{3,2,1,0:T(8,128)(2,1)S(1)}, bf16[2,4,128,128]{3,2,1,0:T(8,128)(2,1)S(1)}, u32[]{:S(2)}, u32[]{:S(2)}) collective-permute-start(bf16[2,4,128,128]{3,2,1,0:T(8,128)(2,1)S(1)} %collective-permute-done.17), channel_id=1, source_target_pairs={{0,4},{4,0},{1,5},{5,1},{2,6},{6,2},{3,7},{7,3},{8,12},{12,8},{9,1... | collective-permute-start | bytes 786440 | tf_op jit(solution)/shard_map/ppermute | solution.py:25
  620.1 7.1 %collective-permute-start.19 = (bf16[2,2,64,256]{3,2,1,0:T(8,128)(2,1)}, bf16[2,2,64,256]{3,2,1,0:T(8,128)(2,1)S(1)}, u32[]{:S(2)}, u32[]{:S(2)}) collective-permute-start(bf16[2,2,64,256]{3,2,1,0:T(8,128)(2,1)} %get-tuple-element.110), channel_id=1, source_target_pairs={{2,0},{3,1},{4,2},{5,3},{6,4},{7,5},{10,8},{11,9},{12,10},{13,11},... | collective-permute-start | bytes 393224 | tf_op jit(solution)/shard_map/ppermute | solution.py:1309
  627.9 13.8 %copy-start = (bf16[512,2048]{1,0:T(8,128)(2,1)S(1)}, bf16[512,2048]{1,0:T(8,128)(2,1)}, u32[]{:S(2)}) copy-start(bf16[512,2048]{1,0:T(8,128)(2,1)} %branch.1.refs_3_) | copy-start | bytes 6291460
  627.9 13.8 %copy-start.20 = (bf16[512,128]{1,0:T(8,128)(2,1)S(1)}, bf16[512,128]{1,0:T(8,128)(2,1)}, u32[]{:S(2)}) copy-start(bf16[512,128]{1,0:T(8,128)(2,1)} %get-tuple-element.115) | copy-start | bytes 393220
  641.5 4.8 collective-permute-start.20
  (34 other events, 141.6 us)
Sparse Core Ops, SparseCore 0:
  10.2 171.0 all-gather.7
  183.5 144.3 all-gather.3
  330.1 79.3 all-gather.5

commit v5 on v4

--- a/solution.py
+++ b/solution.py
@@ -1415,6 +1415,7 @@
     by_rows = jnp.concatenate([sum_in, sum_o_out], axis=0)
     width = model_dim // (rows * seqs * heads)
     by_rows = by_rows.reshape(4 * RANK, rows, seqs, heads, width).transpose(3, 2, 1, 0, 4)
+    by_rows = by_rows.reshape(heads, seqs, rows, -1, 2 * HD)
 
     def lanes_of(v):
         v = v.reshape(2, RANK, -1, 2 * HD).transpose(0, 2, 1, 3)

time: 695 us -> 693 us (level)
  no operation moved by 1% of the time
where the time goes in v5:
time: 693 us; the launch traced here: 688 us
  Pallas kernels  552 us (80%)
  waiting for transfers between devices  55.4 us (8%)
  local copies, waits for them, and re-layouts  27.3 us (4%)
  other arithmetic  21.5 us (3%)
  starting transfers between devices  16.3 us (2%)
  between operations  15.6 us (2%)
    pallas_call x18, Pallas kernels, kernel_call(): pl.pallas_call(body, grid_spec=pltpu.PrefetchScalarGridSpec(num_scalar_pr...  351 us
    pallas_call x1, Pallas kernels, gather(): pl.pallas_call(functools.partial(gather_kernel, plan, rows, seqs, parts,...  180 us
    ppermute x10, waiting for transfers between devices, flip_core(): lax.ppermute(block, 'head', [(i, i ^ 1) for i in range(lax.axis_size('hea...  21.2 us
    pallas_call x1, Pallas kernels, final_sums(): pl.pallas_call(functools.partial(sums_kernel, rows, seqs, heads), in_spec...  20.8 us
    ppermute x5, waiting for transfers between devices, flip_x(): lax.ppermute(block, 'head', [(i, i ^ 2) for i in range(lax.axis_size('hea...  20.4 us
  transfers between devices with their start and end apart: 24, of which 13 were waited for; matrix products, arithmetic and copies ran while one was open for 5% of the time, Pallas kernels for 69%

profile of v5, /device:TPU:0, one launch (start us, length us, event | category | flops | bytes accessed | tf_op | source)
XLA Modules:
  0.0 688.3 jit_solution(5944628416399394653)
XLA Ops:
  18.5 179.8 %gather.1 = (bf16[2,2048,768]{2,1,0:T(8,128)(2,1)}, bf16[2,2048,512]{2,1,0:T(8,128)(2,1)}, bf16[2048,1152]{1,0:T(8,128)(2,1)}, bf16[8,64,64]{2,1,0:T(8,128)(2,1)...) custom-call(bf16[256,768]{1,0:T(8,128)(2,1)} %pad_maximum_fusion.4.r, ...), custom_call_target="tpu_custom_call" | custom-call | tf_op jit(solution)/shard_map/gather/pallas_call | solution.py:274
  201.3 16.8 %project.1 = (bf16[2,16,512,64]{3,2,1,0:T(8,128)(2,1)}, bf16[2,4,512,128]{3,2,1,0:T(8,128)(2,1)}, bf16[2,512,128]{2,1,0:T(8,128)(2,1)}) custom-call(s32[1]{0:T(128)} %bitcast.1.refs_0_, bf16[2,256,2048]{2,1,0:T(8,128)(2,1)} %refs_1_.1, bf16[2,256,2048]{2,1,0:T(8,128)(2,1)} %get-tuple-element.67.refs_2_, f32[1,2048]{1,0:T(1,128)} %bitcast.105, ...), custom_call_target="tpu_custom_call" | custom-call | flops 1610612736 | bytes 2621440 | tf_op jit(solution)/shard_map/project/pallas_call | solution.py:51
  219.1 7.3 %collective-permute-start = (bf16[2,4,64,128]{3,2,1,0:T(8,128)(2,1)S(1)}, bf16[2,4,64,128]{3,2,1,0:T(8,128)(2,1)S(1)}, u32[]{:S(2)}, u32[]{:S(2)}) collective-permute-start(bf16[2,4,64,128]{3,2,1,0:T(8,128)(2,1)S(1)} %slice.147), channel_id=1, source_target_pairs={{0,2},{1,3},{2,4},{3,5},{4,6},{5,7},{8,10},{9,11},{10,12},{11,13},... | collective-permute-start | bytes 393224 | tf_op jit(solution)/shard_map/ppermute | solution.py:1309
  232.7 8.8 %key_state.1 = (bf16[2,4,576,128]{3,2,1,0:T(8,128)(2,1)}, bf16[2,4,128,128]{3,2,1,0:T(8,128)(2,1)}) custom-call(s32[2,9]{1,0:T(2,128)} %bitcast.111, bf16[2,4,576,128]{3,2,1,0:T(8,128)(2,1)} %copy-done.1, bf16[4,64,128]{2,1,0:T(8,128)(2,1)} %pad_maximum_fusion.7.refs_2_.refs_3_, s32[2,576,128]{2,1,0:T(8,128)} %broadcast_in_dim.69.refs_3_.refs_7_.refs_8_.refs_5_), custom_call_target="tpu_custom_call" | custom-call | tf_op jit(solution)/shard_map/key_state/pallas_call | solution.py:51
  241.9 6.2 collective-permute-done.2
  248.7 10.2 %query_features.1.refs_4_ = bf16[2,16,512,128]{3,2,1,0:T(8,128)(2,1)} custom-call(bf16[2,16,512,64]{3,2,1,0:T(8,128)(2,1)} %get-tuple-element.72.refs_0_.refs_1_, bf16[16,64,128]{2,1,0:T(8,128)(2,1)} %pad_maximum_fusion.5.refs_1_.refs_5_), custom_call_target="tpu_custom_call" | custom-call | tf_op jit(solution)/shard_map/query_features/pallas_call | solution.py:51
  259.8 5.0 collective-permute-done.3
  266.8 16.1 %attend.1.refs_1_.refs_2_.refs_3_ = bf16[2,512,1024]{2,1,0:T(8,128)(2,1)} custom-call(s32[2,9]{1,0:T(2,128)} %bitcast.112, bf16[2,16,512,64]{3,2,1,0:T(8,128)(2,1)} %get-tuple-element.72.refs_0_.refs_1_, bf16[2,4,576,128]{3,2,1,0:T(8,128)(2,1)} %copy-done.1, bf16[2,4,576,128]{3,2,1,0:T(8,128)(2,1)} %get-tuple-element.75.refs_3_.refs_2_, ...), custom_call_target="tpu_custom_call" | custom-call | tf_op jit(solution)/shard_map/attend/pallas_call | solution.py:51
  283.0 8.9 %out_project.1 = (bf16[2,256,2176]{2,1,0:T(8,128)(2,1)}, bf16[2,256,2176]{2,1,0:T(8,128)(2,1)}) custom-call(s32[1]{0:T(128)} %bitcast.1.refs_0_, bf16[2,512,1024]{2,1,0:T(8,128)(2,1)} %attend.1.refs_1_.refs_2_.refs_3_, bf16[2,512,1024]{2,1,0:T(8,128)(2,1)} %attend.1.refs_1_.refs_2_.refs_3_, bf16[2,2048,512]{2,1,0:T(8,128)(2,1)} %get-tuple-element.78.refs_3_.refs_4_, ...), custom_call_target="tpu_custom_call" | custom-call | tf_op jit(solution)/shard_map/out_project/pallas_call | solution.py:51
  293.3 3.1 collective-permute-done.4
  297.8 5.4 middle.1
  308.9 36.2 %ffn.4 = (bf16[512,2048]{1,0:T(8,128)(2,1)}, bf16[512,2048]{1,0:T(8,128)(2,1)}, bf16[512,2048]{1,0:T(8,128)(2,1)}, bf16[512,2048]{1,0:T(8,128)(2,1)}) custom-call(s32[1]{0:T(128)S(6)} %copy.100.refs_0_, bf16[512,2048]{1,0:T(8,128)(2,1)} %get-tuple-element.83.refs_1_, bf16[512,2048]{1,0:T(8,128)(2,1)} %copy-done.5, bf16[1024,2048]{1,0:T(8,128)(2,1)} %bitcast.86, ...), custom_call_target="tpu_custom_call" | custom-call | flops 5637144576 | bytes 6946816 | tf_op jit(solution)/shard_map/ffn/pallas_call | solution.py:51
  345.2 6.4 collective-permute-done.6.refs_0_
  351.6 2.6 hold.1.refs_1_
  354.2 4.4 collective-permute-done.7.refs_2_
  359.9 59.4 %ffn.5 = (bf16[512,2048]{1,0:T(8,128)(2,1)}, bf16[512,2048]{1,0:T(8,128)(2,1)}, bf16[512,2048]{1,0:T(8,128)(2,1)}, bf16[512,2048]{1,0:T(8,128)(2,1)}) custom-call(s32[1]{0:T(128)S(6)} %copy.100.refs_0_, bf16[512,2048]{1,0:T(8,128)(2,1)} %hold.1.refs_1_, bf16[512,2048]{1,0:T(8,128)(2,1)} %copy-done.6, bf16[1024,2048]{1,0:T(8,128)(2,1)} %bitcast.91, ...), custom_call_target="tpu_custom_call" | custom-call | flops 10468982784 | bytes 9306112 | tf_op jit(solution)/shard_map/ffn/pallas_call | solution.py:51
  419.3 23.8 %ffn.6 = (bf16[512,2048]{1,0:T(8,128)(2,1)}, bf16[512,2048]{1,0:T(8,128)(2,1)}, bf16[512,2048]{1,0:T(8,128)(2,1)}, bf16[512,2048]{1,0:T(8,128)(2,1)}) custom-call(s32[1]{0:T(128)S(6)} %copy.100.refs_0_, bf16[512,2048]{1,0:T(8,128)(2,1)} %hold.1.refs_1_, bf16[512,2048]{1,0:T(8,128)(2,1)} %copy-done.6, bf16[1024,2048]{1,0:T(8,128)(2,1)} %bitcast.92, ...), custom_call_target="tpu_custom_call" | custom-call | flops 2415919104 | bytes 5373952 | tf_op jit(solution)/shard_map/ffn/pallas_call | solution.py:51
  443.8 5.5 collective-permute-done.8
  453.4 47.3 %ffn.7 = (bf16[512,2048]{1,0:T(8,128)(2,1)}, bf16[512,2048]{1,0:T(8,128)(2,1)}, bf16[512,2048]{1,0:T(8,128)(2,1)}, bf16[512,2048]{1,0:T(8,128)(2,1)}) custom-call(s32[1]{0:T(128)S(6)} %copy.100.refs_0_, bf16[512,2048]{1,0:T(8,128)(2,1)} %get-tuple-element.83.refs_1_, bf16[512,2048]{1,0:T(8,128)(2,1)} %copy-done.5, bf16[1024,2048]{1,0:T(8,128)(2,1)} %bitcast.87, ...), custom_call_target="tpu_custom_call" | custom-call | flops 7247757312 | bytes 7733248 | tf_op jit(solution)/shard_map/ffn/pallas_call | solution.py:51
  507.7 7.7 %branch.1.refs_3_ = bf16[512,2048]{1,0:T(8,128)(2,1)} custom-call(s32[1]{0:T(128)S(6)} %copy.100.refs_0_, bf16[512,2048]{1,0:T(8,128)(2,1)} %get-tuple-element.82.refs_1_.refs_0_, bf16[512,2048]{1,0:T(8,128)(2,1)} %get-tuple-element.101.refs_2_, bf16[512,2048]{1,0:T(8,128)(2,1)} %collective-permute-done.12.refs_3_, bf16[512,2048]{1,0:T(8,128)(2,1)} %bitcast.84, ...), custom_call_target="tpu_custom_call" | custom-call | tf_op jit(solution)/shard_map/branch/pallas_call | solution.py:51
  515.5 3.1 add_convert_fusion.refs_11_
  520.0 12.9 %attn_grad.1 = (bf16[2,512,1024]{2,1,0:T(8,128)(2,1)}, f32[128,1024]{1,0:T(8,128)}) custom-call(s32[1]{0:T(128)} %bitcast.1.refs_0_, bf16[2,256,2048]{2,1,0:T(8,128)(2,1)} %bitcast.83, bf16[2,256,2048]{2,1,0:T(8,128)(2,1)} %bitcast.12.refs_2_, bf16[2,512,1024]{2,1,0:T(8,128)(2,1)} %attend.1.refs_1_.refs_2_.refs_3_, ...), custom_call_target="tpu_custom_call" | custom-call | tf_op jit(solution)/shard_map/attn_grad/pallas_call | solution.py:51
  533.0 60.3 %attend_back.1 = (bf16[2,512,1024]{2,1,0:T(8,128)(2,1)}, f32[2,8,64,128]{3,2,1,0:T(8,128)}, f32[2,4,576,128]{3,2,1,0:T(8,128)}, f32[2,4,576,128]{3,2,1,0:T(8,128)}, bf16[2,4,128,128]{3,2,1,0:T(8,128)(2,1)}) custom-call(s32[2,9]{1,0:T(2,128)} %bitcast.113, bf16[2,16,512,64]{3,2,1,0:T(8,128)(2,1)} %get-tuple-element.72.refs_0_.refs_1_, ...), custom_call_target="tpu_custom_call" | custom-call | tf_op jit(solution)/shard_map/attend_back/pallas_call | solution.py:51
  594.3 7.8 %collective-permute-done.17 = bf16[2,4,128,128]{3,2,1,0:T(8,128)(2,1)S(1)} collective-permute-done((bf16[2,4,128,128]{3,2,1,0:T(8,128)(2,1)}, bf16[2,4,128,128]{3,2,1,0:T(8,128)(2,1)S(1)}, u32[]{:S(2)}, u32[]{:S(2)}) %collective-permute-start.17) | collective-permute-done | bytes 262176 | tf_op jit(solution)/shard_map/ppermute | solution.py:40
  602.2 4.9 sum_y.1.refs_8_
  607.1 2.9 collective-permute-done.18
  611.0 9.1 %key_back.1 = (f32[2,2,512,256]{3,2,1,0:T(8,128)}, bf16[2,2,64,256]{3,2,1,0:T(8,128)(2,1)}, f32[2,2,64,128]{3,2,1,0:T(8,128)}) custom-call(s32[2,9]{1,0:T(2,128)} %bitcast.114, bf16[2,4,576,128]{3,2,1,0:T(8,128)(2,1)} %copy-done.1, bf16[2,4,576,128]{3,2,1,0:T(8,128)(2,1)} %get-tuple-element.75.refs_3_.refs_2_, ...), custom_call_target="tpu_custom_call" | custom-call | tf_op jit(solution)/shard_map/key_back/pallas_call | solution.py:51
  621.4 5.8 collective-permute-done.19.refs_7_
  627.9 13.6 %normed_grad.1 = (bf16[2,256,2176]{2,1,0:T(8,128)(2,1)}, bf16[2,256,2176]{2,1,0:T(8,128)(2,1)}, f32[2,128,768]{2,1,0:T(8,128)}) custom-call(s32[1]{0:T(128)} %bitcast.1.refs_0_, bf16[2,512,1024]{2,1,0:T(8,128)(2,1)} %get-tuple-element.105.refs_1_.refs_2_, bf16[2,512,1024]{2,1,0:T(8,128)(2,1)} %get-tuple-element.105.refs_1_.refs_2_, ...), custom_call_target="tpu_custom_call" | custom-call | tf_op jit(solution)/shard_map/normed_grad/pallas_call | solution.py:51
  643.5 2.8 collective-permute-done.20
  646.3 7.0 %finish.1 = (bf16[512,2048]{1,0:T(8,128)(2,1)}, f32[128,2048]{1,0:T(8,128)}) custom-call(bf16[512,2176]{1,0:T(8,128)(2,1)} %bitcast.93, bf16[512,2176]{1,0:T(8,128)(2,1)} %bitcast.15.refs_1_, bf16[512,2048]{1,0:T(8,128)(2,1)} %bitcast.82, bf16[512,2048]{1,0:T(8,128)(2,1)} %branch.1.refs_3_, f32[1,2048]{1,0:T(1,128)} %bitcast.106, ...), custom_call_target="tpu_custom_call" | custom-call | tf_op jit(solution)/shard_map/finish/pallas_call | solution.py:51
  655.0 20.8 %final_sums.1 = (f32[16,128]{1,0:T(8,128)S(1)}, f32[400,128]{1,0:T(8,128)S(1)}) custom-call(f32[4,2,4,16,128]{4,3,2,1,0:T(8,128)S(1)} %reshape.229.part_ref, f32[2,400,128]{2,1,0:T(8,128)S(1)} %constant_dynamic-update-slice_fusion.14.pack_ref), custom_call_target="tpu_custom_call" | custom-call | tf_op jit(solution)/shard_map/final_sums/pallas_call | solution.py:1124
  (218 shorter events, 60.7 us)
Async XLA Ops:
  7.2 300.4 %all-gather.8.cloned.1.call-start = ((), (), s32[]{:S(2)}) async-start(), calls=%async_computation.2 | async-start | bytes 7077888 | tf_op jit(solution)/shard_map/all_gather | solution.py:1213
  9.9 348.7 %all-gather.4.cloned.1.call-start = ((), (), s32[]{:S(2)}) async-start(), calls=%async_computation | async-start | bytes 10616832 | tf_op jit(solution)/shard_map/all_gather | solution.py:1213
  11.4 407.9 %all-gather.6.cloned.1.call-start = ((), (), s32[]{:S(2)}) async-start(), calls=%async_computation.1 | async-start | bytes 5308416 | tf_op jit(solution)/shard_map/all_gather | solution.py:1213
  18.5 179.8 %copy-start.32 = (bf16[8,128]{1,0:T(8,128)(2,1)S(1)}, bf16[8,128]{1,0:T(8,128)(2,1)}, u32[]{:S(2)}) copy-start(bf16[8,128]{1,0:T(8,128)(2,1)} %refs_6_.1) | copy-start | bytes 6148
  18.5 180.6 %copy-start.33 = (bf16[8,128]{1,0:T(8,128)(2,1)S(1)}, bf16[8,128]{1,0:T(8,128)(2,1)}, u32[]{:S(2)}) copy-start(bf16[8,128]{1,0:T(8,128)(2,1)} %refs_7_.1) | copy-start | bytes 6148
  18.5 181.3 %copy-start.26 = (bf16[8,512]{1,0:T(8,128)(2,1)S(1)}, bf16[8,512]{1,0:T(8,128)(2,1)}, u32[]{:S(2)}) copy-start(bf16[8,512]{1,0:T(8,128)(2,1)} %refs_5_.1) | copy-start | bytes 24580
  201.3 26.0 %copy-start.18 = (bf16[2,64,64]{2,1,0:T(8,128)(2,1)S(1)}, bf16[2,64,64]{2,1,0:T(8,128)(2,1)}, u32[]{:S(2)}) copy-start(bf16[2,64,64]{2,1,0:T(8,128)(2,1)} %refs_4_.1) | copy-start | bytes 49156
  201.3 26.0 %copy-start.31 = (bf16[2,64,64]{2,1,0:T(8,128)(2,1)S(1)}, bf16[2,64,64]{2,1,0:T(8,128)(2,1)}, u32[]{:S(2)}) copy-start(bf16[2,64,64]{2,1,0:T(8,128)(2,1)} %get-tuple-element.74) | copy-start | bytes 49156
  219.1 12.2 %collective-permute-start = (bf16[2,4,64,128]{3,2,1,0:T(8,128)(2,1)S(1)}, bf16[2,4,64,128]{3,2,1,0:T(8,128)(2,1)S(1)}, u32[]{:S(2)}, u32[]{:S(2)}) collective-permute-start(bf16[2,4,64,128]{3,2,1,0:T(8,128)(2,1)S(1)} %slice.147), channel_id=1, source_target_pairs={{0,2},{1,3},{2,4},{3,5},{4,6},{5,7},{8,10},{9,11},{10,12},{11,13},... | collective-permute-start | bytes 393224 | tf_op jit(solution)/shard_map/ppermute | solution.py:1309
  241.5 6.6 collective-permute-start.2
  241.8 18.0 %collective-permute-start.1 = (bf16[2,4,128,128]{3,2,1,0:T(8,128)(2,1)}, bf16[2,4,128,128]{3,2,1,0:T(8,128)(2,1)S(1)}, u32[]{:S(2)}, u32[]{:S(2)}) collective-permute-start(bf16[2,4,128,128]{3,2,1,0:T(8,128)(2,1)} %get-tuple-element.77), channel_id=1, source_target_pairs={{0,4},{4,0},{1,5},{5,1},{2,6},{6,2},{3,7},{7,3},{8,12},{12,8},{9,1... | collective-permute-start | bytes 786440 | tf_op jit(solution)/shard_map/ppermute | solution.py:25
  248.0 16.7 %collective-permute-start.3 = (bf16[2,4,128,128]{3,2,1,0:T(8,128)(2,1)S(1)}, bf16[2,4,128,128]{3,2,1,0:T(8,128)(2,1)S(1)}, u32[]{:S(2)}, u32[]{:S(2)}) collective-permute-start(bf16[2,4,128,128]{3,2,1,0:T(8,128)(2,1)S(1)} %collective-permute-done.2), channel_id=1, source_target_pairs={{0,4},{4,0},{1,5},{5,1},{2,6},{6,2},{3,7},{7,3},{8,12},{12,8},{9,1... | collective-permute-start | bytes 786440 | tf_op jit(solution)/shard_map/ppermute | solution.py:25
  291.9 4.6 collective-permute-start.4
  303.2 4.4 collective-permute-start.5
  303.3 48.2 %collective-permute-start.6 = (bf16[512,2048]{1,0:T(8,128)(2,1)}, bf16[512,2048]{1,0:T(8,128)(2,1)}, u32[]{:S(2)}, u32[]{:S(2)}) collective-permute-start(bf16[512,2048]{1,0:T(8,128)(2,1)} %get-tuple-element.83.refs_1_), channel_id=1, source_target_pairs={{0,2},{1,3},{2,0},{3,1},{4,6},{5,7},{6,4},{7,5},{8,10},{9,11},{10,... | collective-permute-start | bytes 6291464 | tf_op jit(solution)/shard_map/ppermute | solution.py:40
  354.2 4.4 collective-permute-start.7
  443.2 6.0 collective-permute-start.8
  443.4 72.1 %collective-permute-start.10 = (bf16[512,2048]{1,0:T(8,128)(2,1)}, bf16[512,2048]{1,0:T(8,128)(2,1)}, u32[]{:S(2)}, u32[]{:S(2)}) collective-permute-start(bf16[512,2048]{1,0:T(8,128)(2,1)} %get-tuple-element.100), channel_id=1, source_target_pairs={{0,1},{1,0},{2,3},{3,2},{4,5},{5,4},{6,7},{7,6},{8,9},{9,8},{10,11... | collective-permute-start | bytes 6291464 | tf_op jit(solution)/shard_map/ppermute | solution.py:29
  451.6 55.1 %collective-permute-start.12 = (bf16[512,2048]{1,0:T(8,128)(2,1)S(1)}, bf16[512,2048]{1,0:T(8,128)(2,1)}, u32[]{:S(2)}, u32[]{:S(2)}) collective-permute-start(bf16[512,2048]{1,0:T(8,128)(2,1)S(1)} %add_convert_fusion.1.refs_10_), channel_id=1, source_target_pairs={{0,2},{1,3},{2,0},{3,1},{4,6},{5,7},{6,4},{7,5},{8,10},{9,11},{10,... | collective-permute-start | bytes 6291464 | tf_op jit(solution)/shard_map/ppermute | solution.py:40
  502.5 2.7 collective-permute-start.13
  502.5 4.1 collective-permute-start.14
  515.4 4.7 collective-permute-start.15
  518.6 14.3 %copy-start.3 = (bf16[512,2048]{1,0:T(8,128)(2,1)}, bf16[512,2048]{1,0:T(8,128)(2,1)S(1)}, u32[]{:S(2)}) copy-start(bf16[512,2048]{1,0:T(8,128)(2,1)S(1)} %add_convert_fusion.refs_11_) | copy-start | bytes 6291460
  518.7 83.5 %collective-permute-start.11 = (bf16[512,2048]{1,0:T(8,128)(2,1)S(1)}, bf16[512,2048]{1,0:T(8,128)(2,1)}, u32[]{:S(2)}, u32[]{:S(2)}) collective-permute-start(bf16[512,2048]{1,0:T(8,128)(2,1)S(1)} %add_convert_fusion.refs_11_), channel_id=1, source_target_pairs={{0,2},{1,3},{2,0},{3,1},{4,6},{5,7},{6,4},{7,5},{8,10},{9,11},{10,... | collective-permute-start | bytes 6291464 | tf_op jit(solution)/shard_map/ppermute | solution.py:40
  520.0 82.2 %collective-permute-start.9 = (bf16[512,2048]{1,0:T(8,128)(2,1)}, bf16[512,2048]{1,0:T(8,128)(2,1)}, u32[]{:S(2)}, u32[]{:S(2)}) collective-permute-start(bf16[512,2048]{1,0:T(8,128)(2,1)} %get-tuple-element.98), channel_id=1, source_target_pairs={{0,1},{1,0},{2,3},{3,2},{4,5},{5,4},{6,7},{7,6},{8,9},{9,8},{10,11... | collective-permute-start | bytes 6291464 | tf_op jit(solution)/shard_map/ppermute | solution.py:29
  593.2 8.9 %collective-permute-start.17 = (bf16[2,4,128,128]{3,2,1,0:T(8,128)(2,1)}, bf16[2,4,128,128]{3,2,1,0:T(8,128)(2,1)S(1)}, u32[]{:S(2)}, u32[]{:S(2)}) collective-permute-start(bf16[2,4,128,128]{3,2,1,0:T(8,128)(2,1)} %get-tuple-element.104.refs_4_), channel_id=1, source_target_pairs={{0,2},{1,3},{2,0},{3,1},{4,6},{5,7},{6,4},{7,5},{8,10},{9,11},{10,... | collective-permute-start | bytes 786440 | tf_op jit(solution)/shard_map/ppermute | solution.py:40
  594.3 12.8 %collective-permute-start.16 = (bf16[2,4,128,128]{3,2,1,0:T(8,128)(2,1)}, bf16[2,4,128,128]{3,2,1,0:T(8,128)(2,1)S(1)}, u32[]{:S(2)}, u32[]{:S(2)}) collective-permute-start(bf16[2,4,128,128]{3,2,1,0:T(8,128)(2,1)} %get-tuple-element.104.refs_4_), channel_id=1, source_target_pairs={{0,4},{4,0},{1,5},{5,1},{2,6},{6,2},{3,7},{7,3},{8,12},{12,8},{9,1... | collective-permute-start | bytes 786440 | tf_op jit(solution)/shard_map/ppermute | solution.py:25
  602.2 7.9 %collective-permute-start.18 = (bf16[2,4,128,128]{3,2,1,0:T(8,128)(2,1)S(1)}, bf16[2,4,128,128]{3,2,1,0:T(8,128)(2,1)S(1)}, u32[]{:S(2)}, u32[]{:S(2)}) collective-permute-start(bf16[2,4,128,128]{3,2,1,0:T(8,128)(2,1)S(1)} %collective-permute-done.17), channel_id=1, source_target_pairs={{0,4},{4,0},{1,5},{5,1},{2,6},{6,2},{3,7},{7,3},{8,12},{12,8},{9,1... | collective-permute-start | bytes 786440 | tf_op jit(solution)/shard_map/ppermute | solution.py:25
  620.1 7.1 %collective-permute-start.19 = (bf16[2,2,64,256]{3,2,1,0:T(8,128)(2,1)}, bf16[2,2,64,256]{3,2,1,0:T(8,128)(2,1)S(1)}, u32[]{:S(2)}, u32[]{:S(2)}) collective-permute-start(bf16[2,2,64,256]{3,2,1,0:T(8,128)(2,1)} %get-tuple-element.110), channel_id=1, source_target_pairs={{2,0},{3,1},{4,2},{5,3},{6,4},{7,5},{10,8},{11,9},{12,10},{13,11},... | collective-permute-start | bytes 393224 | tf_op jit(solution)/shard_map/ppermute | solution.py:1309
  627.9 13.8 %copy-start = (bf16[512,2048]{1,0:T(8,128)(2,1)S(1)}, bf16[512,2048]{1,0:T(8,128)(2,1)}, u32[]{:S(2)}) copy-start(bf16[512,2048]{1,0:T(8,128)(2,1)} %branch.1.refs_3_) | copy-start | bytes 6291460
  627.9 13.8 %copy-start.20 = (bf16[512,128]{1,0:T(8,128)(2,1)S(1)}, bf16[512,128]{1,0:T(8,128)(2,1)}, u32[]{:S(2)}) copy-start(bf16[512,128]{1,0:T(8,128)(2,1)} %get-tuple-element.115) | copy-start | bytes 393220
  641.5 4.8 collective-permute-start.20
  (34 other events, 141.6 us)
Sparse Core Ops, SparseCore 0:
  10.2 171.0 all-gather.7
  183.5 144.3 all-gather.3
  330.1 79.3 all-gather.5

commit v6 on v5

--- a/solution.py
+++ b/solution.py
@@ -872,7 +872,7 @@
     normed_ref[...] = normalize(mid, gain_ref[...])
 
 
-def tokens_call(kernel, tiled, whole, outs, name, prefetch=(), sums=(), tile=256, after=()):
+def tokens_call(kernel, tiled, whole, outs, name, prefetch=(), sums=(), tile=128, after=()):
     tokens = tiled[0].shape[0]
     tile = min(tile, tokens)
     rows = lambda v: pl.BlockSpec((tile, v.shape[1]), lambda i, *_: (i, 0))

time: 693 us -> 695 us (level)
  no operation moved by 1% of the time
where the time goes in v6:
time: 695 us; the launch traced here: 690 us
  Pallas kernels  554 us (80%)
  waiting for transfers between devices  54.9 us (8%)
  local copies, waits for them, and re-layouts  27.3 us (4%)
  other arithmetic  21.5 us (3%)
  starting transfers between devices  16.2 us (2%)
  between operations  15.6 us (2%)
    pallas_call x18, Pallas kernels, kernel_call(): pl.pallas_call(body, grid_spec=pltpu.PrefetchScalarGridSpec(num_scalar_pr...  354 us
    pallas_call x1, Pallas kernels, gather(): pl.pallas_call(functools.partial(gather_kernel, plan, rows, seqs, parts,...  180 us
    ppermute x10, waiting for transfers between devices, flip_core(): lax.ppermute(block, 'head', [(i, i ^ 1) for i in range(lax.axis_size('hea...  21.2 us
    pallas_call x1, Pallas kernels, final_sums(): pl.pallas_call(functools.partial(sums_kernel, rows, seqs, heads), in_spec...  20.8 us
    ppermute x5, waiting for transfers between devices, flip_x(): lax.ppermute(block, 'head', [(i, i ^ 2) for i in range(lax.axis_size('hea...  20.4 us
  transfers between devices with their start and end apart: 24, of which 13 were waited for; matrix products, arithmetic and copies ran while one was open for 5% of the time, Pallas kernels for 69%

profile of v6, /device:TPU:0, one launch (start us, length us, event | category | flops | bytes accessed | tf_op | source)
XLA Modules:
  0.0 690.0 jit_solution(16415661018279497465)
XLA Ops:
  18.5 179.8 %gather.1 = (bf16[2,2048,768]{2,1,0:T(8,128)(2,1)}, bf16[2,2048,512]{2,1,0:T(8,128)(2,1)}, bf16[2048,1152]{1,0:T(8,128)(2,1)}, bf16[8,64,64]{2,1,0:T(8,128)(2,1)...) custom-call(bf16[256,768]{1,0:T(8,128)(2,1)} %pad_maximum_fusion.4.r, ...), custom_call_target="tpu_custom_call" | custom-call | tf_op jit(solution)/shard_map/gather/pallas_call | solution.py:274
  201.3 16.8 %project.1 = (bf16[2,16,512,64]{3,2,1,0:T(8,128)(2,1)}, bf16[2,4,512,128]{3,2,1,0:T(8,128)(2,1)}, bf16[2,512,128]{2,1,0:T(8,128)(2,1)}) custom-call(s32[1]{0:T(128)} %bitcast.1.refs_0_, bf16[2,256,2048]{2,1,0:T(8,128)(2,1)} %refs_1_.1, bf16[2,256,2048]{2,1,0:T(8,128)(2,1)} %get-tuple-element.67.refs_2_, f32[1,2048]{1,0:T(1,128)} %bitcast.105, ...), custom_call_target="tpu_custom_call" | custom-call | flops 1610612736 | bytes 2621440 | tf_op jit(solution)/shard_map/project/pallas_call | solution.py:51
  219.1 7.3 %collective-permute-start = (bf16[2,4,64,128]{3,2,1,0:T(8,128)(2,1)S(1)}, bf16[2,4,64,128]{3,2,1,0:T(8,128)(2,1)S(1)}, u32[]{:S(2)}, u32[]{:S(2)}) collective-permute-start(bf16[2,4,64,128]{3,2,1,0:T(8,128)(2,1)S(1)} %slice.147), channel_id=1, source_target_pairs={{0,2},{1,3},{2,4},{3,5},{4,6},{5,7},{8,10},{9,11},{10,12},{11,13},... | collective-permute-start | bytes 393224 | tf_op jit(solution)/shard_map/ppermute | solution.py:1309
  232.7 8.8 %key_state.1 = (bf16[2,4,576,128]{3,2,1,0:T(8,128)(2,1)}, bf16[2,4,128,128]{3,2,1,0:T(8,128)(2,1)}) custom-call(s32[2,9]{1,0:T(2,128)} %bitcast.111, bf16[2,4,576,128]{3,2,1,0:T(8,128)(2,1)} %copy-done.1, bf16[4,64,128]{2,1,0:T(8,128)(2,1)} %pad_maximum_fusion.7.refs_2_.refs_3_, s32[2,576,128]{2,1,0:T(8,128)} %broadcast_in_dim.69.refs_3_.refs_7_.refs_8_.refs_5_), custom_call_target="tpu_custom_call" | custom-call | tf_op jit(solution)/shard_map/key_state/pallas_call | solution.py:51
  241.9 6.2 collective-permute-done.2
  248.7 10.2 %query_features.1.refs_4_ = bf16[2,16,512,128]{3,2,1,0:T(8,128)(2,1)} custom-call(bf16[2,16,512,64]{3,2,1,0:T(8,128)(2,1)} %get-tuple-element.72.refs_0_.refs_1_, bf16[16,64,128]{2,1,0:T(8,128)(2,1)} %pad_maximum_fusion.5.refs_1_.refs_5_), custom_call_target="tpu_custom_call" | custom-call | tf_op jit(solution)/shard_map/query_features/pallas_call | solution.py:51
  259.8 5.0 collective-permute-done.3
  266.8 16.1 %attend.1.refs_1_.refs_2_.refs_3_ = bf16[2,512,1024]{2,1,0:T(8,128)(2,1)} custom-call(s32[2,9]{1,0:T(2,128)} %bitcast.112, bf16[2,16,512,64]{3,2,1,0:T(8,128)(2,1)} %get-tuple-element.72.refs_0_.refs_1_, bf16[2,4,576,128]{3,2,1,0:T(8,128)(2,1)} %copy-done.1, bf16[2,4,576,128]{3,2,1,0:T(8,128)(2,1)} %get-tuple-element.75.refs_3_.refs_2_, ...), custom_call_target="tpu_custom_call" | custom-call | tf_op jit(solution)/shard_map/attend/pallas_call | solution.py:51
  283.0 8.9 %out_project.1 = (bf16[2,256,2176]{2,1,0:T(8,128)(2,1)}, bf16[2,256,2176]{2,1,0:T(8,128)(2,1)}) custom-call(s32[1]{0:T(128)} %bitcast.1.refs_0_, bf16[2,512,1024]{2,1,0:T(8,128)(2,1)} %attend.1.refs_1_.refs_2_.refs_3_, bf16[2,512,1024]{2,1,0:T(8,128)(2,1)} %attend.1.refs_1_.refs_2_.refs_3_, bf16[2,2048,512]{2,1,0:T(8,128)(2,1)} %get-tuple-element.78.refs_3_.refs_4_, ...), custom_call_target="tpu_custom_call" | custom-call | tf_op jit(solution)/shard_map/out_project/pallas_call | solution.py:51
  293.3 3.1 collective-permute-done.4
  297.8 6.4 middle.1
  309.9 36.2 %ffn.4 = (bf16[512,2048]{1,0:T(8,128)(2,1)}, bf16[512,2048]{1,0:T(8,128)(2,1)}, bf16[512,2048]{1,0:T(8,128)(2,1)}, bf16[512,2048]{1,0:T(8,128)(2,1)}) custom-call(s32[1]{0:T(128)S(6)} %copy.100.refs_0_, bf16[512,2048]{1,0:T(8,128)(2,1)} %get-tuple-element.83.refs_1_, bf16[512,2048]{1,0:T(8,128)(2,1)} %copy-done.5, bf16[1024,2048]{1,0:T(8,128)(2,1)} %bitcast.86, ...), custom_call_target="tpu_custom_call" | custom-call | flops 5637144576 | bytes 6946816 | tf_op jit(solution)/shard_map/ffn/pallas_call | solution.py:51
  346.2 6.4 collective-permute-done.6.refs_0_
  352.6 2.6 hold.1.refs_1_
  355.2 4.4 collective-permute-done.7.refs_2_
  360.9 59.4 %ffn.5 = (bf16[512,2048]{1,0:T(8,128)(2,1)}, bf16[512,2048]{1,0:T(8,128)(2,1)}, bf16[512,2048]{1,0:T(8,128)(2,1)}, bf16[512,2048]{1,0:T(8,128)(2,1)}) custom-call(s32[1]{0:T(128)S(6)} %copy.100.refs_0_, bf16[512,2048]{1,0:T(8,128)(2,1)} %hold.1.refs_1_, bf16[512,2048]{1,0:T(8,128)(2,1)} %copy-done.6, bf16[1024,2048]{1,0:T(8,128)(2,1)} %bitcast.91, ...), custom_call_target="tpu_custom_call" | custom-call | flops 10468982784 | bytes 9306112 | tf_op jit(solution)/shard_map/ffn/pallas_call | solution.py:51
  420.4 23.9 %ffn.6 = (bf16[512,2048]{1,0:T(8,128)(2,1)}, bf16[512,2048]{1,0:T(8,128)(2,1)}, bf16[512,2048]{1,0:T(8,128)(2,1)}, bf16[512,2048]{1,0:T(8,128)(2,1)}) custom-call(s32[1]{0:T(128)S(6)} %copy.100.refs_0_, bf16[512,2048]{1,0:T(8,128)(2,1)} %hold.1.refs_1_, bf16[512,2048]{1,0:T(8,128)(2,1)} %copy-done.6, bf16[1024,2048]{1,0:T(8,128)(2,1)} %bitcast.92, ...), custom_call_target="tpu_custom_call" | custom-call | flops 2415919104 | bytes 5373952 | tf_op jit(solution)/shard_map/ffn/pallas_call | solution.py:51
  444.8 5.5 collective-permute-done.8
  454.4 47.3 %ffn.7 = (bf16[512,2048]{1,0:T(8,128)(2,1)}, bf16[512,2048]{1,0:T(8,128)(2,1)}, bf16[512,2048]{1,0:T(8,128)(2,1)}, bf16[512,2048]{1,0:T(8,128)(2,1)}) custom-call(s32[1]{0:T(128)S(6)} %copy.100.refs_0_, bf16[512,2048]{1,0:T(8,128)(2,1)} %get-tuple-element.83.refs_1_, bf16[512,2048]{1,0:T(8,128)(2,1)} %copy-done.5, bf16[1024,2048]{1,0:T(8,128)(2,1)} %bitcast.87, ...), custom_call_target="tpu_custom_call" | custom-call | flops 7247757312 | bytes 7733248 | tf_op jit(solution)/shard_map/ffn/pallas_call | solution.py:51
  508.6 7.7 %branch.1.refs_3_ = bf16[512,2048]{1,0:T(8,128)(2,1)} custom-call(s32[1]{0:T(128)S(6)} %copy.100.refs_0_, bf16[512,2048]{1,0:T(8,128)(2,1)} %get-tuple-element.82.refs_1_.refs_0_, bf16[512,2048]{1,0:T(8,128)(2,1)} %get-tuple-element.101.refs_2_, bf16[512,2048]{1,0:T(8,128)(2,1)} %collective-permute-done.12.refs_3_, bf16[512,2048]{1,0:T(8,128)(2,1)} %bitcast.84, ...), custom_call_target="tpu_custom_call" | custom-call | tf_op jit(solution)/shard_map/branch/pallas_call | solution.py:51
  516.5 3.1 add_convert_fusion.refs_11_
  521.0 12.9 %attn_grad.1 = (bf16[2,512,1024]{2,1,0:T(8,128)(2,1)}, f32[128,1024]{1,0:T(8,128)}) custom-call(s32[1]{0:T(128)} %bitcast.1.refs_0_, bf16[2,256,2048]{2,1,0:T(8,128)(2,1)} %bitcast.83, bf16[2,256,2048]{2,1,0:T(8,128)(2,1)} %bitcast.12.refs_2_, bf16[2,512,1024]{2,1,0:T(8,128)(2,1)} %attend.1.refs_1_.refs_2_.refs_3_, ...), custom_call_target="tpu_custom_call" | custom-call | tf_op jit(solution)/shard_map/attn_grad/pallas_call | solution.py:51
  533.9 60.3 %attend_back.1 = (bf16[2,512,1024]{2,1,0:T(8,128)(2,1)}, f32[2,8,64,128]{3,2,1,0:T(8,128)}, f32[2,4,576,128]{3,2,1,0:T(8,128)}, f32[2,4,576,128]{3,2,1,0:T(8,128)}, bf16[2,4,128,128]{3,2,1,0:T(8,128)(2,1)}) custom-call(s32[2,9]{1,0:T(2,128)} %bitcast.113, bf16[2,16,512,64]{3,2,1,0:T(8,128)(2,1)} %get-tuple-element.72.refs_0_.refs_1_, ...), custom_call_target="tpu_custom_call" | custom-call | tf_op jit(solution)/shard_map/attend_back/pallas_call | solution.py:51
  595.3 7.8 %collective-permute-done.17 = bf16[2,4,128,128]{3,2,1,0:T(8,128)(2,1)S(1)} collective-permute-done((bf16[2,4,128,128]{3,2,1,0:T(8,128)(2,1)}, bf16[2,4,128,128]{3,2,1,0:T(8,128)(2,1)S(1)}, u32[]{:S(2)}, u32[]{:S(2)}) %collective-permute-start.17) | collective-permute-done | bytes 262176 | tf_op jit(solution)/shard_map/ppermute | solution.py:40
  603.2 5.5 sum_y.1.refs_8_
  608.7 2.4 collective-permute-done.18
  612.0 9.1 %key_back.1 = (f32[2,2,512,256]{3,2,1,0:T(8,128)}, bf16[2,2,64,256]{3,2,1,0:T(8,128)(2,1)}, f32[2,2,64,128]{3,2,1,0:T(8,128)}) custom-call(s32[2,9]{1,0:T(2,128)} %bitcast.114, bf16[2,4,576,128]{3,2,1,0:T(8,128)(2,1)} %copy-done.1, bf16[2,4,576,128]{3,2,1,0:T(8,128)(2,1)} %get-tuple-element.75.refs_3_.refs_2_, ...), custom_call_target="tpu_custom_call" | custom-call | tf_op jit(solution)/shard_map/key_back/pallas_call | solution.py:51
  622.4 5.8 collective-permute-done.19.refs_7_
  628.8 13.6 %normed_grad.1 = (bf16[2,256,2176]{2,1,0:T(8,128)(2,1)}, bf16[2,256,2176]{2,1,0:T(8,128)(2,1)}, f32[2,128,768]{2,1,0:T(8,128)}) custom-call(s32[1]{0:T(128)} %bitcast.1.refs_0_, bf16[2,512,1024]{2,1,0:T(8,128)(2,1)} %get-tuple-element.105.refs_1_.refs_2_, bf16[2,512,1024]{2,1,0:T(8,128)(2,1)} %get-tuple-element.105.refs_1_.refs_2_, ...), custom_call_target="tpu_custom_call" | custom-call | tf_op jit(solution)/shard_map/normed_grad/pallas_call | solution.py:51
  644.5 2.8 collective-permute-done.20
  647.3 7.7 %finish.1 = (bf16[512,2048]{1,0:T(8,128)(2,1)}, f32[128,2048]{1,0:T(8,128)}) custom-call(bf16[512,2176]{1,0:T(8,128)(2,1)} %bitcast.93, bf16[512,2176]{1,0:T(8,128)(2,1)} %bitcast.15.refs_1_, bf16[512,2048]{1,0:T(8,128)(2,1)} %bitcast.82, bf16[512,2048]{1,0:T(8,128)(2,1)} %branch.1.refs_3_, f32[1,2048]{1,0:T(1,128)} %bitcast.106, ...), custom_call_target="tpu_custom_call" | custom-call | tf_op jit(solution)/shard_map/finish/pallas_call | solution.py:51
  656.7 20.8 %final_sums.1 = (f32[16,128]{1,0:T(8,128)S(1)}, f32[400,128]{1,0:T(8,128)S(1)}) custom-call(f32[4,2,4,16,128]{4,3,2,1,0:T(8,128)S(1)} %reshape.229.part_ref, f32[2,400,128]{2,1,0:T(8,128)S(1)} %constant_dynamic-update-slice_fusion.14.pack_ref), custom_call_target="tpu_custom_call" | custom-call | tf_op jit(solution)/shard_map/final_sums/pallas_call | solution.py:1124
  (218 shorter events, 60.6 us)
Async XLA Ops:
  7.2 301.4 %all-gather.8.cloned.1.call-start = ((), (), s32[]{:S(2)}) async-start(), calls=%async_computation.2 | async-start | bytes 7077888 | tf_op jit(solution)/shard_map/all_gather | solution.py:1213
  9.9 349.7 %all-gather.4.cloned.1.call-start = ((), (), s32[]{:S(2)}) async-start(), calls=%async_computation | async-start | bytes 10616832 | tf_op jit(solution)/shard_map/all_gather | solution.py:1213
  11.4 409.0 %all-gather.6.cloned.1.call-start = ((), (), s32[]{:S(2)}) async-start(), calls=%async_computation.1 | async-start | bytes 5308416 | tf_op jit(solution)/shard_map/all_gather | solution.py:1213
  18.5 179.8 %copy-start.32 = (bf16[8,128]{1,0:T(8,128)(2,1)S(1)}, bf16[8,128]{1,0:T(8,128)(2,1)}, u32[]{:S(2)}) copy-start(bf16[8,128]{1,0:T(8,128)(2,1)} %refs_6_.1) | copy-start | bytes 6148
  18.5 180.6 %copy-start.33 = (bf16[8,128]{1,0:T(8,128)(2,1)S(1)}, bf16[8,128]{1,0:T(8,128)(2,1)}, u32[]{:S(2)}) copy-start(bf16[8,128]{1,0:T(8,128)(2,1)} %refs_7_.1) | copy-start | bytes 6148
  18.5 181.3 %copy-start.26 = (bf16[8,512]{1,0:T(8,128)(2,1)S(1)}, bf16[8,512]{1,0:T(8,128)(2,1)}, u32[]{:S(2)}) copy-start(bf16[8,512]{1,0:T(8,128)(2,1)} %refs_5_.1) | copy-start | bytes 24580
  201.3 26.0 %copy-start.18 = (bf16[2,64,64]{2,1,0:T(8,128)(2,1)S(1)}, bf16[2,64,64]{2,1,0:T(8,128)(2,1)}, u32[]{:S(2)}) copy-start(bf16[2,64,64]{2,1,0:T(8,128)(2,1)} %refs_4_.1) | copy-start | bytes 49156
  201.3 26.0 %copy-start.31 = (bf16[2,64,64]{2,1,0:T(8,128)(2,1)S(1)}, bf16[2,64,64]{2,1,0:T(8,128)(2,1)}, u32[]{:S(2)}) copy-start(bf16[2,64,64]{2,1,0:T(8,128)(2,1)} %get-tuple-element.74) | copy-start | bytes 49156
  219.1 12.2 %collective-permute-start = (bf16[2,4,64,128]{3,2,1,0:T(8,128)(2,1)S(1)}, bf16[2,4,64,128]{3,2,1,0:T(8,128)(2,1)S(1)}, u32[]{:S(2)}, u32[]{:S(2)}) collective-permute-start(bf16[2,4,64,128]{3,2,1,0:T(8,128)(2,1)S(1)} %slice.147), channel_id=1, source_target_pairs={{0,2},{1,3},{2,4},{3,5},{4,6},{5,7},{8,10},{9,11},{10,12},{11,13},... | collective-permute-start | bytes 393224 | tf_op jit(solution)/shard_map/ppermute | solution.py:1309
  241.5 6.6 collective-permute-start.2
  241.8 18.0 %collective-permute-start.1 = (bf16[2,4,128,128]{3,2,1,0:T(8,128)(2,1)}, bf16[2,4,128,128]{3,2,1,0:T(8,128)(2,1)S(1)}, u32[]{:S(2)}, u32[]{:S(2)}) collective-permute-start(bf16[2,4,128,128]{3,2,1,0:T(8,128)(2,1)} %get-tuple-element.77), channel_id=1, source_target_pairs={{0,4},{4,0},{1,5},{5,1},{2,6},{6,2},{3,7},{7,3},{8,12},{12,8},{9,1... | collective-permute-start | bytes 786440 | tf_op jit(solution)/shard_map/ppermute | solution.py:25
  248.0 16.7 %collective-permute-start.3 = (bf16[2,4,128,128]{3,2,1,0:T(8,128)(2,1)S(1)}, bf16[2,4,128,128]{3,2,1,0:T(8,128)(2,1)S(1)}, u32[]{:S(2)}, u32[]{:S(2)}) collective-permute-start(bf16[2,4,128,128]{3,2,1,0:T(8,128)(2,1)S(1)} %collective-permute-done.2), channel_id=1, source_target_pairs={{0,4},{4,0},{1,5},{5,1},{2,6},{6,2},{3,7},{7,3},{8,12},{12,8},{9,1... | collective-permute-start | bytes 786440 | tf_op jit(solution)/shard_map/ppermute | solution.py:25
  291.9 4.6 collective-permute-start.4
  304.2 4.4 collective-permute-start.5
  304.4 48.2 %collective-permute-start.6 = (bf16[512,2048]{1,0:T(8,128)(2,1)}, bf16[512,2048]{1,0:T(8,128)(2,1)}, u32[]{:S(2)}, u32[]{:S(2)}) collective-permute-start(bf16[512,2048]{1,0:T(8,128)(2,1)} %get-tuple-element.83.refs_1_), channel_id=1, source_target_pairs={{0,2},{1,3},{2,0},{3,1},{4,6},{5,7},{6,4},{7,5},{8,10},{9,11},{10,... | collective-permute-start | bytes 6291464 | tf_op jit(solution)/shard_map/ppermute | solution.py:40
  355.2 4.4 collective-permute-start.7
  444.2 6.1 collective-permute-start.8
  444.4 72.1 %collective-permute-start.10 = (bf16[512,2048]{1,0:T(8,128)(2,1)}, bf16[512,2048]{1,0:T(8,128)(2,1)}, u32[]{:S(2)}, u32[]{:S(2)}) collective-permute-start(bf16[512,2048]{1,0:T(8,128)(2,1)} %get-tuple-element.100), channel_id=1, source_target_pairs={{0,1},{1,0},{2,3},{3,2},{4,5},{5,4},{6,7},{7,6},{8,9},{9,8},{10,11... | collective-permute-start | bytes 6291464 | tf_op jit(solution)/shard_map/ppermute | solution.py:29
  452.7 55.0 %collective-permute-start.12 = (bf16[512,2048]{1,0:T(8,128)(2,1)S(1)}, bf16[512,2048]{1,0:T(8,128)(2,1)}, u32[]{:S(2)}, u32[]{:S(2)}) collective-permute-start(bf16[512,2048]{1,0:T(8,128)(2,1)S(1)} %add_convert_fusion.1.refs_10_), channel_id=1, source_target_pairs={{0,2},{1,3},{2,0},{3,1},{4,6},{5,7},{6,4},{7,5},{8,10},{9,11},{10,... | collective-permute-start | bytes 6291464 | tf_op jit(solution)/shard_map/ppermute | solution.py:40
  503.5 2.7 collective-permute-start.13
  503.5 4.1 collective-permute-start.14
  516.4 4.7 collective-permute-start.15
  519.6 14.3 %copy-start.3 = (bf16[512,2048]{1,0:T(8,128)(2,1)}, bf16[512,2048]{1,0:T(8,128)(2,1)S(1)}, u32[]{:S(2)}) copy-start(bf16[512,2048]{1,0:T(8,128)(2,1)S(1)} %add_convert_fusion.refs_11_) | copy-start | bytes 6291460
  519.6 83.5 %collective-permute-start.11 = (bf16[512,2048]{1,0:T(8,128)(2,1)S(1)}, bf16[512,2048]{1,0:T(8,128)(2,1)}, u32[]{:S(2)}, u32[]{:S(2)}) collective-permute-start(bf16[512,2048]{1,0:T(8,128)(2,1)S(1)} %add_convert_fusion.refs_11_), channel_id=1, source_target_pairs={{0,2},{1,3},{2,0},{3,1},{4,6},{5,7},{6,4},{7,5},{8,10},{9,11},{10,... | collective-permute-start | bytes 6291464 | tf_op jit(solution)/shard_map/ppermute | solution.py:40
  520.9 82.2 %collective-permute-start.9 = (bf16[512,2048]{1,0:T(8,128)(2,1)}, bf16[512,2048]{1,0:T(8,128)(2,1)}, u32[]{:S(2)}, u32[]{:S(2)}) collective-permute-start(bf16[512,2048]{1,0:T(8,128)(2,1)} %get-tuple-element.98), channel_id=1, source_target_pairs={{0,1},{1,0},{2,3},{3,2},{4,5},{5,4},{6,7},{7,6},{8,9},{9,8},{10,11... | collective-permute-start | bytes 6291464 | tf_op jit(solution)/shard_map/ppermute | solution.py:29
  594.2 8.9 %collective-permute-start.17 = (bf16[2,4,128,128]{3,2,1,0:T(8,128)(2,1)}, bf16[2,4,128,128]{3,2,1,0:T(8,128)(2,1)S(1)}, u32[]{:S(2)}, u32[]{:S(2)}) collective-permute-start(bf16[2,4,128,128]{3,2,1,0:T(8,128)(2,1)} %get-tuple-element.104.refs_4_), channel_id=1, source_target_pairs={{0,2},{1,3},{2,0},{3,1},{4,6},{5,7},{6,4},{7,5},{8,10},{9,11},{10,... | collective-permute-start | bytes 786440 | tf_op jit(solution)/shard_map/ppermute | solution.py:40
  595.3 13.3 %collective-permute-start.16 = (bf16[2,4,128,128]{3,2,1,0:T(8,128)(2,1)}, bf16[2,4,128,128]{3,2,1,0:T(8,128)(2,1)S(1)}, u32[]{:S(2)}, u32[]{:S(2)}) collective-permute-start(bf16[2,4,128,128]{3,2,1,0:T(8,128)(2,1)} %get-tuple-element.104.refs_4_), channel_id=1, source_target_pairs={{0,4},{4,0},{1,5},{5,1},{2,6},{6,2},{3,7},{7,3},{8,12},{12,8},{9,1... | collective-permute-start | bytes 786440 | tf_op jit(solution)/shard_map/ppermute | solution.py:25
  603.2 7.9 %collective-permute-start.18 = (bf16[2,4,128,128]{3,2,1,0:T(8,128)(2,1)S(1)}, bf16[2,4,128,128]{3,2,1,0:T(8,128)(2,1)S(1)}, u32[]{:S(2)}, u32[]{:S(2)}) collective-permute-start(bf16[2,4,128,128]{3,2,1,0:T(8,128)(2,1)S(1)} %collective-permute-done.17), channel_id=1, source_target_pairs={{0,4},{4,0},{1,5},{5,1},{2,6},{6,2},{3,7},{7,3},{8,12},{12,8},{9,1... | collective-permute-start | bytes 786440 | tf_op jit(solution)/shard_map/ppermute | solution.py:25
  621.1 7.1 %collective-permute-start.19 = (bf16[2,2,64,256]{3,2,1,0:T(8,128)(2,1)}, bf16[2,2,64,256]{3,2,1,0:T(8,128)(2,1)S(1)}, u32[]{:S(2)}, u32[]{:S(2)}) collective-permute-start(bf16[2,2,64,256]{3,2,1,0:T(8,128)(2,1)} %get-tuple-element.110), channel_id=1, source_target_pairs={{2,0},{3,1},{4,2},{5,3},{6,4},{7,5},{10,8},{11,9},{12,10},{13,11},... | collective-permute-start | bytes 393224 | tf_op jit(solution)/shard_map/ppermute | solution.py:1309
  628.8 13.8 %copy-start = (bf16[512,2048]{1,0:T(8,128)(2,1)S(1)}, bf16[512,2048]{1,0:T(8,128)(2,1)}, u32[]{:S(2)}) copy-start(bf16[512,2048]{1,0:T(8,128)(2,1)} %branch.1.refs_3_) | copy-start | bytes 6291460
  628.8 13.8 %copy-start.20 = (bf16[512,128]{1,0:T(8,128)(2,1)S(1)}, bf16[512,128]{1,0:T(8,128)(2,1)}, u32[]{:S(2)}) copy-start(bf16[512,128]{1,0:T(8,128)(2,1)} %get-tuple-element.115) | copy-start | bytes 393220
  642.5 4.8 collective-permute-start.20
  (34 other events, 141.5 us)
Sparse Core Ops, SparseCore 0:
  10.2 171.0 all-gather.7
  183.5 144.3 all-gather.3
  330.1 79.3 all-gather.5
